TPU v7x, 512 devices: a whole 4x8x8 slice. The times are simulated.
512 devices in a mesh: ctx: 4 (over x), att: 16 (over y, core), exp: 8 (over z).
Axes of the slice: x: 4, y: 8, z: 8, core: 2. Of those that a mesh axis runs over, the one named last changes fastest.
Arguments:
- queries: bfloat16 [16, 64, 4096], P('att', ('ctx', 'exp')), may hold values from -16 to 16
- keys: bfloat16 [16, 2, 16384, 256], P('att', None, ('ctx', 'exp')), may hold values from -40 to 40
- values: bfloat16 [16, 2, 16384, 256], P('att', None, ('ctx', 'exp')), may hold values from -6 to 6
- lengths: int32 [16, 2], P('att'), may hold values from 2 to 16353, as said below
- residual: bfloat16 [16, 64, 4096], P('att', 'ctx'), may hold values from -6 to 6
- norm_gain: float32 [4096], replicated, may hold values from 0.1 to 1.9
- expert_ids: int32 [16, 64, 8], P('att', 'ctx'), may hold values from 0 to 63, all different within a row; in each aligned block of 16 rows (0 to 15, 16 to 31, ..., all dimensions but the last counted through in order) at most 6 rows name the same one
- gate_values: bfloat16 [16, 64, 8], P('att', 'ctx'), may hold values from 0.049804688 to 0.5
- gate_weight: bfloat16 [64, 4096, 1024], P(('ctx', 'att'), None, 'exp'), may hold values from -0.09375 to 0.09375
- up_weight: bfloat16 [64, 4096, 1024], P(('ctx', 'att'), None, 'exp'), may hold values from -0.09375 to 0.09375
- down_weight: bfloat16 [64, 1024, 4096], P(('ctx', 'att'), 'exp'), may hold values from -0.1875 to 0.1875
Outputs:
- mixed: bfloat16 [16, 64, 4096], P('att', 'ctx', 'exp')
Inputs may be any that keep to these rules, and one draw needn't show every extreme that they name: `lengths`: every request's first draft token sees at least 2 positions, and some request's first draft token sees 16384 - 31, so that its last draft token sees all 16384. `expert_ids`: the 8 experts of a token are distinct. Taking the tokens in order (a, r, j) in aligned blocks of 16 (the tokens one device hands to the experts), no expert is named more than 6 times in a block, and in some block one expert is named exactly 6 times.
All inputs are finite; a program needn't handle non-finite values.
Results may differ from a plain program's by a relative error of at most 0.015.
Values may be sent and summed in bfloat16 or wider, within the bound.
No kernel may reach another device: no remote copies, remote signals or barrier semaphores. Data moves between devices by JAX's collectives and lax.ppermute only.
A program may use at most 128 MiB of HBM per device.

v0:
```python
import jax
import jax.numpy as jnp
from jax import lax
from jax.sharding import PartitionSpec as P

D = 4096
QUERY_HEADS = 32
KEY_VALUE_HEADS = 2
HEAD_SIZE = 128
TOP = 8


def per_device(
    queries,
    keys,
    values,
    lengths,
    residual,
    norm_gain,
    expert_ids,
    gate_values,
    gate_weight,
    up_weight,
    down_weight,
):
    collected_rows = lax.all_gather(queries, ("ctx", "exp"), axis=1, tiled=True)
    request_batch = keys.shape[1]
    draft_tokens = collected_rows.shape[1] // request_batch
    head_groups = QUERY_HEADS // KEY_VALUE_HEADS
    device_extent = keys.shape[2]
    heads_of_queries = collected_rows.reshape(
        request_batch, draft_tokens, KEY_VALUE_HEADS, head_groups, HEAD_SIZE
    )
    heads_of_keys = keys.reshape(request_batch, device_extent, KEY_VALUE_HEADS, HEAD_SIZE)
    heads_of_values = values.reshape(request_batch, device_extent, KEY_VALUE_HEADS, HEAD_SIZE)
    scores = jnp.einsum(
        "rjhgd,rphd->rjhgp", heads_of_queries, heads_of_keys, preferred_element_type=jnp.float32
    ) * HEAD_SIZE ** (-0.5)
    shard_start = lax.axis_index(("ctx", "exp")) * device_extent
    position = shard_start + jnp.arange(device_extent, dtype=jnp.int32)
    limit = lengths[0][:, None] + jnp.arange(draft_tokens, dtype=jnp.int32)[None, :]
    usable = (position[None, None, :] < limit[:, :, None])[:, :, None, None, :]
    masked = jnp.where(usable, scores, -1e30)
    peaks = jnp.max(masked, axis=-1)
    weights = jnp.where(usable, jnp.exp(masked - peaks[..., None]), 0.0)
    totals = jnp.sum(weights, axis=-1)
    partial_value = jnp.einsum(
        "rjhgp,rphd->rjhgd",
        weights.astype(jnp.bfloat16),
        heads_of_values,
        preferred_element_type=jnp.float32,
    )
    highest = lax.pmax(peaks, ("ctx", "exp"))
    factors = jnp.exp(peaks - highest)
    denominator, numerator = (
        lax.psum((factors * totals).astype(jnp.bfloat16), ("ctx", "exp")).astype(jnp.float32),
        lax.psum((factors[..., None] * partial_value).astype(jnp.bfloat16), ("ctx", "exp")).astype(
            jnp.float32
        ),
    )
    attended = (numerator / denominator[..., None]).reshape(
        request_batch * draft_tokens, QUERY_HEADS * HEAD_SIZE
    )
    token_count = residual.shape[1]
    quarter = lax.axis_index("ctx")
    own_rows = lax.dynamic_slice_in_dim(attended, quarter * token_count, token_count, 0)
    hidden_state = residual[0].astype(jnp.float32) + own_rows
    mean_square = jnp.mean(hidden_state * hidden_state, axis=-1, keepdims=True)
    normed = (hidden_state * lax.rsqrt(mean_square + 1e-06) * norm_gain).astype(jnp.bfloat16)
    experts = lax.axis_size(("ctx", "att"))
    capacity = min(token_count, 3 * token_count * TOP // experts)
    slot_count = experts * capacity
    route_ids = expert_ids[0]
    flat_ids = route_ids.reshape(-1)
    onehot = (flat_ids[:, None] == jnp.arange(experts, dtype=jnp.int32)[None, :]).astype(jnp.int32)
    before = jnp.cumsum(onehot, axis=0) - onehot
    slot_of = jnp.sum(before * onehot, axis=1)
    target = (flat_ids * capacity + slot_of).reshape(token_count, TOP)
    slot_ids = jnp.arange(slot_count, dtype=jnp.int32)
    chosen = target[:, :, None] == slot_ids[None, None, :]
    placing = jnp.any(chosen, axis=1).astype(jnp.bfloat16)
    mixing = jnp.sum(jnp.where(chosen, gate_values[0].astype(jnp.float32)[:, :, None], 0.0), axis=1)
    outbound = jnp.dot(placing.T, normed, preferred_element_type=jnp.float32).astype(jnp.bfloat16)
    outbound = outbound.reshape(experts, capacity, D)
    arrived = lax.all_to_all(outbound, ("ctx", "att"), split_axis=0, concat_axis=0, tiled=True)
    flat_in = arrived.reshape(-1, D)
    gate_part = jnp.dot(flat_in, gate_weight[0], preferred_element_type=jnp.float32)
    up_part = jnp.dot(flat_in, up_weight[0], preferred_element_type=jnp.float32)
    inner_act = (jax.nn.silu(gate_part) * up_part).astype(jnp.bfloat16)
    produced = jnp.dot(inner_act, down_weight[0], preferred_element_type=jnp.float32).astype(
        jnp.bfloat16
    )
    expert_out = produced.reshape(arrived.shape)
    returned = lax.all_to_all(expert_out, ("ctx", "att"), split_axis=0, concat_axis=0, tiled=True)
    combined = jnp.dot(
        mixing.astype(jnp.bfloat16),
        returned.reshape(slot_count, D),
        preferred_element_type=jnp.float32,
    )
    expert_sum = lax.psum_scatter(
        combined.astype(jnp.bfloat16), "exp", scatter_dimension=1, tiled=True
    ).astype(jnp.float32)
    col_width = expert_sum.shape[1]
    own_cols = lax.dynamic_slice_in_dim(
        hidden_state, lax.axis_index("exp") * col_width, col_width, 1
    )
    return (own_cols + expert_sum).astype(jnp.bfloat16)[None]


def solution(mesh):
    in_specs = (
        P("att", ("ctx", "exp"), None),
        P("att", None, ("ctx", "exp"), None),
        P("att", None, ("ctx", "exp"), None),
        P("att", None),
        P("att", "ctx", None),
        P(),
        P("att", "ctx", None),
        P("att", "ctx", None),
        P(("ctx", "att"), None, "exp"),
        P(("ctx", "att"), None, "exp"),
        P(("ctx", "att"), "exp", None),
    )
    out_specs = P("att", "ctx", "exp")
    return jax.shard_map(
        per_device, mesh=mesh, in_specs=in_specs, out_specs=out_specs, check_vma=False
    )
```

profile of v0, /device:TPU:1, one launch (start us, length us, event | category | flops | bytes accessed | tf_op | source)
XLA Modules:
  0.0 659.1 jit_solution(8295053357874017471)
XLA Ops:
  8.1 44.7 %all_gather.3 = bf16[1,64,4096]{2,0,1:T(2,128)(2,1)S(1)} all-gather(bf16[1,2,4096]{2,0,1:T(2,128)(2,1)S(1)} %copy.44), channel_id=1, replica_groups=mesh['ctx'=4,'att'=16,'exp'=8] {'ctx','exp'}, dimensions={1}, use_global_device_ids=true | all-gather | bytes 540672 | tf_op jit(solution)/shard_map/all_gather | solution.py:26
  52.8 3.1 reduce
  56.1 1.2 reshape.87
  57.4 2.8 fusion
  60.2 112.8 %pmax.7 = f32[2,32,2,16]{1,3,2,0:T(8,128)S(1)} all-reduce(f32[2,32,2,16]{1,3,2,0:T(8,128)S(1)} %get-tuple-element.11), channel_id=1, replica_groups=mesh['ctx'=4,'att'=16,'exp'=8] {'ctx','exp'}, use_global_device_ids=true, to_apply=%region_1.2 | all-reduce | flops 2048 | bytes 16384 | tf_op jit(solution)/shard_map/pmax | solution.py:53
  173.0 3.0 fusion.1
  176.1 2.0 reshape.89
  178.1 3.2 fusion.11
  181.6 110.5 %psum.15 = bf16[2,32,2,16]{1,3,2,0:T(8,128)(2,1)S(1)} all-reduce(bf16[2,32,2,16]{1,3,2,0:T(8,128)(2,1)S(1)} %get-tuple-element.7), channel_id=1, replica_groups=mesh['ctx'=4,'att'=16,'exp'=8] {'ctx','exp'}, use_global_device_ids=true, to_apply=%region_4.5 | all-reduce | flops 2048 | bytes 8192 | tf_op jit(solution)/shard_map/psum | solution.py:56
  292.9 76.8 %all-reduce.2.cloned.1.call-done = bf16[2,32,2,16,128]{4,3,1,2,0:T(8,128)(2,1)} async-done(((bf16[2,32,2,16,128]{4,3,1,2,0:T(8,128)(2,1)}), bf16[2,32,2,16,128]{4,3,1,2,0:T(8,128)(2,1)}) %all-reduce.2.cloned.1.call-update) | async-done | bytes 524304 | tf_op jit(solution)/shard_map/psum | solution.py:57
  369.7 1.4 convert_divide_fusion
  371.6 2.7 convolution_convert_fusion.1
  374.4 5.6 reshape.91
  380.0 109.8 %all_to_all.10 = bf16[64,6,4096]{2,1,0:T(8,128)(2,1)} all-to-all(bf16[64,6,4096]{2,1,0:T(8,128)(2,1)} %reshape.91), channel_id=1, replica_groups=mesh['ctx'=4,'att'=16,'exp'=8] {'ctx','att'}, dimensions={0} | all-to-all | bytes 6291456 | tf_op jit(solution)/shard_map/all_to_all | solution.py:85
  489.8 5.9 reshape.92
  495.7 3.5 fusion.18
  499.2 7.0 %convolution_convert_fusion = bf16[384,4096]{1,0:T(8,128)(2,1)} fusion(bf16[384,4096]{1,0:T(8,128)(2,1)} %reshape.92, bf16[1,128,4096]{2,1,0:T(8,128)(2,1)S(1)} %copy-done, bf16[1,4096,128]{2,1,0:T(8,128)(2,1)S(1)} %copy-done.2, f32[384,128]{1,0:T(8,128)} %fusion.18), kind=kOutput, calls=%fused_computation | convolution fusion | flops 807174144 | bytes 8585216 | tf_op jit(solution)/shard_map/dot_general | solution.py:90
  506.2 5.7 reshape.93
  511.9 6.1 all-to-all-start.1
  518.4 95.6 %all-to-all-done.1 = bf16[64,6,4096]{2,1,0:T(8,128)(2,1)} async-done(((bf16[64,6,4096]{2,1,0:T(8,128)(2,1)}), bf16[64,6,4096]{2,1,0:T(8,128)(2,1)}, u32[]{:S(2)}, u32[]{:S(2)}) %all-to-all-start.1) | async-done | bytes 3145760 | tf_op jit(solution)/shard_map/all_to_all | solution.py:94
  614.0 5.7 reshape.94
  619.7 3.1 convolution_convert_fusion.2
  622.8 28.2 %reduce-scatter.2.cloned.1.call-done = bf16[16,512]{1,0:T(8,128)(2,1)} async-done(((bf16[16,4096]{1,0:T(8,128)(2,1)}), bf16[16,512]{1,0:T(8,128)(2,1)}) %reduce-scatter.2.cloned.1.call-update) | async-done | bytes 16400 | tf_op jit(solution)/shard_map/reduce_scatter | solution.py:100
  650.9 1.3 fusion.34
  (43 shorter events, 3.7 us)
Async XLA Ops:
  6.5 492.7 %copy-start = (bf16[1,128,4096]{2,1,0:T(8,128)(2,1)S(1)}, bf16[1,128,4096]{2,1,0:T(8,128)(2,1)}, u32[]{:S(2)}) copy-start(bf16[1,128,4096]{2,1,0:T(8,128)(2,1)} %param.21) | copy-start | bytes 3145732
  6.5 363.2 %all-reduce.2.cloned.1.call-start = ((), (), s32[]{:S(2)}) async-start(), calls=%async_computation.3 | async-start | bytes 1048576 | tf_op jit(solution)/shard_map/psum | solution.py:57
  176.0 5.4 copy-start.5
  181.3 190.2 %copy-start.3 = (bf16[1,16,4096]{2,1,0:T(8,128)(2,1)S(1)}, bf16[1,16,4096]{2,1,0:T(8,128)(2,1)}, u32[]{:S(2)}) copy-start(bf16[1,16,4096]{2,1,0:T(8,128)(2,1)} %param.15) | copy-start | bytes 393220
  181.3 190.3 %copy-start.4 = (f32[4096]{0:T(1024)S(1)}, f32[4096]{0:T(1024)}, u32[]{:S(2)}) copy-start(f32[4096]{0:T(1024)} %param.16) | copy-start | bytes 49156
  489.8 5.9 copy-start.1
  489.8 9.4 %copy-start.2 = (bf16[1,4096,128]{2,1,0:T(8,128)(2,1)S(1)}, bf16[1,4096,128]{2,1,0:T(8,128)(2,1)}, u32[]{:S(2)}) copy-start(bf16[1,4096,128]{2,1,0:T(8,128)(2,1)} %param.20) | copy-start | bytes 3145732
  511.9 6.2 copy-start.6
  511.9 102.0 %all-to-all-start.1 = ((bf16[64,6,4096]{2,1,0:T(8,128)(2,1)}), bf16[64,6,4096]{2,1,0:T(8,128)(2,1)}, u32[]{:S(2)}, u32[]{:S(2)}) async-start(bf16[64,6,4096]{2,1,0:T(8,128)(2,1)} %reshape.93), calls=%async_computation.1 | async-start | bytes 8388608 | tf_op jit(solution)/shard_map/all_to_all | solution.py:94
  518.1 132.9 %reduce-scatter.2.cloned.1.call-start = ((), (), s32[]{:S(2)}) async-start(), calls=%async_computation.4 | async-start | bytes 147456 | tf_op jit(solution)/shard_map/reduce_scatter | solution.py:100
Sparse Core Ops, SparseCore 0:
  181.4 188.2 all-reduce.1
  622.9 28.0 reduce-scatter.1
where the time goes:
time: 665 us; the launch traced here: 659 us
  blocking collectives  378 us (57%)
  waiting for transfers between devices  201 us (30%)
  local copies, waits for them, and re-layouts  27.9 us (4%)
  matrix products  22.4 us (3%)
  between operations  13.6 us (2%)
  other arithmetic  10.6 us (2%)
    pmax x1, blocking collectives, per_device(): highest = lax.pmax(peaks, ('ctx', 'exp'))  113 us
    psum x1, blocking collectives, per_device(): lax.psum((factors * totals).astype(jnp.bfloat16), ('ctx', 'exp'))  110 us
    all_to_all x1, blocking collectives, per_device(): lax.all_to_all(outbound, ('ctx', 'att'), split_axis=0, concat_axis=0, til...  110 us
    all_to_all x1, waiting for transfers between devices, per_device(): lax.all_to_all(expert_out, ('ctx', 'att'), split_axis=0, concat_axis=0, t...  95.6 us
    psum x1, waiting for transfers between devices, per_device(): lax.psum((factors[..., None] * partial_value).astype(jnp.bfloat16), ('ctx...  76.8 us
    all_gather x1, blocking collectives, per_device(): collected_rows = lax.all_gather(queries, ('ctx', 'exp'), axis=1, tiled=True)  44.7 us
    reduce_scatter x1, waiting for transfers between devices, per_device(): lax.psum_scatter(combined.astype(jnp.bfloat16), 'exp', scatter_dimension=...  28.2 us
  transfers between devices with their start and end apart: 3, of which 3 were waited for; matrix products, arithmetic and copies ran while one was open for 0% of the time, Pallas kernels for 0%

commit v1 on v0

v1 whole, which is shorter than its diff:
```python
import jax
import jax.numpy as jnp
from jax import lax
from jax.experimental import pallas as pl
from jax.experimental.pallas import tpu as pltpu
from jax.sharding import PartitionSpec as P

D = 4096
QUERY_HEADS = 32
KEY_VALUE_HEADS = 2
HEAD_SIZE = 128
TOP = 8
CAP = 6
SLOTS = 8
F32 = jnp.float32
BF16 = jnp.bfloat16
VMEM_LIMIT = 48 * 1024 * 1024

VMEM_SPEC = pl.BlockSpec(memory_space=pltpu.VMEM)
SMEM_SPEC = pl.BlockSpec(memory_space=pltpu.SMEM)


def params():
    return pltpu.CompilerParams(vmem_limit_bytes=VMEM_LIMIT)


def cost(flops, bytes_accessed, transcendentals=0):
    return pl.CostEstimate(
        flops=flops, bytes_accessed=bytes_accessed, transcendentals=transcendentals
    )


def attention_kernel(limit_ref, q_ref, k_ref, v_ref, out_ref):
    group = QUERY_HEADS // KEY_VALUE_HEADS
    lane = lax.broadcasted_iota(jnp.int32, (16, 128), 1)
    extent = k_ref.shape[1]
    rows = group * 32
    position = lax.broadcasted_iota(jnp.int32, (rows, extent), 1)
    draft = lax.broadcasted_iota(jnp.int32, (rows, extent), 0) & 31
    offset = position - draft
    for r in range(2):
        usable = offset < limit_ref[r]
        for g in range(KEY_VALUE_HEADS):
            query = jnp.concatenate(
                [
                    q_ref[r * 32 : (r + 1) * 32, (g * group + h) * 128 : (g * group + h + 1) * 128]
                    for h in range(group)
                ],
                axis=0,
            )
            key = k_ref[r, :, g * 128 : (g + 1) * 128]
            value = v_ref[r, :, g * 128 : (g + 1) * 128]
            scores = lax.dot_general(
                query, key, (((1,), (1,)), ((), ())), preferred_element_type=F32
            ) * (HEAD_SIZE ** (-0.5))
            masked = jnp.where(usable, scores, -1e30)
            peak = jnp.max(masked, axis=1, keepdims=True).astype(BF16).astype(F32)
            weight = jnp.where(usable, jnp.exp(masked - peak), 0.0)
            total = jnp.sum(weight, axis=1, keepdims=True)
            partial = jnp.dot(weight.astype(BF16), value, preferred_element_type=F32)
            for z4 in range(group // 4):
                z = g * (group // 4) + z4
                for jb in range(2):
                    target = (r * 2 + jb) * 8 + z
                    stats = jnp.zeros((16, 128), F32)
                    for hh in range(4):
                        lo = (z4 * 4 + hh) * 32 + jb * 16
                        out_ref[target, hh * 16 : (hh + 1) * 16, :] = partial[lo : lo + 16].astype(
                            BF16
                        )
                        stats = jnp.where(lane == hh, peak[lo : lo + 16], stats)
                        stats = jnp.where(lane == 4 + hh, total[lo : lo + 16], stats)
                    out_ref[target, 64:80, :] = stats.astype(BF16)


def attention(limits, q, keys, values):
    return pl.pallas_call(
        attention_kernel,
        out_shape=jax.ShapeDtypeStruct((32, 80, 128), BF16),
        in_specs=[SMEM_SPEC, VMEM_SPEC, VMEM_SPEC, VMEM_SPEC],
        out_specs=VMEM_SPEC,
        compiler_params=params(),
        cost_estimate=cost(540_000_000, 2_200_000, 1_100_000),
        name="attention",
    )(limits, q, keys, values)


def routed(ids):
    row = lax.broadcasted_iota(jnp.int32, (16, 512), 1)
    expert, place = row >> 3, row & 7
    named = ids[:, 0:1] == expert
    for k in range(1, TOP):
        named = named | (ids[:, k : k + 1] == expert)
    named = named.astype(F32)
    earlier = lax.broadcasted_iota(jnp.int32, (16, 16), 1) < lax.broadcasted_iota(
        jnp.int32, (16, 16), 0
    )
    before = jnp.dot(
        earlier.astype(F32).astype(BF16), named.astype(BF16), preferred_element_type=F32
    )
    return jnp.where(before == place.astype(F32), named, 0.0), expert


def combine_kernel(z_ref, part_ref, res_ref, gain_ref, ids_ref, hidden_ref, send_ref):
    start = pl.multiple_of(z_ref[0] * 512, 512)
    sources = part_ref.shape[0]
    stats = part_ref[:, 64:80, :].astype(F32)
    highest = jnp.max(stats, axis=0)
    factor = jnp.exp(stats - highest[None])
    totals = pltpu.roll(stats.reshape(sources * 16, 128), 124, 1).reshape(sources, 16, 128)
    denominator = jnp.sum(factor * totals, axis=0)
    columns = []
    for hh in range(4):
        numerator = jnp.sum(
            part_ref[:, hh * 16 : (hh + 1) * 16, :].astype(F32) * factor[:, :, hh : hh + 1], axis=0
        )
        columns.append(numerator / denominator[:, hh : hh + 1])
    hidden = jnp.concatenate(columns, axis=1) + res_ref[:, pl.ds(start, 512)].astype(F32)
    hidden_ref[...] = hidden
    row = (hidden * gain_ref[:, pl.ds(start, 512)]).astype(BF16)
    table, _ = routed(ids_ref[...])
    send_ref[...] = lax.dot_general(
        table.astype(BF16), row, (((0,), (0,)), ((), ())), preferred_element_type=F32
    ).astype(BF16)


def combine(z, part, res, gain, ids):
    return pl.pallas_call(
        combine_kernel,
        out_shape=(
            jax.ShapeDtypeStruct((16, 512), F32),
            jax.ShapeDtypeStruct((512, 512), BF16),
        ),
        in_specs=[SMEM_SPEC] + [VMEM_SPEC] * 4,
        out_specs=(VMEM_SPEC, VMEM_SPEC),
        compiler_params=params(),
        cost_estimate=cost(10_000_000, 1_500_000),
        name="combine",
    )(z, part, res, gain, ids)


def compact_kernel(arrived_ref, out_ref, wide):
    for c in range(4):
        wide[c * 512 : (c + 1) * 512, :] = arrived_ref[:, c * 128 : (c + 1) * 128].astype(F32)
    for s in range(CAP):
        for c in range(4):
            block = wide[pl.ds(c * 512 + s, 64, stride=SLOTS), :]
            out_ref[s * 64 : (s + 1) * 64, c * 128 : (c + 1) * 128] = block.astype(BF16)


def compact(arrived):
    return pl.pallas_call(
        compact_kernel,
        out_shape=jax.ShapeDtypeStruct((384, 512), BF16),
        in_specs=[VMEM_SPEC],
        out_specs=VMEM_SPEC,
        scratch_shapes=[pltpu.VMEM((2048, 128), F32)],
        compiler_params=params(),
        cost_estimate=cost(1_000_000, 1_000_000),
        name="compact",
    )(arrived)


def expand_kernel(sum_ref, out_ref, wide):
    for s in range(SLOTS):
        for c in range(4):
            if s < CAP:
                block = sum_ref[s * 64 : (s + 1) * 64, c * 128 : (c + 1) * 128].astype(F32)
            else:
                block = jnp.zeros((64, 128), F32)
            wide[pl.ds(c * 512 + s, 64, stride=SLOTS), :] = block
    for c in range(4):
        out_ref[:, c * 128 : (c + 1) * 128] = wide[c * 512 : (c + 1) * 512, :].astype(BF16)


def expand(summed):
    return pl.pallas_call(
        expand_kernel,
        out_shape=jax.ShapeDtypeStruct((512, 512), BF16),
        in_specs=[VMEM_SPEC],
        out_specs=VMEM_SPEC,
        scratch_shapes=[pltpu.VMEM((2048, 128), F32)],
        compiler_params=params(),
        cost_estimate=cost(1_000_000, 1_000_000),
        name="expand",
    )(summed)


def expert_kernel(x_ref, gate_ref, up_ref, gain_ref, down_ref, out_ref, acc, square, inner):
    step = pl.program_id(0)

    @pl.when(step == 0)
    def _():
        acc[...] = jnp.zeros_like(acc)
        square[...] = jnp.zeros_like(square)

    @pl.when(step < 8)
    def _():
        x = x_ref[0]
        weight = jnp.concatenate([gate_ref[...], up_ref[...]], axis=1)
        acc[...] += jnp.dot(x, weight, preferred_element_type=F32)
        plain = x.astype(F32) * (1.0 / gain_ref[...])
        sq = plain * plain
        square[...] += sq[:, 0:128] + sq[:, 128:256] + sq[:, 256:384] + sq[:, 384:512]

    @pl.when(step == 7)
    def _():
        mean = jnp.sum(square[...], axis=1, keepdims=True) * (1.0 / D)
        scale = lax.rsqrt(mean + 1e-6)
        gate = acc[:, 0:128] * scale
        up = acc[:, 128:256] * scale
        inner[...] = (gate / (1.0 + jnp.exp(-gate)) * up).astype(BF16)

    @pl.when(step >= 8)
    def _():
        out_ref[0] = jnp.dot(inner[...], down_ref[...], preferred_element_type=F32).astype(BF16)


def expert(x, gate, up, gain, down):
    early = lambda g: jnp.minimum(g, 7)
    late = lambda g: jnp.maximum(g - 8, 0)
    return pl.pallas_call(
        expert_kernel,
        out_shape=jax.ShapeDtypeStruct((8, 384, 512), BF16),
        grid=(16,),
        in_specs=[
            pl.BlockSpec((1, 384, 512), lambda g: (early(g), 0, 0)),
            pl.BlockSpec((512, 128), lambda g: (early(g), 0)),
            pl.BlockSpec((512, 128), lambda g: (early(g), 0)),
            pl.BlockSpec((1, 512), lambda g: (0, early(g))),
            pl.BlockSpec((128, 512), lambda g: (0, late(g))),
        ],
        out_specs=pl.BlockSpec((1, 384, 512), lambda g: (late(g), 0, 0)),
        scratch_shapes=[
            pltpu.VMEM((384, 256), F32),
            pltpu.VMEM((384, 128), F32),
            pltpu.VMEM((384, 128), BF16),
        ],
        compiler_params=params(),
        cost_estimate=cost(1_200_000_000, 10_000_000),
        name="expert",
    )(x, gate, up, gain, down)


def mix_kernel(hidden_ref, back_ref, ids_ref, gates_ref, out_ref):
    ids = ids_ref[...]
    gates = gates_ref[...].astype(F32)
    table, expert = routed(ids)
    weight = jnp.zeros((16, 512), F32)
    for k in range(TOP):
        weight = weight + jnp.where(ids[:, k : k + 1] == expert, gates[:, k : k + 1], 0.0)
    mixing = (weight * table).astype(BF16)
    out_ref[...] = (
        hidden_ref[...] + jnp.dot(mixing, back_ref[...], preferred_element_type=F32)
    ).astype(BF16)


def mix(hidden, back, ids, gates):
    return pl.pallas_call(
        mix_kernel,
        out_shape=jax.ShapeDtypeStruct((16, 512), BF16),
        in_specs=[VMEM_SPEC] * 4,
        out_specs=VMEM_SPEC,
        compiler_params=params(),
        cost_estimate=cost(10_000_000, 600_000),
        name="mix",
    )(hidden, back, ids, gates)


def per_device(
    queries,
    keys,
    values,
    lengths,
    residual,
    norm_gain,
    expert_ids,
    gate_values,
    gate_weight,
    up_weight,
    down_weight,
):
    z = lax.axis_index("exp")
    devices = lax.axis_size(("ctx", "exp"))
    context = keys.shape[2]
    start = lax.axis_index(("ctx", "exp")) * context
    gain = norm_gain.reshape(1, D)
    ids, gates = expert_ids[0], gate_values[0]
    gate, up, down = gate_weight[0], up_weight[0], down_weight[0]

    spread = jnp.broadcast_to(queries, (devices,) + queries.shape[1:])
    q = lax.all_to_all(spread, ("ctx", "exp"), split_axis=0, concat_axis=0, tiled=True)
    q = q.reshape(devices * queries.shape[1], D)
    part = attention(lengths[0] - start, q, keys[0], values[0])
    part = lax.all_to_all(part, ("ctx", "exp"), split_axis=0, concat_axis=0, tiled=True)
    hidden, outbound = combine(z.reshape(1), part, residual[0], gain, ids)
    arrived = lax.all_to_all(
        outbound.reshape(64, SLOTS, 512), ("ctx", "att"), split_axis=0, concat_axis=0, tiled=True
    )
    own = compact(arrived.reshape(512, 512))
    rows = lax.all_gather(own, "exp", axis=0)
    sums = expert(rows, gate, up, gain, down)
    back = expand(lax.psum_scatter(sums, "exp", scatter_dimension=0))
    back = lax.all_to_all(
        back.reshape(64, SLOTS, 512), ("ctx", "att"), split_axis=0, concat_axis=0, tiled=True
    )
    return mix(hidden, back.reshape(512, 512), ids, gates)[None]


def solution(mesh):
    in_specs = (
        P("att", ("ctx", "exp"), None),
        P("att", None, ("ctx", "exp"), None),
        P("att", None, ("ctx", "exp"), None),
        P("att", None),
        P("att", "ctx", None),
        P(),
        P("att", "ctx", None),
        P("att", "ctx", None),
        P(("ctx", "att"), None, "exp"),
        P(("ctx", "att"), None, "exp"),
        P(("ctx", "att"), "exp", None),
    )
    out_specs = P("att", "ctx", "exp")
    return jax.shard_map(
        per_device, mesh=mesh, in_specs=in_specs, out_specs=out_specs, check_vma=False
    )
```

time: 665 us -> 239 us (0.36)
  blocking collectives: 378 us -> 30 us
  waiting for transfers between devices: 201 us -> 136 us
  starting transfers between devices: 6.18 us -> 34.1 us
  matrix products: 22.4 us -> 0 us
  local copies, waits for them, and re-layouts: 27.9 us -> 6.69 us
  Pallas kernels: 0 us -> 18.1 us
  other arithmetic: 10.6 us -> 0.66 us
    pmax x1 -> x0, blocking collectives: 113 us -> none  [per_device(): highest = lax.pmax(peaks, ('ctx', 'exp'))]
    psum x1 -> x0, blocking collectives: 110 us -> none  [per_device(): lax.psum((factors * totals).astype(jnp.bfloat16), ('ctx', 'exp'))]
    all_to_all x1, blocking collectives: 110 us -> 30 us  [per_device(): lax.all_to_all(outbound.reshape(64, SLOTS, 512), ('ctx', 'att'), split_ax...]
    psum x1 -> x0, waiting for transfers between devices: 76.8 us -> none  [per_device(): lax.psum((factors[..., None] * partial_value).astype(jnp.bfloat16), ('ctx...]
    all_to_all x1 -> x3, waiting for transfers between devices: 95.6 us -> 47.2 us  [the longest x1 17.2 us: per_device(): lax.all_to_all(back.reshape(64, SLOTS, 512), ('ctx', 'att'), split_axis=0...]
    all_gather x1 -> x0, blocking collectives: 44.7 us -> none  [per_device(): collected_rows = lax.all_gather(queries, ('ctx', 'exp'), axis=1, tiled=True)]
    all_gather x0 -> x1, waiting for transfers between devices: none -> 42.6 us  [per_device(): rows = lax.all_gather(own, 'exp', axis=0)]
    all_to_all x1 -> x3, starting transfers between devices: 6.14 us -> 34 us  [the longest x1 13.7 us: per_device(): lax.all_to_all(spread, ('ctx', 'exp'), split_axis=0, concat_axis=0, tiled...]
  transfers between devices with their start and end apart: 3 -> 5, of which waited for: 3 -> 5; matrix products, arithmetic and copies ran while one was open for 0% -> 0% of each run, Pallas kernels for 0% -> 0%
where the time goes in v1:
time: 239 us
  waiting for transfers between devices  136 us (57%)
  starting transfers between devices  34.1 us (14%)
  blocking collectives  30 us (13%)
  Pallas kernels  18.1 us (8%)
  between operations  13.5 us (6%)
  local copies, waits for them, and re-layouts  6.69 us (3%)
    reduce_scatter x1, waiting for transfers between devices, per_device(): back = expand(lax.psum_scatter(sums, 'exp', scatter_dimension=0))  45.9 us
    all_gather x1, waiting for transfers between devices, per_device(): rows = lax.all_gather(own, 'exp', axis=0)  42.6 us
    all_to_all x1, blocking collectives, per_device(): lax.all_to_all(outbound.reshape(64, SLOTS, 512), ('ctx', 'att'), split_ax...  30 us
    all_to_all x1, waiting for transfers between devices, per_device(): lax.all_to_all(back.reshape(64, SLOTS, 512), ('ctx', 'att'), split_axis=0...  17.2 us
    all_to_all x1, waiting for transfers between devices, per_device(): lax.all_to_all(part, ('ctx', 'exp'), split_axis=0, concat_axis=0, tiled=T...  16.3 us
    all_to_all x1, starting transfers between devices, per_device(): lax.all_to_all(spread, ('ctx', 'exp'), split_axis=0, concat_axis=0, tiled...  13.7 us
    all_to_all x1, waiting for transfers between devices, per_device(): lax.all_to_all(spread, ('ctx', 'exp'), split_axis=0, concat_axis=0, tiled...  13.6 us
    all_to_all x1, starting transfers between devices, per_device(): lax.all_to_all(back.reshape(64, SLOTS, 512), ('ctx', 'att'), split_axis=0...  12.8 us
  transfers between devices with their start and end apart: 5, of which 5 were waited for; matrix products, arithmetic and copies ran while one was open for 0% of the time, Pallas kernels for 0%

profile of v1, /device:TPU:1, one launch (start us, length us, event | category | flops | bytes accessed | tf_op | source)
XLA Modules:
  0.0 238.7 jit_solution(15463197945346017944)
XLA Ops:
  6.5 2.0 broadcast_in_dim.11
  8.6 13.7 %all-to-all-start = ((bf16[32,2,4096]{2,1,0:T(2,128)(2,1)}), bf16[32,2,4096]{2,1,0:T(2,128)(2,1)S(1)}, u32[]{:S(2)}, u32[]{:S(2)}) async-start(bf16[32,2,4096]{2,1,0:T(2,128)(2,1)} %broadcast_in_dim.11), calls=%async_computation | async-start | bytes 1048576 | tf_op jit(solution)/shard_map/all_to_all | solution.py:292
  22.3 0.7 subtract_bitcast_fusion.limit_ref
  23.0 13.6 %all-to-all-done = bf16[32,2,4096]{2,1,0:T(2,128)(2,1)S(1)} async-done(((bf16[32,2,4096]{2,1,0:T(2,128)(2,1)}), bf16[32,2,4096]{2,1,0:T(2,128)(2,1)S(1)}, u32[]{:S(2)}, u32[]{:S(2)}) %all-to-all-start) | async-done | bytes 524320 | tf_op jit(solution)/shard_map/all_to_all | solution.py:292
  36.6 0.2 reshape.24.q_ref
  36.8 1.0 copy-done.3
  37.8 1.0 copy-done.4
  38.9 3.8 %attention.1 = bf16[32,80,128]{2,1,0:T(8,128)(2,1)} custom-call(s32[2]{0:T(128)S(1)} %subtract_bitcast_fusion.limit_ref, bf16[64,4096]{1,0:T(8,128)(2,1)S(1)} %reshape.24.q_ref, bf16[2,512,256]{2,1,0:T(8,128)(2,1)S(1)} %bitcast.25, bf16[2,512,256]{2,1,0:T(8,128)(2,1)S(1)} %bitcast.26), custom_call_target="tpu_custom_call" | custom-call | flops 540000000 | bytes 2200000 | tf_op jit(solution)/shard_map/attention/pallas_call | solution.py:77
  42.7 7.5 %all-to-all-start.1 = ((bf16[32,80,128]{2,1,0:T(8,128)(2,1)}), bf16[32,80,128]{2,1,0:T(8,128)(2,1)S(1)}, u32[]{:S(2)}, u32[]{:S(2)}) async-start(bf16[32,80,128]{2,1,0:T(8,128)(2,1)} %attention.1), calls=%async_computation.1 | async-start | bytes 1310720 | tf_op jit(solution)/shard_map/all_to_all | solution.py:295
  50.3 0.1 copy.12.ids_ref
  50.3 16.3 %all-to-all-done.1.part_ref = bf16[32,80,128]{2,1,0:T(8,128)(2,1)S(1)} async-done(((bf16[32,80,128]{2,1,0:T(8,128)(2,1)}), bf16[32,80,128]{2,1,0:T(8,128)(2,1)S(1)}, u32[]{:S(2)}, u32[]{:S(2)}) %all-to-all-start.1) | async-done | bytes 655392 | tf_op jit(solution)/shard_map/all_to_all | solution.py:295
  66.6 0.8 combine.1
  67.4 30.0 %all_to_all.20 = bf16[64,8,512]{2,1,0:T(8,128)(2,1)S(1)} all-to-all(bf16[64,8,512]{2,1,0:T(8,128)(2,1)S(1)} %bitcast.27), channel_id=1, replica_groups=mesh['ctx'=4,'att'=16,'exp'=8] {'ctx','att'}, dimensions={0} | all-to-all | bytes 1048576 | tf_op jit(solution)/shard_map/all_to_all | solution.py:297
  97.4 1.0 compact.1
  98.5 42.6 %all-gather.3.cloned.1.call-done = bf16[3072,512]{1,0:T(8,128)(2,1)} async-done(((bf16[384,512]{1,0:T(8,128)(2,1)}), bf16[3072,512]{1,0:T(8,128)(2,1)}) %all-gather.3.cloned.1.call-update) | async-done | bytes 3145744 | tf_op jit(solution)/shard_map/all_gather | solution.py:301
  141.1 1.2 copy-done.2
  142.3 10.3 %expert.1 = bf16[8,384,512]{2,1,0:T(8,128)(2,1)} custom-call(bf16[8,384,512]{2,1,0:T(8,128)(2,1)} %bitcast.32, bf16[4096,128]{1,0:T(8,128)(2,1)S(1)} %bitcast.22, bf16[4096,128]{1,0:T(8,128)(2,1)S(1)} %bitcast.23, f32[1,4096]{1,0:T(1,128)S(1)} %bitcast.31, bf16[128,4096]{1,0:T(8,128)(2,1)S(1)} %bitcast.24), custom_call_target="tpu_custom_call" | custom-call | flops 1200000000 | bytes 10000000 | tf_op jit(solution)/shard_map/expert/pallas_call | solution.py:222
  152.7 45.9 %reduce-scatter.2.cloned.1.call-done = bf16[1,384,512]{2,1,0:T(8,128)(2,1)} async-done(((bf16[8,384,512]{2,1,0:T(8,128)(2,1)}), bf16[1,384,512]{2,1,0:T(8,128)(2,1)}) %reduce-scatter.2.cloned.1.call-update) | async-done | bytes 393232 | tf_op jit(solution)/shard_map/reduce_scatter | solution.py:303
  198.6 1.0 copy-done.5
  199.6 1.1 expand.1
  200.7 12.8 %all-to-all-start.3 = ((bf16[64,8,512]{2,1,0:T(8,128)(2,1)}), bf16[64,8,512]{2,1,0:T(8,128)(2,1)S(1)}, u32[]{:S(2)}, u32[]{:S(2)}) async-start(bf16[64,8,512]{2,1,0:T(8,128)(2,1)} %bitcast.15), calls=%async_computation.4 | async-start | bytes 1048576 | tf_op jit(solution)/shard_map/all_to_all | solution.py:304
  213.5 0.1 copy.14.gates_ref
  213.6 17.2 %all-to-all-done.3 = bf16[64,8,512]{2,1,0:T(8,128)(2,1)S(1)} async-done(((bf16[64,8,512]{2,1,0:T(8,128)(2,1)}), bf16[64,8,512]{2,1,0:T(8,128)(2,1)S(1)}, u32[]{:S(2)}, u32[]{:S(2)}) %all-to-all-start.3) | async-done | bytes 524320 | tf_op jit(solution)/shard_map/all_to_all | solution.py:304
  230.8 1.0 mix.1
  (20 shorter events, 0.1 us)
Async XLA Ops:
  6.5 43.7 %copy-start.8 = (s32[1,16,8]{1,2,0:T(8,128)S(1)}, s32[1,16,8]{1,2,0:T(8,128)}, u32[]{:S(2)}) copy-start(s32[1,16,8]{1,2,0:T(8,128)} %param.17) | copy-start | bytes 1540
  6.5 60.1 %copy-start.6 = (bf16[1,16,4096]{2,1,0:T(8,128)(2,1)S(1)}, bf16[1,16,4096]{2,1,0:T(8,128)(2,1)}, u32[]{:S(2)}) copy-start(bf16[1,16,4096]{2,1,0:T(8,128)(2,1)} %param.15) | copy-start | bytes 393220
  6.5 60.1 %copy-start.7 = (f32[4096]{0:T(1024)S(1)}, f32[4096]{0:T(1024)}, u32[]{:S(2)}) copy-start(f32[4096]{0:T(1024)} %param.16) | copy-start | bytes 49156
  8.6 28.0 %all-to-all-start = ((bf16[32,2,4096]{2,1,0:T(2,128)(2,1)}), bf16[32,2,4096]{2,1,0:T(2,128)(2,1)S(1)}, u32[]{:S(2)}, u32[]{:S(2)}) async-start(bf16[32,2,4096]{2,1,0:T(2,128)(2,1)} %broadcast_in_dim.11), calls=%async_computation | async-start | bytes 1048576 | tf_op jit(solution)/shard_map/all_to_all | solution.py:292
  36.8 1.0 copy-start.3
  37.8 1.0 copy-start.4
  38.9 102.2 %copy-start = (bf16[1,4096,128]{2,1,0:T(8,128)(2,1)S(1)}, bf16[1,4096,128]{2,1,0:T(8,128)(2,1)}, u32[]{:S(2)}) copy-start(bf16[1,4096,128]{2,1,0:T(8,128)(2,1)} %param.19) | copy-start | bytes 3145732
  38.9 102.2 %copy-start.1 = (bf16[1,4096,128]{2,1,0:T(8,128)(2,1)S(1)}, bf16[1,4096,128]{2,1,0:T(8,128)(2,1)}, u32[]{:S(2)}) copy-start(bf16[1,4096,128]{2,1,0:T(8,128)(2,1)} %param.20) | copy-start | bytes 3145732
  42.7 23.9 %all-to-all-start.1 = ((bf16[32,80,128]{2,1,0:T(8,128)(2,1)}), bf16[32,80,128]{2,1,0:T(8,128)(2,1)S(1)}, u32[]{:S(2)}, u32[]{:S(2)}) async-start(bf16[32,80,128]{2,1,0:T(8,128)(2,1)} %attention.1), calls=%async_computation.1 | async-start | bytes 1310720 | tf_op jit(solution)/shard_map/all_to_all | solution.py:295
  50.2 90.9 %all-gather.3.cloned.1.call-start = ((), (), s32[]{:S(2)}) async-start(), calls=%async_computation.6 | async-start | bytes 3538944 | tf_op jit(solution)/shard_map/all_gather | solution.py:301
  98.5 100.1 %reduce-scatter.2.cloned.1.call-start = ((), (), s32[]{:S(2)}) async-start(), calls=%async_computation.5 | async-start | bytes 3538944 | tf_op jit(solution)/shard_map/reduce_scatter | solution.py:303
  141.1 1.2 copy-start.2
  152.7 60.8 %copy-start.9 = (bf16[1,16,8]{1,2,0:T(8,128)(2,1)S(1)}, bf16[1,16,8]{1,2,0:T(8,128)(2,1)}, u32[]{:S(2)}) copy-start(bf16[1,16,8]{1,2,0:T(8,128)(2,1)} %param.18) | copy-start | bytes 772
  198.6 1.0 copy-start.5
  200.7 30.1 %all-to-all-start.3 = ((bf16[64,8,512]{2,1,0:T(8,128)(2,1)}), bf16[64,8,512]{2,1,0:T(8,128)(2,1)S(1)}, u32[]{:S(2)}, u32[]{:S(2)}) async-start(bf16[64,8,512]{2,1,0:T(8,128)(2,1)} %bitcast.15), calls=%async_computation.4 | async-start | bytes 1048576 | tf_op jit(solution)/shard_map/all_to_all | solution.py:304
Sparse Core Ops, SparseCore 0:
  98.6 42.4 all-gather.2
  152.8 45.7 reduce-scatter.1

commit v2 on v1

--- a/solution.py
+++ b/solution.py
@@ -11,7 +11,6 @@
 HEAD_SIZE = 128
 TOP = 8
 CAP = 6
-SLOTS = 8
 F32 = jnp.float32
 BF16 = jnp.bfloat16
 VMEM_LIMIT = 48 * 1024 * 1024
@@ -86,8 +85,11 @@
 
 
 def routed(ids):
-    row = lax.broadcasted_iota(jnp.int32, (16, 512), 1)
-    expert, place = row >> 3, row & 7
+    lane = lax.broadcasted_iota(jnp.int32, (16, 64 * 24), 1)
+    expert = (lane * 2731) >> 16
+    rest = lane - 24 * expert
+    piece = (rest * 10923) >> 16
+    place = rest - CAP * piece
     named = ids[:, 0:1] == expert
     for k in range(1, TOP):
         named = named | (ids[:, k : k + 1] == expert)
@@ -98,7 +100,13 @@
     before = jnp.dot(
         earlier.astype(F32).astype(BF16), named.astype(BF16), preferred_element_type=F32
     )
-    return jnp.where(before == place.astype(F32), named, 0.0), expert
+    return jnp.where(before == place.astype(F32), named, 0.0), expert, piece
+
+
+def by_piece(table, piece):
+    return jnp.concatenate(
+        [jnp.where(piece == c, table, 0.0) for c in range(4)], axis=0
+    ).astype(BF16)
 
 
 def combine_kernel(z_ref, part_ref, res_ref, gain_ref, ids_ref, hidden_ref, send_ref):
@@ -118,9 +126,10 @@
     hidden = jnp.concatenate(columns, axis=1) + res_ref[:, pl.ds(start, 512)].astype(F32)
     hidden_ref[...] = hidden
     row = (hidden * gain_ref[:, pl.ds(start, 512)]).astype(BF16)
-    table, _ = routed(ids_ref[...])
+    stacked = jnp.concatenate([row[:, c * 128 : (c + 1) * 128] for c in range(4)], axis=0)
+    table, _, piece = routed(ids_ref[...])
     send_ref[...] = lax.dot_general(
-        table.astype(BF16), row, (((0,), (0,)), ((), ())), preferred_element_type=F32
+        by_piece(table, piece), stacked, (((0,), (0,)), ((), ())), preferred_element_type=F32
     ).astype(BF16)
 
 
@@ -129,7 +138,7 @@
         combine_kernel,
         out_shape=(
             jax.ShapeDtypeStruct((16, 512), F32),
-            jax.ShapeDtypeStruct((512, 512), BF16),
+            jax.ShapeDtypeStruct((1536, 128), BF16),
         ),
         in_specs=[SMEM_SPEC] + [VMEM_SPEC] * 4,
         out_specs=(VMEM_SPEC, VMEM_SPEC),
@@ -139,12 +148,28 @@
     )(z, part, res, gain, ids)
 
 
+def pack_kernel(down_ref, out_ref):
+    for d in range(8):
+        out_ref[d] = down_ref[:, d * 512 : (d + 1) * 512]
+
+
+def pack(down):
+    return pl.pallas_call(
+        pack_kernel,
+        out_shape=jax.ShapeDtypeStruct((8, 128, 512), BF16),
+        in_specs=[VMEM_SPEC],
+        out_specs=VMEM_SPEC,
+        compiler_params=params(),
+        cost_estimate=cost(0, 2_100_000),
+        name="pack",
+    )(down)
+
+
 def compact_kernel(arrived_ref, out_ref, wide):
-    for c in range(4):
-        wide[c * 512 : (c + 1) * 512, :] = arrived_ref[:, c * 128 : (c + 1) * 128].astype(F32)
+    wide[...] = arrived_ref[...].astype(F32)
     for s in range(CAP):
         for c in range(4):
-            block = wide[pl.ds(c * 512 + s, 64, stride=SLOTS), :]
+            block = wide[pl.ds(c * CAP + s, 64, stride=4 * CAP), :]
             out_ref[s * 64 : (s + 1) * 64, c * 128 : (c + 1) * 128] = block.astype(BF16)
 
 
@@ -154,105 +179,92 @@
         out_shape=jax.ShapeDtypeStruct((384, 512), BF16),
         in_specs=[VMEM_SPEC],
         out_specs=VMEM_SPEC,
-        scratch_shapes=[pltpu.VMEM((2048, 128), F32)],
+        scratch_shapes=[pltpu.VMEM((1536, 128), F32)],
         compiler_params=params(),
         cost_estimate=cost(1_000_000, 1_000_000),
         name="compact",
     )(arrived)
 
 
-def expand_kernel(sum_ref, out_ref, wide):
-    for s in range(SLOTS):
+def gated_kernel(rows_ref, gate_ref, up_ref, gain_ref, out_ref, chunks, arrivals):
+    copies = [
+        pltpu.make_async_copy(rows_ref.at[d], chunks.at[d], arrivals.at[d]) for d in range(8)
+    ]
+    for copy in copies:
+        copy.start()
+    acc, square = None, None
+    for d in range(8):
+        copies[d].wait()
+        x = chunks[d]
+        cols = slice(d * 512, (d + 1) * 512)
+        weight = jnp.concatenate([gate_ref[cols, :], up_ref[cols, :]], axis=1)
+        dot = jnp.dot(x, weight, preferred_element_type=F32)
+        plain = x.astype(F32) * (1.0 / gain_ref[:, cols])
+        sq = plain * plain
+        sq = sq[:, 0:128] + sq[:, 128:256] + sq[:, 256:384] + sq[:, 384:512]
+        acc = dot if acc is None else acc + dot
+        square = sq if square is None else square + sq
+    mean = jnp.sum(square, axis=1, keepdims=True) * (1.0 / D)
+    scale = lax.rsqrt(mean + 1e-6)
+    gate = acc[:, 0:128] * scale
+    up = acc[:, 128:256] * scale
+    inner = (gate / (1.0 + jnp.exp(-gate)) * up).astype(BF16)
+    for d in range(8):
+        out_ref[d] = inner
+
+
+def gated(rows, gate, up, gain):
+    return pl.pallas_call(
+        gated_kernel,
+        out_shape=jax.ShapeDtypeStruct((8, 384, 128), BF16),
+        in_specs=[pl.BlockSpec(memory_space=pl.ANY)] + [VMEM_SPEC] * 3,
+        out_specs=VMEM_SPEC,
+        scratch_shapes=[pltpu.VMEM((8, 384, 512), BF16), pltpu.SemaphoreType.DMA((8,))],
+        compiler_params=params(),
+        cost_estimate=cost(810_000_000, 6_000_000, 50_000),
+        name="gated",
+    )(rows, gate, up, gain)
+
+
+def down_kernel(inner_ref, weight_ref, out_ref, wide):
+    total = None
+    for s in range(0, 8, 2):
+        inner = jnp.concatenate([inner_ref[s], inner_ref[s + 1]], axis=1)
+        weight = jnp.concatenate([weight_ref[s], weight_ref[s + 1]], axis=0)
+        dot = jnp.dot(inner, weight, preferred_element_type=F32)
+        total = dot if total is None else total + dot
+    for s in range(CAP):
         for c in range(4):
-            if s < CAP:
-                block = sum_ref[s * 64 : (s + 1) * 64, c * 128 : (c + 1) * 128].astype(F32)
-            else:
-                block = jnp.zeros((64, 128), F32)
-            wide[pl.ds(c * 512 + s, 64, stride=SLOTS), :] = block
-    for c in range(4):
-        out_ref[:, c * 128 : (c + 1) * 128] = wide[c * 512 : (c + 1) * 512, :].astype(BF16)
-
-
-def expand(summed):
-    return pl.pallas_call(
-        expand_kernel,
-        out_shape=jax.ShapeDtypeStruct((512, 512), BF16),
-        in_specs=[VMEM_SPEC],
-        out_specs=VMEM_SPEC,
-        scratch_shapes=[pltpu.VMEM((2048, 128), F32)],
-        compiler_params=params(),
-        cost_estimate=cost(1_000_000, 1_000_000),
-        name="expand",
-    )(summed)
-
-
-def expert_kernel(x_ref, gate_ref, up_ref, gain_ref, down_ref, out_ref, acc, square, inner):
-    step = pl.program_id(0)
-
-    @pl.when(step == 0)
-    def _():
-        acc[...] = jnp.zeros_like(acc)
-        square[...] = jnp.zeros_like(square)
-
-    @pl.when(step < 8)
-    def _():
-        x = x_ref[0]
-        weight = jnp.concatenate([gate_ref[...], up_ref[...]], axis=1)
-        acc[...] += jnp.dot(x, weight, preferred_element_type=F32)
-        plain = x.astype(F32) * (1.0 / gain_ref[...])
-        sq = plain * plain
-        square[...] += sq[:, 0:128] + sq[:, 128:256] + sq[:, 256:384] + sq[:, 384:512]
-
-    @pl.when(step == 7)
-    def _():
-        mean = jnp.sum(square[...], axis=1, keepdims=True) * (1.0 / D)
-        scale = lax.rsqrt(mean + 1e-6)
-        gate = acc[:, 0:128] * scale
-        up = acc[:, 128:256] * scale
-        inner[...] = (gate / (1.0 + jnp.exp(-gate)) * up).astype(BF16)
-
-    @pl.when(step >= 8)
-    def _():
-        out_ref[0] = jnp.dot(inner[...], down_ref[...], preferred_element_type=F32).astype(BF16)
-
-
-def expert(x, gate, up, gain, down):
-    early = lambda g: jnp.minimum(g, 7)
-    late = lambda g: jnp.maximum(g - 8, 0)
-    return pl.pallas_call(
-        expert_kernel,
-        out_shape=jax.ShapeDtypeStruct((8, 384, 512), BF16),
-        grid=(16,),
-        in_specs=[
-            pl.BlockSpec((1, 384, 512), lambda g: (early(g), 0, 0)),
-            pl.BlockSpec((512, 128), lambda g: (early(g), 0)),
-            pl.BlockSpec((512, 128), lambda g: (early(g), 0)),
-            pl.BlockSpec((1, 512), lambda g: (0, early(g))),
-            pl.BlockSpec((128, 512), lambda g: (0, late(g))),
-        ],
-        out_specs=pl.BlockSpec((1, 384, 512), lambda g: (late(g), 0, 0)),
-        scratch_shapes=[
-            pltpu.VMEM((384, 256), F32),
-            pltpu.VMEM((384, 128), F32),
-            pltpu.VMEM((384, 128), BF16),
-        ],
-        compiler_params=params(),
-        cost_estimate=cost(1_200_000_000, 10_000_000),
-        name="expert",
-    )(x, gate, up, gain, down)
+            block = total[s * 64 : (s + 1) * 64, c * 128 : (c + 1) * 128]
+            wide[pl.ds(c * CAP + s, 64, stride=4 * CAP), :] = block
+    out_ref[...] = wide[...].astype(BF16)
+
+
+def down_columns(inner, weight):
+    return pl.pallas_call(
+        down_kernel,
+        out_shape=jax.ShapeDtypeStruct((1536, 128), BF16),
+        in_specs=[VMEM_SPEC] * 2,
+        out_specs=VMEM_SPEC,
+        scratch_shapes=[pltpu.VMEM((1536, 128), F32)],
+        compiler_params=params(),
+        cost_estimate=cost(400_000_000, 2_500_000),
+        name="down",
+    )(inner, weight)
 
 
 def mix_kernel(hidden_ref, back_ref, ids_ref, gates_ref, out_ref):
     ids = ids_ref[...]
     gates = gates_ref[...].astype(F32)
-    table, expert = routed(ids)
-    weight = jnp.zeros((16, 512), F32)
+    table, expert, piece = routed(ids)
+    weight = jnp.zeros(table.shape, F32)
     for k in range(TOP):
         weight = weight + jnp.where(ids[:, k : k + 1] == expert, gates[:, k : k + 1], 0.0)
-    mixing = (weight * table).astype(BF16)
-    out_ref[...] = (
-        hidden_ref[...] + jnp.dot(mixing, back_ref[...], preferred_element_type=F32)
-    ).astype(BF16)
+    total = jnp.dot(by_piece(weight * table, piece), back_ref[...], preferred_element_type=F32)
+    for c in range(4):
+        out_ref[:, c * 128 : (c + 1) * 128] = (
+            hidden_ref[:, c * 128 : (c + 1) * 128] + total[c * 16 : (c + 1) * 16]
+        ).astype(BF16)
 
 
 def mix(hidden, back, ids, gates):
@@ -265,6 +277,15 @@
         cost_estimate=cost(10_000_000, 600_000),
         name="mix",
     )(hidden, back, ids, gates)
+
+
+def exchange(v, axes):
+    return lax.all_to_all(v, axes, split_axis=0, concat_axis=0, tiled=True)
+
+
+def plane_exchange(v):
+    v = exchange(v.reshape(64, 4 * CAP, 128), ("ctx", "att"))
+    return v.reshape(256 * CAP, 128)
 
 
 def per_device(
@@ -282,29 +303,30 @@
 ):
     z = lax.axis_index("exp")
     devices = lax.axis_size(("ctx", "exp"))
+    ring = lax.axis_size("exp")
     context = keys.shape[2]
     start = lax.axis_index(("ctx", "exp")) * context
     gain = norm_gain.reshape(1, D)
     ids, gates = expert_ids[0], gate_values[0]
     gate, up, down = gate_weight[0], up_weight[0], down_weight[0]
 
-    spread = jnp.broadcast_to(queries, (devices,) + queries.shape[1:])
-    q = lax.all_to_all(spread, ("ctx", "exp"), split_axis=0, concat_axis=0, tiled=True)
-    q = q.reshape(devices * queries.shape[1], D)
+    def gathered(v, axis):
+        v = jnp.broadcast_to(v[None], (lax.axis_size(axis),) + v.shape)
+        return exchange(v, axis)
+
+    q = gathered(queries[0], "exp").reshape(ring * queries.shape[1], D)
+    q = gathered(q, "ctx").reshape(devices * queries.shape[1], D)
     part = attention(lengths[0] - start, q, keys[0], values[0])
-    part = lax.all_to_all(part, ("ctx", "exp"), split_axis=0, concat_axis=0, tiled=True)
+    part = exchange(part, ("ctx", "exp"))
     hidden, outbound = combine(z.reshape(1), part, residual[0], gain, ids)
-    arrived = lax.all_to_all(
-        outbound.reshape(64, SLOTS, 512), ("ctx", "att"), split_axis=0, concat_axis=0, tiled=True
-    )
-    own = compact(arrived.reshape(512, 512))
+    own = compact(plane_exchange(outbound))
+
+    own, down = lax.optimization_barrier((own, down))
     rows = lax.all_gather(own, "exp", axis=0)
-    sums = expert(rows, gate, up, gain, down)
-    back = expand(lax.psum_scatter(sums, "exp", scatter_dimension=0))
-    back = lax.all_to_all(
-        back.reshape(64, SLOTS, 512), ("ctx", "att"), split_axis=0, concat_axis=0, tiled=True
-    )
-    return mix(hidden, back.reshape(512, 512), ids, gates)[None]
+    by_column = exchange(pack(down), "exp")
+    units = exchange(gated(rows, gate, up, gain), "exp")
+    back = down_columns(units, by_column)
+    return mix(hidden, plane_exchange(back), ids, gates)[None]
 
 
 def solution(mesh):

time: 239 us -> 220 us (0.921)
  waiting for transfers between devices: 136 us -> 90.6 us
  blocking collectives: 30 us -> 74.7 us
  starting transfers between devices: 34.1 us -> 20 us
  Pallas kernels: 18.1 us -> 12.9 us
    reduce_scatter x1 -> x0, waiting for transfers between devices: 45.9 us -> none  [per_device(): back = expand(lax.psum_scatter(sums, 'exp', scatter_dimension=0))]
    all_to_all x1 -> x3, blocking collectives: 30 us -> 74.7 us  [exchange(): return lax.all_to_all(v, axes, split_axis=0, concat_axis=0, tiled=True)]
    all_to_all x3 -> x4, starting transfers between devices: 34 us -> 20 us  [exchange(): return lax.all_to_all(v, axes, split_axis=0, concat_axis=0, tiled=True)]
    all_gather x1, waiting for transfers between devices: 42.6 us -> 56.1 us  [per_device(): rows = lax.all_gather(own, 'exp', axis=0)]
    all_to_all x3 -> x4, waiting for transfers between devices: 47.2 us -> 34.4 us  [exchange(): return lax.all_to_all(v, axes, split_axis=0, concat_axis=0, tiled=True)]
    pallas_call x2 -> x3, Pallas kernels: 11.5 us -> 6.32 us  [the longest x1 3.86 us: gated(): pl.pallas_call(gated_kernel, out_shape=jax.ShapeDtypeStruct((8, 384, 128)...]
  transfers between devices with their start and end apart: 5 -> 5, of which waited for: 5 -> 4; matrix products, arithmetic and copies ran while one was open for 0% -> 0% of each run, Pallas kernels for 0% -> 2%
where the time goes in v2:
time: 220 us; the launch traced here: 219 us
  waiting for transfers between devices  90.6 us (41%)
  blocking collectives  74.7 us (34%)
  starting transfers between devices  20 us (9%)
  between operations  13.5 us (6%)
  Pallas kernels  12.9 us (6%)
  local copies, waits for them, and re-layouts  7.09 us (3%)
    all_to_all x3, blocking collectives, exchange(): return lax.all_to_all(v, axes, split_axis=0, concat_axis=0, tiled=True)  74.7 us
    all_gather x1, waiting for transfers between devices, per_device(): rows = lax.all_gather(own, 'exp', axis=0)  56.1 us
    all_to_all x4, waiting for transfers between devices, exchange(): return lax.all_to_all(v, axes, split_axis=0, concat_axis=0, tiled=True)  34.4 us
    all_to_all x4, starting transfers between devices, exchange(): return lax.all_to_all(v, axes, split_axis=0, concat_axis=0, tiled=True)  20 us
    unnamed x20, local copies, waits for them, and re-layouts  5.22 us
  transfers between devices with their start and end apart: 5, of which 4 were waited for; matrix products, arithmetic and copies ran while one was open for 0% of the time, Pallas kernels for 2%

profile of v2, /device:TPU:1, one launch (start us, length us, event | category | flops | bytes accessed | tf_op | source)
XLA Modules:
  0.0 219.4 jit_solution(5454014002240007040)
XLA Ops:
  6.5 0.8 broadcast_in_dim.18
  7.4 18.4 %all_to_all.35 = bf16[8,2,4096]{2,1,0:T(2,128)(2,1)S(1)} all-to-all(bf16[8,2,4096]{2,1,0:T(2,128)(2,1)S(1)} %broadcast_in_dim.18), channel_id=1, replica_groups=mesh['ctx'=4,'att'=16,'exp'=8] {'exp'}, dimensions={0} | all-to-all | bytes 262144 | tf_op jit(solution)/shard_map/all_to_all | solution.py:283
  25.9 0.8 broadcast_in_dim.20
  26.7 4.0 %all-to-all-start.1 = ((bf16[4,16,4096]{2,1,0:T(8,128)(2,1)}), bf16[4,16,4096]{2,1,0:T(8,128)(2,1)S(1)}, u32[]{:S(2)}, u32[]{:S(2)}) async-start(bf16[4,16,4096]{2,1,0:T(8,128)(2,1)} %broadcast_in_dim.20), calls=%async_computation.1 | async-start | bytes 1048576 | tf_op jit(solution)/shard_map/all_to_all | solution.py:283
  31.4 6.3 %all-to-all-done.1 = bf16[4,16,4096]{2,1,0:T(8,128)(2,1)S(1)} async-done(((bf16[4,16,4096]{2,1,0:T(8,128)(2,1)}), bf16[4,16,4096]{2,1,0:T(8,128)(2,1)S(1)}, u32[]{:S(2)}, u32[]{:S(2)}) %all-to-all-start.1) | async-done | bytes 524320 | tf_op jit(solution)/shard_map/all_to_all | solution.py:283
  37.7 1.0 copy-done.4
  38.7 1.0 copy-done.5
  39.7 3.8 %attention.1 = bf16[32,80,128]{2,1,0:T(8,128)(2,1)} custom-call(s32[2]{0:T(128)S(1)} %subtract_bitcast_fusion.limit_ref, bf16[64,4096]{1,0:T(8,128)(2,1)S(1)} %bitcast.21, bf16[2,512,256]{2,1,0:T(8,128)(2,1)S(1)} %bitcast.27, bf16[2,512,256]{2,1,0:T(8,128)(2,1)S(1)} %bitcast.28), custom_call_target="tpu_custom_call" | custom-call | flops 540000000 | bytes 2200000 | tf_op jit(solution)/shard_map/attention/pallas_call | solution.py:76
  43.6 3.9 %all-to-all-start.2 = ((bf16[32,80,128]{2,1,0:T(8,128)(2,1)}), bf16[32,80,128]{2,1,0:T(8,128)(2,1)S(1)}, u32[]{:S(2)}, u32[]{:S(2)}) async-start(bf16[32,80,128]{2,1,0:T(8,128)(2,1)} %attention.1), calls=%async_computation.2 | async-start | bytes 1310720 | tf_op jit(solution)/shard_map/all_to_all | solution.py:283
  47.6 13.6 %all-to-all-done.2.part_ref = bf16[32,80,128]{2,1,0:T(8,128)(2,1)S(1)} async-done(((bf16[32,80,128]{2,1,0:T(8,128)(2,1)}), bf16[32,80,128]{2,1,0:T(8,128)(2,1)S(1)}, u32[]{:S(2)}, u32[]{:S(2)}) %all-to-all-start.2) | async-done | bytes 655392 | tf_op jit(solution)/shard_map/all_to_all | solution.py:283
  61.3 0.7 combine.1
  62.0 29.7 %all_to_all.36 = bf16[64,24,128]{2,1,0:T(8,128)(2,1)S(1)} all-to-all(bf16[64,24,128]{2,1,0:T(8,128)(2,1)S(1)} %bitcast.29), channel_id=1, replica_groups=mesh['ctx'=4,'att'=16,'exp'=8] {'ctx','att'}, dimensions={0} | all-to-all | bytes 786432 | tf_op jit(solution)/shard_map/all_to_all | solution.py:283
  91.7 0.9 compact.1
  92.7 1.0 pack.1
  93.7 4.3 %all-to-all-start.5 = ((bf16[8,128,512]{2,1,0:T(8,128)(2,1)}), bf16[8,128,512]{2,1,0:T(8,128)(2,1)S(1)}, u32[]{:S(2)}, u32[]{:S(2)}) async-start(bf16[8,128,512]{2,1,0:T(8,128)(2,1)} %pack.1), calls=%async_computation.5 | async-start | bytes 2097152 | tf_op jit(solution)/shard_map/all_to_all | solution.py:283
  98.1 56.1 %all-gather.3.cloned.1.call-done = bf16[3072,512]{1,0:T(8,128)(2,1)} async-done(((bf16[384,512]{1,0:T(8,128)(2,1)}), bf16[3072,512]{1,0:T(8,128)(2,1)}) %all-gather.3.cloned.1.call-update) | async-done | bytes 3145744 | tf_op jit(solution)/shard_map/all_gather | solution.py:325
  154.2 1.9 copy-done
  156.1 1.2 copy-done.3
  157.3 3.9 %gated.1 = bf16[8,384,128]{2,1,0:T(8,128)(2,1)S(1)} custom-call(bf16[8,384,512]{2,1,0:T(8,128)(2,1)S(1)} %bitcast.20, bf16[4096,128]{1,0:T(8,128)(2,1)S(1)} %bitcast.25, bf16[4096,128]{1,0:T(8,128)(2,1)S(1)} %bitcast.26, f32[1,4096]{1,0:T(1,128)S(1)} %bitcast.32), custom_call_target="tpu_custom_call" | custom-call | flops 810000000 | bytes 6000000 | tf_op jit(solution)/shard_map/gated/pallas_call | solution.py:217
  161.2 26.6 %all_to_all.37.inner_ref = bf16[8,384,128]{2,1,0:T(8,128)(2,1)S(1)} all-to-all(bf16[8,384,128]{2,1,0:T(8,128)(2,1)S(1)} %gated.1), channel_id=1, replica_groups=mesh['ctx'=4,'att'=16,'exp'=8] {'exp'}, dimensions={0} | all-to-all | bytes 1572864 | tf_op jit(solution)/shard_map/all_to_all | solution.py:283
  187.8 1.4 down.1
  189.2 7.7 %all-to-all-start.6 = ((bf16[64,24,128]{2,1,0:T(8,128)(2,1)}), bf16[64,24,128]{2,1,0:T(8,128)(2,1)S(1)}, u32[]{:S(2)}, u32[]{:S(2)}) async-start(bf16[64,24,128]{2,1,0:T(8,128)(2,1)} %bitcast.15), calls=%async_computation.6 | async-start | bytes 786432 | tf_op jit(solution)/shard_map/all_to_all | solution.py:283
  197.0 14.5 %all-to-all-done.6 = bf16[64,24,128]{2,1,0:T(8,128)(2,1)S(1)} async-done(((bf16[64,24,128]{2,1,0:T(8,128)(2,1)}), bf16[64,24,128]{2,1,0:T(8,128)(2,1)S(1)}, u32[]{:S(2)}, u32[]{:S(2)}) %all-to-all-start.6) | async-done | bytes 393248 | tf_op jit(solution)/shard_map/all_to_all | solution.py:283
  211.5 1.1 mix.1
  (23 shorter events, 1.0 us)
Async XLA Ops:
  6.5 41.0 %copy-start.8 = (s32[1,16,8]{1,2,0:T(8,128)S(1)}, s32[1,16,8]{1,2,0:T(8,128)}, u32[]{:S(2)}) copy-start(s32[1,16,8]{1,2,0:T(8,128)} %param.17) | copy-start | bytes 1540
  6.5 54.7 %copy-start.6 = (bf16[1,16,4096]{2,1,0:T(8,128)(2,1)S(1)}, bf16[1,16,4096]{2,1,0:T(8,128)(2,1)}, u32[]{:S(2)}) copy-start(bf16[1,16,4096]{2,1,0:T(8,128)(2,1)} %param.15) | copy-start | bytes 393220
  6.5 54.7 %copy-start.7 = (f32[4096]{0:T(1024)S(1)}, f32[4096]{0:T(1024)}, u32[]{:S(2)}) copy-start(f32[4096]{0:T(1024)} %param.16) | copy-start | bytes 49156
  26.7 11.0 %all-to-all-start.1 = ((bf16[4,16,4096]{2,1,0:T(8,128)(2,1)}), bf16[4,16,4096]{2,1,0:T(8,128)(2,1)S(1)}, u32[]{:S(2)}, u32[]{:S(2)}) async-start(bf16[4,16,4096]{2,1,0:T(8,128)(2,1)} %broadcast_in_dim.20), calls=%async_computation.1 | async-start | bytes 1048576 | tf_op jit(solution)/shard_map/all_to_all | solution.py:283
  37.7 1.0 copy-start.4
  38.7 1.0 copy-start.5
  39.7 52.9 %copy-start.1 = (bf16[1,128,4096]{2,1,0:T(8,128)(2,1)S(1)}, bf16[1,128,4096]{2,1,0:T(8,128)(2,1)}, u32[]{:S(2)}) copy-start(bf16[1,128,4096]{2,1,0:T(8,128)(2,1)} %param.21) | copy-start | bytes 3145732
  43.6 17.7 %all-to-all-start.2 = ((bf16[32,80,128]{2,1,0:T(8,128)(2,1)}), bf16[32,80,128]{2,1,0:T(8,128)(2,1)S(1)}, u32[]{:S(2)}, u32[]{:S(2)}) async-start(bf16[32,80,128]{2,1,0:T(8,128)(2,1)} %attention.1), calls=%async_computation.2 | async-start | bytes 1310720 | tf_op jit(solution)/shard_map/all_to_all | solution.py:283
  47.5 106.7 %all-gather.3.cloned.1.call-start = ((), (), s32[]{:S(2)}) async-start(), calls=%async_computation.7 | async-start | bytes 3538944 | tf_op jit(solution)/shard_map/all_gather | solution.py:325
  62.0 92.2 %copy-start.2 = (bf16[1,4096,128]{2,1,0:T(8,128)(2,1)S(1)}, bf16[1,4096,128]{2,1,0:T(8,128)(2,1)}, u32[]{:S(2)}) copy-start(bf16[1,4096,128]{2,1,0:T(8,128)(2,1)} %param.19) | copy-start | bytes 3145732
  93.7 67.5 %all-to-all-start.5 = ((bf16[8,128,512]{2,1,0:T(8,128)(2,1)}), bf16[8,128,512]{2,1,0:T(8,128)(2,1)S(1)}, u32[]{:S(2)}, u32[]{:S(2)}) async-start(bf16[8,128,512]{2,1,0:T(8,128)(2,1)} %pack.1), calls=%async_computation.5 | async-start | bytes 2097152 | tf_op jit(solution)/shard_map/all_to_all | solution.py:283
  154.2 1.9 copy-start
  156.1 1.2 copy-start.3
  161.2 35.7 %copy-start.9 = (bf16[1,16,8]{1,2,0:T(8,128)(2,1)S(1)}, bf16[1,16,8]{1,2,0:T(8,128)(2,1)}, u32[]{:S(2)}) copy-start(bf16[1,16,8]{1,2,0:T(8,128)(2,1)} %param.18) | copy-start | bytes 772
  189.2 22.3 %all-to-all-start.6 = ((bf16[64,24,128]{2,1,0:T(8,128)(2,1)}), bf16[64,24,128]{2,1,0:T(8,128)(2,1)S(1)}, u32[]{:S(2)}, u32[]{:S(2)}) async-start(bf16[64,24,128]{2,1,0:T(8,128)(2,1)} %bitcast.15), calls=%async_computation.6 | async-start | bytes 786432 | tf_op jit(solution)/shard_map/all_to_all | solution.py:283
Sparse Core Ops, SparseCore 0:
  92.8 61.3 all-gather.2

commit v3 on v2

--- a/solution.py
+++ b/solution.py
@@ -14,13 +14,15 @@
 F32 = jnp.float32
 BF16 = jnp.bfloat16
 VMEM_LIMIT = 48 * 1024 * 1024
+WHOLE_VMEM = 60 * 1024 * 1024
 
 VMEM_SPEC = pl.BlockSpec(memory_space=pltpu.VMEM)
+HBM_SPEC = pl.BlockSpec(memory_space=pltpu.HBM)
 SMEM_SPEC = pl.BlockSpec(memory_space=pltpu.SMEM)
 
 
-def params():
-    return pltpu.CompilerParams(vmem_limit_bytes=VMEM_LIMIT)
+def params(limit=VMEM_LIMIT):
+    return pltpu.CompilerParams(vmem_limit_bytes=limit)
 
 
 def cost(flops, bytes_accessed, transcendentals=0):
@@ -29,7 +31,17 @@
     )
 
 
-def attention_kernel(limit_ref, q_ref, k_ref, v_ref, out_ref):
+def attention_kernel(limit_ref, q_ref, keys_ref, values_ref, out_ref, k_ref, v_ref, arrivals):
+    copies = [
+        [
+            pltpu.make_async_copy(source.at[r], target.at[r], arrivals.at[i, r])
+            for i, (source, target) in enumerate(((keys_ref, k_ref), (values_ref, v_ref)))
+        ]
+        for r in range(2)
+    ]
+    for r in range(2):
+        for copy in copies[r]:
+            copy.start()
     group = QUERY_HEADS // KEY_VALUE_HEADS
     lane = lax.broadcasted_iota(jnp.int32, (16, 128), 1)
     extent = k_ref.shape[1]
@@ -38,6 +50,8 @@
     draft = lax.broadcasted_iota(jnp.int32, (rows, extent), 0) & 31
     offset = position - draft
     for r in range(2):
+        for copy in copies[r]:
+            copy.wait()
         usable = offset < limit_ref[r]
         for g in range(KEY_VALUE_HEADS):
             query = jnp.concatenate(
@@ -76,9 +90,14 @@
     return pl.pallas_call(
         attention_kernel,
         out_shape=jax.ShapeDtypeStruct((32, 80, 128), BF16),
-        in_specs=[SMEM_SPEC, VMEM_SPEC, VMEM_SPEC, VMEM_SPEC],
+        in_specs=[SMEM_SPEC, VMEM_SPEC, HBM_SPEC, HBM_SPEC],
         out_specs=VMEM_SPEC,
-        compiler_params=params(),
+        scratch_shapes=[
+            pltpu.VMEM((2, 512, 256), BF16),
+            pltpu.VMEM((2, 512, 256), BF16),
+            pltpu.SemaphoreType.DMA((2, 2)),
+        ],
+        compiler_params=params(WHOLE_VMEM),
         cost_estimate=cost(540_000_000, 2_200_000, 1_100_000),
         name="attention",
     )(limits, q, keys, values)
@@ -148,23 +167,6 @@
     )(z, part, res, gain, ids)
 
 
-def pack_kernel(down_ref, out_ref):
-    for d in range(8):
-        out_ref[d] = down_ref[:, d * 512 : (d + 1) * 512]
-
-
-def pack(down):
-    return pl.pallas_call(
-        pack_kernel,
-        out_shape=jax.ShapeDtypeStruct((8, 128, 512), BF16),
-        in_specs=[VMEM_SPEC],
-        out_specs=VMEM_SPEC,
-        compiler_params=params(),
-        cost_estimate=cost(0, 2_100_000),
-        name="pack",
-    )(down)
-
-
 def compact_kernel(arrived_ref, out_ref, wide):
     wide[...] = arrived_ref[...].astype(F32)
     for s in range(CAP):
@@ -186,20 +188,44 @@
     )(arrived)
 
 
-def gated_kernel(rows_ref, gate_ref, up_ref, gain_ref, out_ref, chunks, arrivals):
-    copies = [
-        pltpu.make_async_copy(rows_ref.at[d], chunks.at[d], arrivals.at[d]) for d in range(8)
-    ]
-    for copy in copies:
-        copy.start()
+def expert_kernel(
+    rows_ref,
+    gate_ref,
+    up_ref,
+    down_ref,
+    gain_ref,
+    out_ref,
+    chunks,
+    gate_chunks,
+    up_chunks,
+    down_chunks,
+    results,
+    arrivals,
+    down_arrival,
+    departures,
+):
+    copies = []
+    for d in range(8):
+        cols = pl.ds(d * 512, 512)
+        copies.append(
+            (
+                pltpu.make_async_copy(gate_ref.at[cols], gate_chunks.at[d], arrivals.at[0, d]),
+                pltpu.make_async_copy(up_ref.at[cols], up_chunks.at[d], arrivals.at[1, d]),
+                pltpu.make_async_copy(rows_ref.at[d], chunks.at[d], arrivals.at[2, d]),
+            )
+        )
+        for copy in copies[d]:
+            copy.start()
+    down_copy = pltpu.make_async_copy(down_ref, down_chunks, down_arrival)
+    down_copy.start()
     acc, square = None, None
     for d in range(8):
-        copies[d].wait()
+        for copy in copies[d]:
+            copy.wait()
         x = chunks[d]
-        cols = slice(d * 512, (d + 1) * 512)
-        weight = jnp.concatenate([gate_ref[cols, :], up_ref[cols, :]], axis=1)
+        weight = jnp.concatenate([gate_chunks[d], up_chunks[d]], axis=1)
         dot = jnp.dot(x, weight, preferred_element_type=F32)
-        plain = x.astype(F32) * (1.0 / gain_ref[:, cols])
+        plain = x.astype(F32) * (1.0 / gain_ref[:, d * 512 : (d + 1) * 512])
         sq = plain * plain
         sq = sq[:, 0:128] + sq[:, 128:256] + sq[:, 256:384] + sq[:, 384:512]
         acc = dot if acc is None else acc + dot
@@ -209,48 +235,59 @@
     gate = acc[:, 0:128] * scale
     up = acc[:, 128:256] * scale
     inner = (gate / (1.0 + jnp.exp(-gate)) * up).astype(BF16)
+    down_copy.wait()
+    sends = []
     for d in range(8):
-        out_ref[d] = inner
-
-
-def gated(rows, gate, up, gain):
-    return pl.pallas_call(
-        gated_kernel,
-        out_shape=jax.ShapeDtypeStruct((8, 384, 128), BF16),
-        in_specs=[pl.BlockSpec(memory_space=pl.ANY)] + [VMEM_SPEC] * 3,
-        out_specs=VMEM_SPEC,
-        scratch_shapes=[pltpu.VMEM((8, 384, 512), BF16), pltpu.SemaphoreType.DMA((8,))],
-        compiler_params=params(),
-        cost_estimate=cost(810_000_000, 6_000_000, 50_000),
-        name="gated",
-    )(rows, gate, up, gain)
-
-
-def down_kernel(inner_ref, weight_ref, out_ref, wide):
-    total = None
-    for s in range(0, 8, 2):
-        inner = jnp.concatenate([inner_ref[s], inner_ref[s + 1]], axis=1)
-        weight = jnp.concatenate([weight_ref[s], weight_ref[s + 1]], axis=0)
-        dot = jnp.dot(inner, weight, preferred_element_type=F32)
-        total = dot if total is None else total + dot
+        results[d] = jnp.dot(
+            inner, down_chunks[:, d * 512 : (d + 1) * 512], preferred_element_type=F32
+        ).astype(BF16)
+        sends.append(pltpu.make_async_copy(results.at[d], out_ref.at[d], departures.at[d]))
+        sends[d].start()
+    for send in sends:
+        send.wait()
+
+
+def expert(rows, gate, up, down, gain):
+    return pl.pallas_call(
+        expert_kernel,
+        out_shape=jax.ShapeDtypeStruct((8, 384, 512), BF16),
+        in_specs=[HBM_SPEC] * 4 + [VMEM_SPEC],
+        out_specs=HBM_SPEC,
+        scratch_shapes=[
+            pltpu.VMEM((8, 384, 512), BF16),
+            pltpu.VMEM((8, 512, 128), BF16),
+            pltpu.VMEM((8, 512, 128), BF16),
+            pltpu.VMEM((128, 4096), BF16),
+            pltpu.VMEM((8, 384, 512), BF16),
+            pltpu.SemaphoreType.DMA((3, 8)),
+            pltpu.SemaphoreType.DMA,
+            pltpu.SemaphoreType.DMA((8,)),
+        ],
+        compiler_params=params(WHOLE_VMEM),
+        cost_estimate=cost(1_200_000_000, 9_500_000, 50_000),
+        name="expert",
+    )(rows, gate, up, down, gain)
+
+
+def expand_kernel(sum_ref, out_ref, wide):
     for s in range(CAP):
         for c in range(4):
-            block = total[s * 64 : (s + 1) * 64, c * 128 : (c + 1) * 128]
+            block = sum_ref[s * 64 : (s + 1) * 64, c * 128 : (c + 1) * 128].astype(F32)
             wide[pl.ds(c * CAP + s, 64, stride=4 * CAP), :] = block
     out_ref[...] = wide[...].astype(BF16)
 
 
-def down_columns(inner, weight):
-    return pl.pallas_call(
-        down_kernel,
+def expand(summed):
+    return pl.pallas_call(
+        expand_kernel,
         out_shape=jax.ShapeDtypeStruct((1536, 128), BF16),
-        in_specs=[VMEM_SPEC] * 2,
+        in_specs=[VMEM_SPEC],
         out_specs=VMEM_SPEC,
         scratch_shapes=[pltpu.VMEM((1536, 128), F32)],
         compiler_params=params(),
-        cost_estimate=cost(400_000_000, 2_500_000),
-        name="down",
-    )(inner, weight)
+        cost_estimate=cost(1_000_000, 1_000_000),
+        name="expand",
+    )(summed)
 
 
 def mix_kernel(hidden_ref, back_ref, ids_ref, gates_ref, out_ref):
@@ -303,29 +340,22 @@
 ):
     z = lax.axis_index("exp")
     devices = lax.axis_size(("ctx", "exp"))
-    ring = lax.axis_size("exp")
     context = keys.shape[2]
     start = lax.axis_index(("ctx", "exp")) * context
     gain = norm_gain.reshape(1, D)
     ids, gates = expert_ids[0], gate_values[0]
     gate, up, down = gate_weight[0], up_weight[0], down_weight[0]
 
-    def gathered(v, axis):
-        v = jnp.broadcast_to(v[None], (lax.axis_size(axis),) + v.shape)
-        return exchange(v, axis)
-
-    q = gathered(queries[0], "exp").reshape(ring * queries.shape[1], D)
-    q = gathered(q, "ctx").reshape(devices * queries.shape[1], D)
+    spread = jnp.broadcast_to(queries, (devices,) + queries.shape[1:])
+    q = exchange(spread, ("ctx", "exp")).reshape(devices * queries.shape[1], D)
     part = attention(lengths[0] - start, q, keys[0], values[0])
     part = exchange(part, ("ctx", "exp"))
     hidden, outbound = combine(z.reshape(1), part, residual[0], gain, ids)
+
     own = compact(plane_exchange(outbound))
-
-    own, down = lax.optimization_barrier((own, down))
     rows = lax.all_gather(own, "exp", axis=0)
-    by_column = exchange(pack(down), "exp")
-    units = exchange(gated(rows, gate, up, gain), "exp")
-    back = down_columns(units, by_column)
+    produced = expert(rows, gate, up, down, gain)
+    back = expand(lax.psum_scatter(produced, "exp", scatter_dimension=0))
     return mix(hidden, plane_exchange(back), ids, gates)[None]
 
 

time: 220 us -> 229 us (1.041)
  blocking collectives: 74.7 us -> 27.3 us
  waiting for transfers between devices: 90.6 us -> 132 us
  starting transfers between devices: 20 us -> 34.2 us
  Pallas kernels: 12.9 us -> 16.3 us
  local copies, waits for them, and re-layouts: 7.09 us -> 4.18 us
    all_to_all x3 -> x1, blocking collectives: 74.7 us -> 27.3 us  [exchange(): return lax.all_to_all(v, axes, split_axis=0, concat_axis=0, tiled=True)]
    reduce_scatter x0 -> x1, waiting for transfers between devices: none -> 45.7 us  [per_device(): back = expand(lax.psum_scatter(produced, 'exp', scatter_dimension=0))]
    all_to_all x4 -> x3, starting transfers between devices: 20 us -> 34.1 us  [exchange(): return lax.all_to_all(v, axes, split_axis=0, concat_axis=0, tiled=True)]
    all_gather x1, waiting for transfers between devices: 56.1 us -> 42.5 us  [per_device(): rows = lax.all_gather(own, 'exp', axis=0)]
    all_to_all x4 -> x3, waiting for transfers between devices: 34.4 us -> 43.9 us  [exchange(): return lax.all_to_all(v, axes, split_axis=0, concat_axis=0, tiled=True)]
    unnamed x20 -> x10, local copies, waits for them, and re-layouts: 5.22 us -> 1.01 us
    pallas_call x3 -> x2, Pallas kernels: 6.32 us -> 7.82 us  [the longest x1 6.87 us: expert(): pl.pallas_call(expert_kernel, out_shape=jax.ShapeDtypeStruct((8, 384, 512...]
  transfers between devices with their start and end apart: 5 -> 5, of which waited for: 4 -> 5; matrix products, arithmetic and copies ran while one was open for 0% -> 1% of each run, Pallas kernels for 2% -> 0%
where the time goes in v3:
time: 229 us
  waiting for transfers between devices  132 us (58%)
  starting transfers between devices  34.2 us (15%)
  blocking collectives  27.3 us (12%)
  Pallas kernels  16.3 us (7%)
  between operations  13.5 us (6%)
  local copies, waits for them, and re-layouts  4.18 us (2%)
    reduce_scatter x1, waiting for transfers between devices, per_device(): back = expand(lax.psum_scatter(produced, 'exp', scatter_dimension=0))  45.7 us
    all_to_all x3, waiting for transfers between devices, exchange(): return lax.all_to_all(v, axes, split_axis=0, concat_axis=0, tiled=True)  43.9 us
    all_gather x1, waiting for transfers between devices, per_device(): rows = lax.all_gather(own, 'exp', axis=0)  42.5 us
    all_to_all x3, starting transfers between devices, exchange(): return lax.all_to_all(v, axes, split_axis=0, concat_axis=0, tiled=True)  34.1 us
    all_to_all x1, blocking collectives, exchange(): return lax.all_to_all(v, axes, split_axis=0, concat_axis=0, tiled=True)  27.3 us
    pallas_call x1, Pallas kernels, expert(): pl.pallas_call(expert_kernel, out_shape=jax.ShapeDtypeStruct((8, 384, 512...  6.87 us
    pallas_call x1, Pallas kernels, attention(): pl.pallas_call(attention_kernel, out_shape=jax.ShapeDtypeStruct((32, 80,...  5.73 us
  transfers between devices with their start and end apart: 5, of which 5 were waited for; matrix products, arithmetic and copies ran while one was open for 1% of the time, Pallas kernels for 0%

profile of v3, /device:TPU:1, one launch (start us, length us, event | category | flops | bytes accessed | tf_op | source)
XLA Modules:
  0.0 228.9 jit_solution(10965477321984306541)
XLA Ops:
  6.5 2.0 broadcast_in_dim.11
  8.6 13.7 %all-to-all-start = ((bf16[32,2,4096]{2,1,0:T(2,128)(2,1)}), bf16[32,2,4096]{2,1,0:T(2,128)(2,1)S(1)}, u32[]{:S(2)}, u32[]{:S(2)}) async-start(bf16[32,2,4096]{2,1,0:T(2,128)(2,1)} %broadcast_in_dim.11), calls=%async_computation | async-start | bytes 1048576 | tf_op jit(solution)/shard_map/all_to_all | solution.py:320
  22.3 1.2 subtract_bitcast_fusion.limit_ref
  23.5 13.1 %all-to-all-done = bf16[32,2,4096]{2,1,0:T(2,128)(2,1)S(1)} async-done(((bf16[32,2,4096]{2,1,0:T(2,128)(2,1)}), bf16[32,2,4096]{2,1,0:T(2,128)(2,1)S(1)}, u32[]{:S(2)}, u32[]{:S(2)}) %all-to-all-start) | async-done | bytes 524320 | tf_op jit(solution)/shard_map/all_to_all | solution.py:320
  36.6 1.0 reshape.24.q_ref
  37.6 5.7 %attention.1 = bf16[32,80,128]{2,1,0:T(8,128)(2,1)} custom-call(s32[2]{0:T(128)} %subtract_bitcast_fusion.limit_ref, bf16[64,4096]{1,0:T(8,128)(2,1)} %reshape.24.q_ref, bf16[2,512,256]{2,1,0:T(8,128)(2,1)} %bitcast.31, bf16[2,512,256]{2,1,0:T(8,128)(2,1)} %bitcast.32), custom_call_target="tpu_custom_call" | custom-call | flops 540000000 | bytes 2200000 | tf_op jit(solution)/shard_map/attention/pallas_call | solution.py:90
  43.3 7.5 %all-to-all-start.1 = ((bf16[32,80,128]{2,1,0:T(8,128)(2,1)}), bf16[32,80,128]{2,1,0:T(8,128)(2,1)S(1)}, u32[]{:S(2)}, u32[]{:S(2)}) async-start(bf16[32,80,128]{2,1,0:T(8,128)(2,1)} %attention.1), calls=%async_computation.1 | async-start | bytes 1310720 | tf_op jit(solution)/shard_map/all_to_all | solution.py:320
  50.8 0.0 all-gather.3.cloned.1.call-start
  50.9 0.1 copy.12.ids_ref
  51.0 16.3 %all-to-all-done.1.part_ref = bf16[32,80,128]{2,1,0:T(8,128)(2,1)S(1)} async-done(((bf16[32,80,128]{2,1,0:T(8,128)(2,1)}), bf16[32,80,128]{2,1,0:T(8,128)(2,1)S(1)}, u32[]{:S(2)}, u32[]{:S(2)}) %all-to-all-start.1) | async-done | bytes 655392 | tf_op jit(solution)/shard_map/all_to_all | solution.py:320
  67.3 0.8 combine.1
  68.0 27.3 %all_to_all.20 = bf16[64,24,128]{2,1,0:T(8,128)(2,1)S(1)} all-to-all(bf16[64,24,128]{2,1,0:T(8,128)(2,1)S(1)} %bitcast.23), channel_id=1, replica_groups=mesh['ctx'=4,'att'=16,'exp'=8] {'ctx','att'}, dimensions={0} | all-to-all | bytes 786432 | tf_op jit(solution)/shard_map/all_to_all | solution.py:320
  95.3 0.9 compact.1
  96.3 0.0 reduce-scatter.2.cloned.1.call-start
  96.4 42.5 %all-gather.3.cloned.1.call-done = bf16[3072,512]{1,0:T(8,128)(2,1)} async-done(((bf16[384,512]{1,0:T(8,128)(2,1)}), bf16[3072,512]{1,0:T(8,128)(2,1)}) %all-gather.3.cloned.1.call-update) | async-done | bytes 3145744 | tf_op jit(solution)/shard_map/all_gather | solution.py:356
  138.9 6.9 %expert.1 = bf16[8,384,512]{2,1,0:T(8,128)(2,1)} custom-call(bf16[8,384,512]{2,1,0:T(8,128)(2,1)} %bitcast.27, bf16[4096,128]{1,0:T(8,128)(2,1)} %bitcast.28, bf16[4096,128]{1,0:T(8,128)(2,1)} %bitcast.29, bf16[128,4096]{1,0:T(8,128)(2,1)} %bitcast.30, f32[1,4096]{1,0:T(1,128)} %bitcast.25), custom_call_target="tpu_custom_call" | custom-call | flops 1200000000 | bytes 9500000 | tf_op jit(solution)/shard_map/expert/pallas_call | solution.py:251
  145.7 0.0 reduce-scatter.2.cloned.1.call-update
  145.8 45.7 %reduce-scatter.2.cloned.1.call-done = bf16[1,384,512]{2,1,0:T(8,128)(2,1)} async-done(((bf16[8,384,512]{2,1,0:T(8,128)(2,1)}), bf16[1,384,512]{2,1,0:T(8,128)(2,1)}) %reduce-scatter.2.cloned.1.call-update) | async-done | bytes 393232 | tf_op jit(solution)/shard_map/reduce_scatter | solution.py:358
  191.5 1.0 copy-done
  192.5 1.0 expand.1
  193.4 12.9 %all-to-all-start.3 = ((bf16[64,24,128]{2,1,0:T(8,128)(2,1)}), bf16[64,24,128]{2,1,0:T(8,128)(2,1)S(1)}, u32[]{:S(2)}, u32[]{:S(2)}) async-start(bf16[64,24,128]{2,1,0:T(8,128)(2,1)} %bitcast.15), calls=%async_computation.4 | async-start | bytes 786432 | tf_op jit(solution)/shard_map/all_to_all | solution.py:320
  206.4 0.1 copy.14.gates_ref
  206.5 14.5 %all-to-all-done.3 = bf16[64,24,128]{2,1,0:T(8,128)(2,1)S(1)} async-done(((bf16[64,24,128]{2,1,0:T(8,128)(2,1)}), bf16[64,24,128]{2,1,0:T(8,128)(2,1)S(1)}, u32[]{:S(2)}, u32[]{:S(2)}) %all-to-all-start.3) | async-done | bytes 393248 | tf_op jit(solution)/shard_map/all_to_all | solution.py:320
  221.0 1.1 mix.1
  (10 shorter events, 0.0 us)
Async XLA Ops:
  6.5 44.3 %copy-start.3 = (s32[1,16,8]{1,2,0:T(8,128)S(1)}, s32[1,16,8]{1,2,0:T(8,128)}, u32[]{:S(2)}) copy-start(s32[1,16,8]{1,2,0:T(8,128)} %param.17) | copy-start | bytes 1540
  6.5 60.7 %copy-start.1 = (bf16[1,16,4096]{2,1,0:T(8,128)(2,1)S(1)}, bf16[1,16,4096]{2,1,0:T(8,128)(2,1)}, u32[]{:S(2)}) copy-start(bf16[1,16,4096]{2,1,0:T(8,128)(2,1)} %param.15) | copy-start | bytes 393220
  6.5 60.7 %copy-start.2 = (f32[4096]{0:T(1024)S(1)}, f32[4096]{0:T(1024)}, u32[]{:S(2)}) copy-start(f32[4096]{0:T(1024)} %param.16) | copy-start | bytes 49156
  8.6 28.0 %all-to-all-start = ((bf16[32,2,4096]{2,1,0:T(2,128)(2,1)}), bf16[32,2,4096]{2,1,0:T(2,128)(2,1)S(1)}, u32[]{:S(2)}, u32[]{:S(2)}) async-start(bf16[32,2,4096]{2,1,0:T(2,128)(2,1)} %broadcast_in_dim.11), calls=%async_computation | async-start | bytes 1048576 | tf_op jit(solution)/shard_map/all_to_all | solution.py:320
  43.3 23.9 %all-to-all-start.1 = ((bf16[32,80,128]{2,1,0:T(8,128)(2,1)}), bf16[32,80,128]{2,1,0:T(8,128)(2,1)S(1)}, u32[]{:S(2)}, u32[]{:S(2)}) async-start(bf16[32,80,128]{2,1,0:T(8,128)(2,1)} %attention.1), calls=%async_computation.1 | async-start | bytes 1310720 | tf_op jit(solution)/shard_map/all_to_all | solution.py:320
  50.8 88.0 %all-gather.3.cloned.1.call-start = ((), (), s32[]{:S(2)}) async-start(), calls=%async_computation.6 | async-start | bytes 3538944 | tf_op jit(solution)/shard_map/all_gather | solution.py:356
  96.3 95.2 %reduce-scatter.2.cloned.1.call-start = ((), (), s32[]{:S(2)}) async-start(), calls=%async_computation.5 | async-start | bytes 3538944 | tf_op jit(solution)/shard_map/reduce_scatter | solution.py:358
  145.7 60.7 %copy-start.4 = (bf16[1,16,8]{1,2,0:T(8,128)(2,1)S(1)}, bf16[1,16,8]{1,2,0:T(8,128)(2,1)}, u32[]{:S(2)}) copy-start(bf16[1,16,8]{1,2,0:T(8,128)(2,1)} %param.18) | copy-start | bytes 772
  191.5 1.0 copy-start
  193.4 27.5 %all-to-all-start.3 = ((bf16[64,24,128]{2,1,0:T(8,128)(2,1)}), bf16[64,24,128]{2,1,0:T(8,128)(2,1)S(1)}, u32[]{:S(2)}, u32[]{:S(2)}) async-start(bf16[64,24,128]{2,1,0:T(8,128)(2,1)} %bitcast.15), calls=%async_computation.4 | async-start | bytes 786432 | tf_op jit(solution)/shard_map/all_to_all | solution.py:320
Sparse Core Ops, SparseCore 0:
  96.4 42.3 all-gather.2
  145.9 45.5 reduce-scatter.1

commit v4 on v2

--- a/solution.py
+++ b/solution.py
@@ -165,20 +165,21 @@
     )(down)
 
 
-def compact_kernel(arrived_ref, out_ref, wide):
+def compact_kernel(arrived_ref, a_ref, b_ref, wide):
     wide[...] = arrived_ref[...].astype(F32)
     for s in range(CAP):
+        out_ref, at = (a_ref, s * 64) if s < 3 else (b_ref, (s - 3) * 64)
         for c in range(4):
             block = wide[pl.ds(c * CAP + s, 64, stride=4 * CAP), :]
-            out_ref[s * 64 : (s + 1) * 64, c * 128 : (c + 1) * 128] = block.astype(BF16)
+            out_ref[at : at + 64, c * 128 : (c + 1) * 128] = block.astype(BF16)
 
 
 def compact(arrived):
     return pl.pallas_call(
         compact_kernel,
-        out_shape=jax.ShapeDtypeStruct((384, 512), BF16),
+        out_shape=(jax.ShapeDtypeStruct((192, 512), BF16),) * 2,
         in_specs=[VMEM_SPEC],
-        out_specs=VMEM_SPEC,
+        out_specs=(VMEM_SPEC, VMEM_SPEC),
         scratch_shapes=[pltpu.VMEM((1536, 128), F32)],
         compiler_params=params(),
         cost_estimate=cost(1_000_000, 1_000_000),
@@ -186,44 +187,68 @@
     )(arrived)
 
 
-def gated_kernel(rows_ref, gate_ref, up_ref, gain_ref, out_ref, chunks, arrivals):
-    copies = [
-        pltpu.make_async_copy(rows_ref.at[d], chunks.at[d], arrivals.at[d]) for d in range(8)
-    ]
-    for copy in copies:
-        copy.start()
-    acc, square = None, None
-    for d in range(8):
-        copies[d].wait()
-        x = chunks[d]
-        cols = slice(d * 512, (d + 1) * 512)
-        weight = jnp.concatenate([gate_ref[cols, :], up_ref[cols, :]], axis=1)
-        dot = jnp.dot(x, weight, preferred_element_type=F32)
-        plain = x.astype(F32) * (1.0 / gain_ref[:, cols])
-        sq = plain * plain
-        sq = sq[:, 0:128] + sq[:, 128:256] + sq[:, 256:384] + sq[:, 384:512]
-        acc = dot if acc is None else acc + dot
-        square = sq if square is None else square + sq
-    mean = jnp.sum(square, axis=1, keepdims=True) * (1.0 / D)
-    scale = lax.rsqrt(mean + 1e-6)
-    gate = acc[:, 0:128] * scale
-    up = acc[:, 128:256] * scale
-    inner = (gate / (1.0 + jnp.exp(-gate)) * up).astype(BF16)
-    for d in range(8):
-        out_ref[d] = inner
-
-
-def gated(rows, gate, up, gain):
+def chunk_sums(index_ref, halves, gate_ref, up_ref, gain_ref):
+    sums, squares = [None, None], [None, None]
+    for i in range(len(halves) // 2):
+        start = pl.multiple_of(index_ref[i] * 512, 512)
+        weight = jnp.concatenate(
+            [gate_ref[pl.ds(start, 512), :], up_ref[pl.ds(start, 512), :]], axis=1
+        )
+        inverse = 1.0 / gain_ref[:, pl.ds(start, 512)]
+        for half in range(2):
+            x = halves[2 * i + half][...]
+            dot = jnp.dot(x, weight, preferred_element_type=F32)
+            plain = x.astype(F32) * inverse
+            sq = plain * plain
+            sq = sq[:, 0:128] + sq[:, 128:256] + sq[:, 256:384] + sq[:, 384:512]
+            sums[half] = dot if i == 0 else sums[half] + dot
+            squares[half] = sq if i == 0 else squares[half] + sq
+    return sums, squares
+
+
+def early_kernel(index_ref, gate_ref, up_ref, gain_ref, *refs):
+    sums, squares = chunk_sums(index_ref, refs[:-1], gate_ref, up_ref, gain_ref)
+    for half in range(2):
+        refs[-1][half * 192 : (half + 1) * 192, 0:256] = sums[half]
+        refs[-1][half * 192 : (half + 1) * 192, 256:384] = squares[half]
+
+
+def early_sums(indices, gate, up, gain, halves):
+    return pl.pallas_call(
+        early_kernel,
+        out_shape=jax.ShapeDtypeStruct((384, 384), F32),
+        in_specs=[SMEM_SPEC] + [VMEM_SPEC] * (3 + len(halves)),
+        out_specs=VMEM_SPEC,
+        compiler_params=params(),
+        cost_estimate=cost(50_000_000 * len(halves), 4_000_000),
+        name="early_sums",
+    )(jnp.stack(indices), gate, up, gain, *halves)
+
+
+def gated_kernel(index_ref, early_ref, gate_ref, up_ref, gain_ref, *refs):
+    out_ref = refs[-1]
+    sums, squares = chunk_sums(index_ref, refs[:-1], gate_ref, up_ref, gain_ref)
+    for half in range(2):
+        rows = slice(half * 192, (half + 1) * 192)
+        square = early_ref[rows, 256:384] + squares[half]
+        scale = lax.rsqrt(jnp.sum(square, axis=1, keepdims=True) * (1.0 / D) + 1e-6)
+        gate = (early_ref[rows, 0:128] + sums[half][:, 0:128]) * scale
+        up = (early_ref[rows, 128:256] + sums[half][:, 128:256]) * scale
+        inner = (gate / (1.0 + jnp.exp(-gate)) * up).astype(BF16)
+        for d in range(8):
+            out_ref[d, rows, :] = inner
+
+
+def gated(indices, early, gate, up, gain, halves):
     return pl.pallas_call(
         gated_kernel,
         out_shape=jax.ShapeDtypeStruct((8, 384, 128), BF16),
-        in_specs=[pl.BlockSpec(memory_space=pl.ANY)] + [VMEM_SPEC] * 3,
-        out_specs=VMEM_SPEC,
-        scratch_shapes=[pltpu.VMEM((8, 384, 512), BF16), pltpu.SemaphoreType.DMA((8,))],
-        compiler_params=params(),
-        cost_estimate=cost(810_000_000, 6_000_000, 50_000),
+        in_specs=[SMEM_SPEC] + [VMEM_SPEC] * (4 + len(halves)),
+        out_specs=VMEM_SPEC,
+        compiler_params=params(),
+        cost_estimate=cost(50_000_000 * len(halves), 4_000_000, 50_000),
         name="gated",
-    )(rows, gate, up, gain)
+    )(jnp.stack(indices), early, gate, up, gain, *halves)
 
 
 def down_kernel(inner_ref, weight_ref, out_ref, wide):
@@ -310,21 +335,33 @@
     ids, gates = expert_ids[0], gate_values[0]
     gate, up, down = gate_weight[0], up_weight[0], down_weight[0]
 
-    def gathered(v, axis):
-        v = jnp.broadcast_to(v[None], (lax.axis_size(axis),) + v.shape)
-        return exchange(v, axis)
-
-    q = gathered(queries[0], "exp").reshape(ring * queries.shape[1], D)
-    q = gathered(q, "ctx").reshape(devices * queries.shape[1], D)
+    spread = jnp.broadcast_to(queries, (devices,) + queries.shape[1:])
+    q = exchange(spread, ("ctx", "exp")).reshape(devices * queries.shape[1], D)
     part = attention(lengths[0] - start, q, keys[0], values[0])
     part = exchange(part, ("ctx", "exp"))
     hidden, outbound = combine(z.reshape(1), part, residual[0], gain, ids)
-    own = compact(plane_exchange(outbound))
-
-    own, down = lax.optimization_barrier((own, down))
-    rows = lax.all_gather(own, "exp", axis=0)
-    by_column = exchange(pack(down), "exp")
-    units = exchange(gated(rows, gate, up, gain), "exp")
+    own_a, own_b = compact(plane_exchange(outbound))
+
+    own_a, own_b, packed = lax.optimization_barrier((own_a, own_b, pack(down)))
+    by_column = exchange(packed, "exp")
+    to_right = [(i, (i + 1) % ring) for i in range(ring)]
+    to_left = [(i, (i - 1) % ring) for i in range(ring)]
+    right = lambda v: lax.ppermute(v, "exp", to_right)
+    left = lambda v: lax.ppermute(v, "exp", to_left)
+    at = lambda k: lax.rem(z + (k + ring), ring).astype(jnp.int32)
+    halves, indices = [own_a, own_b], [at(0)]
+    ra, rb, la, lb = own_a, own_b, own_a, own_b
+    for k in range(1, 4):
+        ra, lb = right(ra), left(lb)
+        rb, la = right(rb), left(la)
+        halves += [ra, rb, la, lb]
+        indices += [at(-k), at(k)]
+    ra, lb, by_column = lax.optimization_barrier((ra, lb, by_column))
+    halves += [right(ra), left(lb)]
+    indices.append(at(4))
+
+    early = early_sums(indices[:5], gate, up, gain, halves[:10])
+    units = exchange(gated(indices[5:], early, gate, up, gain, halves[10:]), "exp")
     back = down_columns(units, by_column)
     return mix(hidden, plane_exchange(back), ids, gates)[None]
 

time: 220 us -> 222 us (level)
  starting transfers between devices: 20 us -> 96.3 us
  blocking collectives: 74.7 us -> 21.3 us
  waiting for transfers between devices: 90.6 us -> 73.6 us
  between operations: 13.5 us -> 0.42 us
  local copies, waits for them, and re-layouts: 7.09 us -> 17.3 us
    all_gather x1 -> x0, waiting for transfers between devices: 56.1 us -> none  [per_device(): rows = lax.all_gather(own, 'exp', axis=0)]
    all_to_all x3 -> x1, blocking collectives: 74.7 us -> 21.3 us  [exchange(): return lax.all_to_all(v, axes, split_axis=0, concat_axis=0, tiled=True)]
    ppermute x0 -> x14, starting transfers between devices: none -> 45.4 us  [the longest x7 29.7 us: per_device(): left = lambda v: lax.ppermute(v, 'exp', to_left)]
    all_to_all x4 -> x5, starting transfers between devices: 20 us -> 50.9 us  [exchange(): return lax.all_to_all(v, axes, split_axis=0, concat_axis=0, tiled=True)]
    all_to_all x4 -> x5, waiting for transfers between devices: 34.4 us -> 56.8 us  [exchange(): return lax.all_to_all(v, axes, split_axis=0, concat_axis=0, tiled=True)]
    ppermute x0 -> x14, waiting for transfers between devices: none -> 16.8 us  [the longest x7 16.8 us: per_device(): right = lambda v: lax.ppermute(v, 'exp', to_right)]
    unnamed x20 -> x60, local copies, waits for them, and re-layouts: 5.22 us -> 14.4 us
  transfers between devices with their start and end apart: 5 -> 19, of which waited for: 4 -> 5; matrix products, arithmetic and copies ran while one was open for 0% -> 0% of each run, Pallas kernels for 2% -> 1%
where the time goes in v4:
time: 222 us; the launch traced here: 221 us
  starting transfers between devices  96.3 us (43%)
  waiting for transfers between devices  73.6 us (33%)
  blocking collectives  21.3 us (10%)
  local copies, waits for them, and re-layouts  17.3 us (8%)
  Pallas kernels  11.9 us (5%)
    all_to_all x5, waiting for transfers between devices, exchange(): return lax.all_to_all(v, axes, split_axis=0, concat_axis=0, tiled=True)  56.8 us
    all_to_all x5, starting transfers between devices, exchange(): return lax.all_to_all(v, axes, split_axis=0, concat_axis=0, tiled=True)  50.9 us
    ppermute x7, starting transfers between devices, per_device(): left = lambda v: lax.ppermute(v, 'exp', to_left)  29.7 us
    all_to_all x1, blocking collectives, exchange(): return lax.all_to_all(v, axes, split_axis=0, concat_axis=0, tiled=True)  21.3 us
    ppermute x7, waiting for transfers between devices, per_device(): right = lambda v: lax.ppermute(v, 'exp', to_right)  16.8 us
    ppermute x7, starting transfers between devices, per_device(): right = lambda v: lax.ppermute(v, 'exp', to_right)  15.7 us
    unnamed x60, local copies, waits for them, and re-layouts  14.4 us
  transfers between devices with their start and end apart: 19, of which 5 were waited for; matrix products, arithmetic and copies ran while one was open for 0% of the time, Pallas kernels for 1%

profile of v4, /device:TPU:1, one launch (start us, length us, event | category | flops | bytes accessed | tf_op | source)
XLA Modules:
  0.0 220.8 jit_solution(16922938197011673995)
XLA Ops:
  0.0 2.0 broadcast_in_dim.11
  2.0 13.7 %all-to-all-start = ((bf16[32,2,4096]{2,1,0:T(2,128)(2,1)}), bf16[32,2,4096]{2,1,0:T(2,128)(2,1)S(1)}, u32[]{:S(2)}, u32[]{:S(2)}) async-start(bf16[32,2,4096]{2,1,0:T(2,128)(2,1)} %broadcast_in_dim.11), calls=%async_computation | async-start | bytes 1048576 | tf_op jit(solution)/shard_map/all_to_all | solution.py:308
  16.4 13.6 %all-to-all-done = bf16[32,2,4096]{2,1,0:T(2,128)(2,1)S(1)} async-done(((bf16[32,2,4096]{2,1,0:T(2,128)(2,1)}), bf16[32,2,4096]{2,1,0:T(2,128)(2,1)S(1)}, u32[]{:S(2)}, u32[]{:S(2)}) %all-to-all-start) | async-done | bytes 524320 | tf_op jit(solution)/shard_map/all_to_all | solution.py:308
  30.2 3.8 %attention.1 = bf16[32,80,128]{2,1,0:T(8,128)(2,1)} custom-call(s32[2]{0:T(128)S(1)} %subtract_bitcast_fusion.limit_ref, bf16[64,4096]{1,0:T(8,128)(2,1)S(1)} %reshape.24.q_ref, bf16[2,512,256]{2,1,0:T(8,128)(2,1)S(1)} %bitcast.33, bf16[2,512,256]{2,1,0:T(8,128)(2,1)S(1)} %bitcast.34), custom_call_target="tpu_custom_call" | custom-call | flops 540000000 | bytes 2200000 | tf_op jit(solution)/shard_map/attention/pallas_call | solution.py:76
  34.0 7.6 %all-to-all-start.1 = ((bf16[32,80,128]{2,1,0:T(8,128)(2,1)}), bf16[32,80,128]{2,1,0:T(8,128)(2,1)S(1)}, u32[]{:S(2)}, u32[]{:S(2)}) async-start(bf16[32,80,128]{2,1,0:T(8,128)(2,1)} %attention.1), calls=%async_computation.1 | async-start | bytes 1310720 | tf_op jit(solution)/shard_map/all_to_all | solution.py:308
  41.8 16.3 %all-to-all-done.1.part_ref = bf16[32,80,128]{2,1,0:T(8,128)(2,1)S(1)} async-done(((bf16[32,80,128]{2,1,0:T(8,128)(2,1)}), bf16[32,80,128]{2,1,0:T(8,128)(2,1)S(1)}, u32[]{:S(2)}, u32[]{:S(2)}) %all-to-all-start.1) | async-done | bytes 655392 | tf_op jit(solution)/shard_map/all_to_all | solution.py:308
  60.2 12.9 %all-to-all-start.2 = ((bf16[64,24,128]{2,1,0:T(8,128)(2,1)}), bf16[64,24,128]{2,1,0:T(8,128)(2,1)S(1)}, u32[]{:S(2)}, u32[]{:S(2)}) async-start(bf16[64,24,128]{2,1,0:T(8,128)(2,1)} %bitcast.18), calls=%async_computation.2 | async-start | bytes 786432 | tf_op jit(solution)/shard_map/all_to_all | solution.py:308
  75.5 12.3 %all-to-all-done.2 = bf16[64,24,128]{2,1,0:T(8,128)(2,1)S(1)} async-done(((bf16[64,24,128]{2,1,0:T(8,128)(2,1)}), bf16[64,24,128]{2,1,0:T(8,128)(2,1)S(1)}, u32[]{:S(2)}, u32[]{:S(2)}) %all-to-all-start.2) | async-done | bytes 393248 | tf_op jit(solution)/shard_map/all_to_all | solution.py:308
  88.0 4.0 %all-to-all-start.3 = ((bf16[8,128,512]{2,1,0:T(8,128)(2,1)}), bf16[8,128,512]{2,1,0:T(8,128)(2,1)S(1)}, u32[]{:S(2)}, u32[]{:S(2)}) async-start(bf16[8,128,512]{2,1,0:T(8,128)(2,1)} %copy-done.2), calls=%async_computation.3 | async-start | bytes 2097152 | tf_op jit(solution)/shard_map/all_to_all | solution.py:308
  92.0 3.7 %collective-permute-start = (bf16[192,512]{1,0:T(8,128)(2,1)S(1)}, bf16[192,512]{1,0:T(8,128)(2,1)S(1)}, u32[]{:S(2)}, u32[]{:S(2)}) collective-permute-start(bf16[192,512]{1,0:T(8,128)(2,1)S(1)} %get-tuple-element.19.refs_0_), channel_id=1, source_target_pairs={{0,1},{1,2},{2,3},{3,4},{4,5},{5,6},{6,7},{7,0},{8,9},{9,10},{10,1... | collective-permute-start | bytes 589832 | tf_op jit(solution)/shard_map/ppermute | solution.py:349
  95.7 2.8 %collective-permute-start.3 = (bf16[192,512]{1,0:T(8,128)(2,1)S(1)}, bf16[192,512]{1,0:T(8,128)(2,1)S(1)}, u32[]{:S(2)}, u32[]{:S(2)}) collective-permute-start(bf16[192,512]{1,0:T(8,128)(2,1)S(1)} %get-tuple-element.20.refs_1_), channel_id=1, source_target_pairs={{0,7},{1,0},{2,1},{3,2},{4,3},{5,4},{6,5},{7,6},{8,15},{9,8},{10,9... | collective-permute-start | bytes 589832 | tf_op jit(solution)/shard_map/ppermute | solution.py:350
  98.5 2.5 %collective-permute-start.1 = (bf16[192,512]{1,0:T(8,128)(2,1)S(1)}, bf16[192,512]{1,0:T(8,128)(2,1)S(1)}, u32[]{:S(2)}, u32[]{:S(2)}) collective-permute-start(bf16[192,512]{1,0:T(8,128)(2,1)S(1)} %get-tuple-element.20.refs_1_), channel_id=1, source_target_pairs={{0,1},{1,2},{2,3},{3,4},{4,5},{5,6},{6,7},{7,0},{8,9},{9,10},{10,1... | collective-permute-start | bytes 589832 | tf_op jit(solution)/shard_map/ppermute | solution.py:349
  101.0 4.0 %collective-permute-start.2 = (bf16[192,512]{1,0:T(8,128)(2,1)S(1)}, bf16[192,512]{1,0:T(8,128)(2,1)S(1)}, u32[]{:S(2)}, u32[]{:S(2)}) collective-permute-start(bf16[192,512]{1,0:T(8,128)(2,1)S(1)} %get-tuple-element.19.refs_0_), channel_id=1, source_target_pairs={{0,7},{1,0},{2,1},{3,2},{4,3},{5,4},{6,5},{7,6},{8,15},{9,8},{10,9... | collective-permute-start | bytes 589832 | tf_op jit(solution)/shard_map/ppermute | solution.py:350
  105.0 16.8 %collective-permute-done.refs_2_ = bf16[192,512]{1,0:T(8,128)(2,1)S(1)} collective-permute-done((bf16[192,512]{1,0:T(8,128)(2,1)S(1)}, bf16[192,512]{1,0:T(8,128)(2,1)S(1)}, u32[]{:S(2)}, u32[]{:S(2)}) %collective-permute-start) | collective-permute-done | bytes 196640 | tf_op jit(solution)/shard_map/ppermute | solution.py:349
  124.4 4.6 %collective-permute-start.7 = (bf16[192,512]{1,0:T(8,128)(2,1)S(1)}, bf16[192,512]{1,0:T(8,128)(2,1)S(1)}, u32[]{:S(2)}, u32[]{:S(2)}) collective-permute-start(bf16[192,512]{1,0:T(8,128)(2,1)S(1)} %collective-permute-done.3.refs_5_), channel_id=1, source_target_pairs={{0,7},{1,0},{2,1},{3,2},{4,3},{5,4},{6,5},{7,6},{8,15},{9,8},{10,9... | collective-permute-start | bytes 589832 | tf_op jit(solution)/shard_map/ppermute | solution.py:350
  132.3 4.6 %collective-permute-start.6 = (bf16[192,512]{1,0:T(8,128)(2,1)S(1)}, bf16[192,512]{1,0:T(8,128)(2,1)}, u32[]{:S(2)}, u32[]{:S(2)}) collective-permute-start(bf16[192,512]{1,0:T(8,128)(2,1)S(1)} %collective-permute-done.2.refs_4_), channel_id=1, source_target_pairs={{0,7},{1,0},{2,1},{3,2},{4,3},{5,4},{6,5},{7,6},{8,15},{9,8},{10,9... | collective-permute-start | bytes 589832 | tf_op jit(solution)/shard_map/ppermute | solution.py:350
  140.1 4.6 %collective-permute-start.11 = (bf16[192,512]{1,0:T(8,128)(2,1)S(1)}, bf16[192,512]{1,0:T(8,128)(2,1)}, u32[]{:S(2)}, u32[]{:S(2)}) collective-permute-start(bf16[192,512]{1,0:T(8,128)(2,1)S(1)} %collective-permute-done.7.refs_9_), channel_id=1, source_target_pairs={{0,7},{1,0},{2,1},{3,2},{4,3},{5,4},{6,5},{7,6},{8,15},{9,8},{10,9... | collective-permute-start | bytes 589832 | tf_op jit(solution)/shard_map/ppermute | solution.py:350
  147.3 4.6 %collective-permute-start.10 = (bf16[192,512]{1,0:T(8,128)(2,1)}, bf16[192,512]{1,0:T(8,128)(2,1)}, u32[]{:S(2)}, u32[]{:S(2)}) collective-permute-start(bf16[192,512]{1,0:T(8,128)(2,1)} %collective-permute-done.6.refs_8_), channel_id=1, source_target_pairs={{0,7},{1,0},{2,1},{3,2},{4,3},{5,4},{6,5},{7,6},{8,15},{9,8},{10,9... | collective-permute-start | bytes 589832 | tf_op jit(solution)/shard_map/ppermute | solution.py:350
  152.6 1.9 collective-permute-start.12
  154.5 4.6 %collective-permute-start.13 = (bf16[192,512]{1,0:T(8,128)(2,1)}, bf16[192,512]{1,0:T(8,128)(2,1)}, u32[]{:S(2)}, u32[]{:S(2)}) collective-permute-start(bf16[192,512]{1,0:T(8,128)(2,1)} %collective-permute-done.11.refs_3_), channel_id=1, source_target_pairs={{0,7},{1,0},{2,1},{3,2},{4,3},{5,4},{6,5},{7,6},{8,15},{9,8},{10,9... | collective-permute-start | bytes 589832 | tf_op jit(solution)/shard_map/ppermute | solution.py:350
  167.8 2.0 gated.1
  169.8 21.3 %all_to_all.30.inner_ref = bf16[8,384,128]{2,1,0:T(8,128)(2,1)S(1)} all-to-all(bf16[8,384,128]{2,1,0:T(8,128)(2,1)S(1)} %gated.1), channel_id=1, replica_groups=mesh['ctx'=4,'att'=16,'exp'=8] {'exp'}, dimensions={0} | all-to-all | bytes 1572864 | tf_op jit(solution)/shard_map/all_to_all | solution.py:308
  192.5 12.6 %all-to-all-start.5 = ((bf16[64,24,128]{2,1,0:T(8,128)(2,1)}), bf16[64,24,128]{2,1,0:T(8,128)(2,1)S(1)}, u32[]{:S(2)}, u32[]{:S(2)}) async-start(bf16[64,24,128]{2,1,0:T(8,128)(2,1)} %bitcast.21), calls=%async_computation.5 | async-start | bytes 786432 | tf_op jit(solution)/shard_map/all_to_all | solution.py:308
  205.2 14.5 %all-to-all-done.5 = bf16[64,24,128]{2,1,0:T(8,128)(2,1)S(1)} async-done(((bf16[64,24,128]{2,1,0:T(8,128)(2,1)}), bf16[64,24,128]{2,1,0:T(8,128)(2,1)S(1)}, u32[]{:S(2)}, u32[]{:S(2)}) %all-to-all-start.5) | async-done | bytes 393248 | tf_op jit(solution)/shard_map/all_to_all | solution.py:308
  (90 shorter events, 29.1 us)
Async XLA Ops:
  2.0 28.0 %all-to-all-start = ((bf16[32,2,4096]{2,1,0:T(2,128)(2,1)}), bf16[32,2,4096]{2,1,0:T(2,128)(2,1)S(1)}, u32[]{:S(2)}, u32[]{:S(2)}) async-start(bf16[32,2,4096]{2,1,0:T(2,128)(2,1)} %broadcast_in_dim.11), calls=%async_computation | async-start | bytes 1048576 | tf_op jit(solution)/shard_map/all_to_all | solution.py:308
  34.0 24.1 %copy-start.21 = (bf16[1,16,4096]{2,1,0:T(8,128)(2,1)S(1)}, bf16[1,16,4096]{2,1,0:T(8,128)(2,1)}, u32[]{:S(2)}) copy-start(bf16[1,16,4096]{2,1,0:T(8,128)(2,1)} %param.15) | copy-start | bytes 393220
  34.0 24.1 %all-to-all-start.1 = ((bf16[32,80,128]{2,1,0:T(8,128)(2,1)}), bf16[32,80,128]{2,1,0:T(8,128)(2,1)S(1)}, u32[]{:S(2)}, u32[]{:S(2)}) async-start(bf16[32,80,128]{2,1,0:T(8,128)(2,1)} %attention.1), calls=%async_computation.1 | async-start | bytes 1310720 | tf_op jit(solution)/shard_map/all_to_all | solution.py:308
  41.8 17.9 %copy-start.22 = (s32[16,8]{1,0:T(8,128)}, s32[16,8]{1,0:T(8,128)S(1)}, u32[]{:S(2)}) copy-start(s32[16,8]{1,0:T(8,128)S(1)} %copy.12.ids_ref) | copy-start | bytes 1540
  60.2 27.5 %all-to-all-start.2 = ((bf16[64,24,128]{2,1,0:T(8,128)(2,1)}), bf16[64,24,128]{2,1,0:T(8,128)(2,1)S(1)}, u32[]{:S(2)}, u32[]{:S(2)}) async-start(bf16[64,24,128]{2,1,0:T(8,128)(2,1)} %bitcast.18), calls=%async_computation.2 | async-start | bytes 786432 | tf_op jit(solution)/shard_map/all_to_all | solution.py:308
  88.0 71.8 %copy-start = (bf16[1,4096,128]{2,1,0:T(8,128)(2,1)S(1)}, bf16[1,4096,128]{2,1,0:T(8,128)(2,1)}, u32[]{:S(2)}) copy-start(bf16[1,4096,128]{2,1,0:T(8,128)(2,1)} %param.19) | copy-start | bytes 3145732
  88.0 71.8 %copy-start.1 = (bf16[1,4096,128]{2,1,0:T(8,128)(2,1)S(1)}, bf16[1,4096,128]{2,1,0:T(8,128)(2,1)}, u32[]{:S(2)}) copy-start(bf16[1,4096,128]{2,1,0:T(8,128)(2,1)} %param.20) | copy-start | bytes 3145732
  88.0 64.6 %all-to-all-start.3 = ((bf16[8,128,512]{2,1,0:T(8,128)(2,1)}), bf16[8,128,512]{2,1,0:T(8,128)(2,1)S(1)}, u32[]{:S(2)}, u32[]{:S(2)}) async-start(bf16[8,128,512]{2,1,0:T(8,128)(2,1)} %copy-done.2), calls=%async_computation.3 | async-start | bytes 2097152 | tf_op jit(solution)/shard_map/all_to_all | solution.py:308
  92.0 29.8 %collective-permute-start = (bf16[192,512]{1,0:T(8,128)(2,1)S(1)}, bf16[192,512]{1,0:T(8,128)(2,1)S(1)}, u32[]{:S(2)}, u32[]{:S(2)}) collective-permute-start(bf16[192,512]{1,0:T(8,128)(2,1)S(1)} %get-tuple-element.19.refs_0_), channel_id=1, source_target_pairs={{0,1},{1,2},{2,3},{3,4},{4,5},{5,6},{6,7},{7,0},{8,9},{9,10},{10,1... | collective-permute-start | bytes 589832 | tf_op jit(solution)/shard_map/ppermute | solution.py:349
  95.7 28.7 %collective-permute-start.3 = (bf16[192,512]{1,0:T(8,128)(2,1)S(1)}, bf16[192,512]{1,0:T(8,128)(2,1)S(1)}, u32[]{:S(2)}, u32[]{:S(2)}) collective-permute-start(bf16[192,512]{1,0:T(8,128)(2,1)S(1)} %get-tuple-element.20.refs_1_), channel_id=1, source_target_pairs={{0,7},{1,0},{2,1},{3,2},{4,3},{5,4},{6,5},{7,6},{8,15},{9,8},{10,9... | collective-permute-start | bytes 589832 | tf_op jit(solution)/shard_map/ppermute | solution.py:350
  98.5 31.2 %collective-permute-start.1 = (bf16[192,512]{1,0:T(8,128)(2,1)S(1)}, bf16[192,512]{1,0:T(8,128)(2,1)S(1)}, u32[]{:S(2)}, u32[]{:S(2)}) collective-permute-start(bf16[192,512]{1,0:T(8,128)(2,1)S(1)} %get-tuple-element.20.refs_1_), channel_id=1, source_target_pairs={{0,1},{1,2},{2,3},{3,4},{4,5},{5,6},{6,7},{7,0},{8,9},{9,10},{10,1... | collective-permute-start | bytes 589832 | tf_op jit(solution)/shard_map/ppermute | solution.py:349
  101.0 31.3 %collective-permute-start.2 = (bf16[192,512]{1,0:T(8,128)(2,1)S(1)}, bf16[192,512]{1,0:T(8,128)(2,1)S(1)}, u32[]{:S(2)}, u32[]{:S(2)}) collective-permute-start(bf16[192,512]{1,0:T(8,128)(2,1)S(1)} %get-tuple-element.19.refs_0_), channel_id=1, source_target_pairs={{0,7},{1,0},{2,1},{3,2},{4,3},{5,4},{6,5},{7,6},{8,15},{9,8},{10,9... | collective-permute-start | bytes 589832 | tf_op jit(solution)/shard_map/ppermute | solution.py:350
  121.8 15.7 %collective-permute-start.4 = (bf16[192,512]{1,0:T(8,128)(2,1)S(1)}, bf16[192,512]{1,0:T(8,128)(2,1)S(1)}, u32[]{:S(2)}, u32[]{:S(2)}) collective-permute-start(bf16[192,512]{1,0:T(8,128)(2,1)S(1)} %collective-permute-done.refs_2_), channel_id=1, source_target_pairs={{0,1},{1,2},{2,3},{3,4},{4,5},{5,6},{6,7},{7,0},{8,9},{9,10},{10,1... | collective-permute-start | bytes 589832 | tf_op jit(solution)/shard_map/ppermute | solution.py:349
  124.4 15.7 %collective-permute-start.7 = (bf16[192,512]{1,0:T(8,128)(2,1)S(1)}, bf16[192,512]{1,0:T(8,128)(2,1)S(1)}, u32[]{:S(2)}, u32[]{:S(2)}) collective-permute-start(bf16[192,512]{1,0:T(8,128)(2,1)S(1)} %collective-permute-done.3.refs_5_), channel_id=1, source_target_pairs={{0,7},{1,0},{2,1},{3,2},{4,3},{5,4},{6,5},{7,6},{8,15},{9,8},{10,9... | collective-permute-start | bytes 589832 | tf_op jit(solution)/shard_map/ppermute | solution.py:350
  129.7 15.7 %collective-permute-start.5 = (bf16[192,512]{1,0:T(8,128)(2,1)S(1)}, bf16[192,512]{1,0:T(8,128)(2,1)}, u32[]{:S(2)}, u32[]{:S(2)}) collective-permute-start(bf16[192,512]{1,0:T(8,128)(2,1)S(1)} %collective-permute-done.1.refs_3_), channel_id=1, source_target_pairs={{0,1},{1,2},{2,3},{3,4},{4,5},{5,6},{6,7},{7,0},{8,9},{9,10},{10,1... | collective-permute-start | bytes 589832 | tf_op jit(solution)/shard_map/ppermute | solution.py:349
  132.3 15.0 %collective-permute-start.6 = (bf16[192,512]{1,0:T(8,128)(2,1)S(1)}, bf16[192,512]{1,0:T(8,128)(2,1)}, u32[]{:S(2)}, u32[]{:S(2)}) collective-permute-start(bf16[192,512]{1,0:T(8,128)(2,1)S(1)} %collective-permute-done.2.refs_4_), channel_id=1, source_target_pairs={{0,7},{1,0},{2,1},{3,2},{4,3},{5,4},{6,5},{7,6},{8,15},{9,8},{10,9... | collective-permute-start | bytes 589832 | tf_op jit(solution)/shard_map/ppermute | solution.py:350
  137.5 14.4 %collective-permute-start.8 = (bf16[192,512]{1,0:T(8,128)(2,1)S(1)}, bf16[192,512]{1,0:T(8,128)(2,1)S(1)}, u32[]{:S(2)}, u32[]{:S(2)}) collective-permute-start(bf16[192,512]{1,0:T(8,128)(2,1)S(1)} %collective-permute-done.4.refs_6_), channel_id=1, source_target_pairs={{0,1},{1,2},{2,3},{3,4},{4,5},{5,6},{6,7},{7,0},{8,9},{9,10},{10,1... | collective-permute-start | bytes 589832 | tf_op jit(solution)/shard_map/ppermute | solution.py:349
  140.1 12.4 %collective-permute-start.11 = (bf16[192,512]{1,0:T(8,128)(2,1)S(1)}, bf16[192,512]{1,0:T(8,128)(2,1)}, u32[]{:S(2)}, u32[]{:S(2)}) collective-permute-start(bf16[192,512]{1,0:T(8,128)(2,1)S(1)} %collective-permute-done.7.refs_9_), channel_id=1, source_target_pairs={{0,7},{1,0},{2,1},{3,2},{4,3},{5,4},{6,5},{7,6},{8,15},{9,8},{10,9... | collective-permute-start | bytes 589832 | tf_op jit(solution)/shard_map/ppermute | solution.py:350
  145.4 22.4 %collective-permute-start.9 = (bf16[192,512]{1,0:T(8,128)(2,1)}, bf16[192,512]{1,0:T(8,128)(2,1)}, u32[]{:S(2)}, u32[]{:S(2)}) collective-permute-start(bf16[192,512]{1,0:T(8,128)(2,1)} %collective-permute-done.5.refs_7_), channel_id=1, source_target_pairs={{0,1},{1,2},{2,3},{3,4},{4,5},{5,6},{6,7},{7,0},{8,9},{9,10},{10,1... | collective-permute-start | bytes 589832 | tf_op jit(solution)/shard_map/ppermute | solution.py:349
  147.3 20.4 %collective-permute-start.10 = (bf16[192,512]{1,0:T(8,128)(2,1)}, bf16[192,512]{1,0:T(8,128)(2,1)}, u32[]{:S(2)}, u32[]{:S(2)}) collective-permute-start(bf16[192,512]{1,0:T(8,128)(2,1)} %collective-permute-done.6.refs_8_), channel_id=1, source_target_pairs={{0,7},{1,0},{2,1},{3,2},{4,3},{5,4},{6,5},{7,6},{8,15},{9,8},{10,9... | collective-permute-start | bytes 589832 | tf_op jit(solution)/shard_map/ppermute | solution.py:350
  152.6 15.2 %collective-permute-start.12 = (bf16[192,512]{1,0:T(8,128)(2,1)}, bf16[192,512]{1,0:T(8,128)(2,1)}, u32[]{:S(2)}, u32[]{:S(2)}) collective-permute-start(bf16[192,512]{1,0:T(8,128)(2,1)} %copy-done.18), channel_id=1, source_target_pairs={{0,1},{1,2},{2,3},{3,4},{4,5},{5,6},{6,7},{7,0},{8,9},{9,10},{10,1... | collective-permute-start | bytes 589832 | tf_op jit(solution)/shard_map/ppermute | solution.py:349
  154.5 13.3 %collective-permute-start.13 = (bf16[192,512]{1,0:T(8,128)(2,1)}, bf16[192,512]{1,0:T(8,128)(2,1)}, u32[]{:S(2)}, u32[]{:S(2)}) collective-permute-start(bf16[192,512]{1,0:T(8,128)(2,1)} %collective-permute-done.11.refs_3_), channel_id=1, source_target_pairs={{0,7},{1,0},{2,1},{3,2},{4,3},{5,4},{6,5},{7,6},{8,15},{9,8},{10,9... | collective-permute-start | bytes 589832 | tf_op jit(solution)/shard_map/ppermute | solution.py:350
  192.5 27.2 %copy-start.25 = (f32[16,512]{1,0:T(8,128)S(1)}, f32[16,512]{1,0:T(8,128)}, u32[]{:S(2)}) copy-start(f32[16,512]{1,0:T(8,128)} %copy-done.24) | copy-start | bytes 98308
  192.5 27.2 %all-to-all-start.5 = ((bf16[64,24,128]{2,1,0:T(8,128)(2,1)}), bf16[64,24,128]{2,1,0:T(8,128)(2,1)S(1)}, u32[]{:S(2)}, u32[]{:S(2)}) async-start(bf16[64,24,128]{2,1,0:T(8,128)(2,1)} %bitcast.21), calls=%async_computation.5 | async-start | bytes 786432 | tf_op jit(solution)/shard_map/all_to_all | solution.py:308
  (25 other events, 95.3 us)

commit v5 on v4

--- a/solution.py
+++ b/solution.py
@@ -148,23 +148,6 @@
     )(z, part, res, gain, ids)
 
 
-def pack_kernel(down_ref, out_ref):
-    for d in range(8):
-        out_ref[d] = down_ref[:, d * 512 : (d + 1) * 512]
-
-
-def pack(down):
-    return pl.pallas_call(
-        pack_kernel,
-        out_shape=jax.ShapeDtypeStruct((8, 128, 512), BF16),
-        in_specs=[VMEM_SPEC],
-        out_specs=VMEM_SPEC,
-        compiler_params=params(),
-        cost_estimate=cost(0, 2_100_000),
-        name="pack",
-    )(down)
-
-
 def compact_kernel(arrived_ref, a_ref, b_ref, wide):
     wide[...] = arrived_ref[...].astype(F32)
     for s in range(CAP):
@@ -206,6 +189,34 @@
     return sums, squares
 
 
+def whole(*shape):
+    return pl.BlockSpec(shape, lambda g, index: (0,) * len(shape))
+
+
+def columns(i):
+    return pl.BlockSpec((128, 512), lambda g, index: (0, index[i]))
+
+
+HALF = jax.ShapeDtypeStruct((192, 512), BF16)
+
+
+def ring_call(kernel, name, flops, out_shape, in_specs, out_specs, scratch=()):
+    return pl.pallas_call(
+        kernel,
+        out_shape=out_shape,
+        grid_spec=pltpu.PrefetchScalarGridSpec(
+            num_scalar_prefetch=1,
+            grid=(1,),
+            in_specs=in_specs,
+            out_specs=out_specs,
+            scratch_shapes=scratch,
+        ),
+        compiler_params=params(),
+        cost_estimate=cost(flops, 2_000_000),
+        name=name,
+    )
+
+
 def early_kernel(index_ref, gate_ref, up_ref, gain_ref, *refs):
     sums, squares = chunk_sums(index_ref, refs[:-1], gate_ref, up_ref, gain_ref)
     for half in range(2):
@@ -214,68 +225,81 @@
 
 
 def early_sums(indices, gate, up, gain, halves):
-    return pl.pallas_call(
+    return ring_call(
         early_kernel,
-        out_shape=jax.ShapeDtypeStruct((384, 384), F32),
-        in_specs=[SMEM_SPEC] + [VMEM_SPEC] * (3 + len(halves)),
-        out_specs=VMEM_SPEC,
-        compiler_params=params(),
-        cost_estimate=cost(50_000_000 * len(halves), 4_000_000),
-        name="early_sums",
+        "early_sums",
+        50_000_000 * len(halves),
+        jax.ShapeDtypeStruct((384, 384), F32),
+        [whole(D, 128), whole(D, 128), whole(1, D)] + [whole(192, 512)] * len(halves),
+        whole(384, 384),
     )(jnp.stack(indices), gate, up, gain, *halves)
 
 
-def gated_kernel(index_ref, early_ref, gate_ref, up_ref, gain_ref, *refs):
-    out_ref = refs[-1]
-    sums, squares = chunk_sums(index_ref, refs[:-1], gate_ref, up_ref, gain_ref)
-    for half in range(2):
+def gated_kernel(index_ref, early_ref, gate_ref, up_ref, gain_ref, down_ref, *refs):
+    halves, (inner_ref, a_ref, b_ref) = refs[:-3], refs[-3:]
+    sums, squares = chunk_sums(index_ref, halves, gate_ref, up_ref, gain_ref)
+    for half, out_ref in enumerate((a_ref, b_ref)):
         rows = slice(half * 192, (half + 1) * 192)
         square = early_ref[rows, 256:384] + squares[half]
         scale = lax.rsqrt(jnp.sum(square, axis=1, keepdims=True) * (1.0 / D) + 1e-6)
         gate = (early_ref[rows, 0:128] + sums[half][:, 0:128]) * scale
         up = (early_ref[rows, 128:256] + sums[half][:, 128:256]) * scale
         inner = (gate / (1.0 + jnp.exp(-gate)) * up).astype(BF16)
-        for d in range(8):
-            out_ref[d, rows, :] = inner
-
-
-def gated(indices, early, gate, up, gain, halves):
-    return pl.pallas_call(
+        inner_ref[rows, :] = inner
+        out_ref[...] = jnp.dot(inner, down_ref[...], preferred_element_type=F32).astype(BF16)
+
+
+def gated(indices, target, early, gate, up, gain, down, halves):
+    return ring_call(
         gated_kernel,
-        out_shape=jax.ShapeDtypeStruct((8, 384, 128), BF16),
-        in_specs=[SMEM_SPEC] + [VMEM_SPEC] * (4 + len(halves)),
-        out_specs=VMEM_SPEC,
-        compiler_params=params(),
-        cost_estimate=cost(50_000_000 * len(halves), 4_000_000, 50_000),
-        name="gated",
-    )(jnp.stack(indices), early, gate, up, gain, *halves)
-
-
-def down_kernel(inner_ref, weight_ref, out_ref, wide):
-    total = None
-    for s in range(0, 8, 2):
-        inner = jnp.concatenate([inner_ref[s], inner_ref[s + 1]], axis=1)
-        weight = jnp.concatenate([weight_ref[s], weight_ref[s + 1]], axis=0)
-        dot = jnp.dot(inner, weight, preferred_element_type=F32)
-        total = dot if total is None else total + dot
+        "gated",
+        50_000_000 * len(halves),
+        (jax.ShapeDtypeStruct((384, 128), BF16), HALF, HALF),
+        [whole(384, 384), whole(D, 128), whole(D, 128), whole(1, D), columns(len(indices))]
+        + [whole(192, 512)] * len(halves),
+        (whole(384, 128), whole(192, 512), whole(192, 512)),
+    )(jnp.stack(indices + [target]), early, gate, up, gain, down, *halves)
+
+
+def down_kernel(index_ref, inner_ref, down_ref, sum_ref, out_ref):
+    out_ref[...] = (
+        sum_ref[...].astype(F32)
+        + jnp.dot(inner_ref[...], down_ref[...], preferred_element_type=F32)
+    ).astype(BF16)
+
+
+def down_step(target, half, inner, down, summed):
+    rows = pl.BlockSpec((192, 128), lambda g, index: (half, 0))
+    return ring_call(
+        down_kernel,
+        "down",
+        25_000_000,
+        HALF,
+        [rows, columns(0), whole(192, 512)],
+        whole(192, 512),
+    )(target.reshape(1), inner, down, summed)
+
+
+def last_kernel(index_ref, inner_ref, down_ref, a_ref, b_ref, out_ref, wide):
+    own = jnp.dot(inner_ref[...], down_ref[...], preferred_element_type=F32)
+    halves = own[0:192] + a_ref[...].astype(F32), own[192:384] + b_ref[...].astype(F32)
     for s in range(CAP):
+        block = halves[s // 3][(s % 3) * 64 : (s % 3 + 1) * 64]
         for c in range(4):
-            block = total[s * 64 : (s + 1) * 64, c * 128 : (c + 1) * 128]
-            wide[pl.ds(c * CAP + s, 64, stride=4 * CAP), :] = block
+            wide[pl.ds(c * CAP + s, 64, stride=4 * CAP), :] = block[:, c * 128 : (c + 1) * 128]
     out_ref[...] = wide[...].astype(BF16)
 
 
-def down_columns(inner, weight):
-    return pl.pallas_call(
-        down_kernel,
-        out_shape=jax.ShapeDtypeStruct((1536, 128), BF16),
-        in_specs=[VMEM_SPEC] * 2,
-        out_specs=VMEM_SPEC,
-        scratch_shapes=[pltpu.VMEM((1536, 128), F32)],
-        compiler_params=params(),
-        cost_estimate=cost(400_000_000, 2_500_000),
-        name="down",
-    )(inner, weight)
+def last_step(target, inner, down, a, b):
+    return ring_call(
+        last_kernel,
+        "last",
+        50_000_000,
+        jax.ShapeDtypeStruct((1536, 128), BF16),
+        [whole(384, 128), columns(0), whole(192, 512), whole(192, 512)],
+        whole(1536, 128),
+        [pltpu.VMEM((1536, 128), F32)],
+    )(target.reshape(1), inner, down, a, b)
 
 
 def mix_kernel(hidden_ref, back_ref, ids_ref, gates_ref, out_ref):
@@ -342,27 +366,30 @@
     hidden, outbound = combine(z.reshape(1), part, residual[0], gain, ids)
     own_a, own_b = compact(plane_exchange(outbound))
 
-    own_a, own_b, packed = lax.optimization_barrier((own_a, own_b, pack(down)))
-    by_column = exchange(packed, "exp")
-    to_right = [(i, (i + 1) % ring) for i in range(ring)]
-    to_left = [(i, (i - 1) % ring) for i in range(ring)]
-    right = lambda v: lax.ppermute(v, "exp", to_right)
-    left = lambda v: lax.ppermute(v, "exp", to_left)
-    at = lambda k: lax.rem(z + (k + ring), ring).astype(jnp.int32)
-    halves, indices = [own_a, own_b], [at(0)]
-    ra, rb, la, lb = own_a, own_b, own_a, own_b
-    for k in range(1, 4):
-        ra, lb = right(ra), left(lb)
-        rb, la = right(rb), left(la)
-        halves += [ra, rb, la, lb]
-        indices += [at(-k), at(k)]
-    ra, lb, by_column = lax.optimization_barrier((ra, lb, by_column))
-    halves += [right(ra), left(lb)]
-    indices.append(at(4))
-
-    early = early_sums(indices[:5], gate, up, gain, halves[:10])
-    units = exchange(gated(indices[5:], early, gate, up, gain, halves[10:]), "exp")
-    back = down_columns(units, by_column)
+    groups = lax.axis_size("att")
+    way = 1 - 2 * (lax.axis_index("att") & 1)
+    turn = [
+        (g * ring + i, g * ring + (i + 1 - 2 * (g % 2)) % ring)
+        for g in range(groups)
+        for i in range(ring)
+    ]
+    onward = lambda v: lax.ppermute(v, ("att", "exp"), turn)
+    behind = lambda k: ((z - way * k) & (ring - 1)).astype(jnp.int32)
+
+    halves, indices = [own_a, own_b], [behind(0)]
+    a, b = own_a, own_b
+    for k in range(1, ring):
+        a, b = onward(a), onward(b)
+        halves += [a, b]
+        indices.append(behind(k))
+    early = early_sums(indices[:6], gate, up, gain, halves[:12])
+
+    inner, a, b = gated(indices[6:], behind(1), early, gate, up, gain, down, halves[12:])
+    for k in range(2, ring):
+        a, b = onward(a), onward(b)
+        a = down_step(behind(k), 0, inner, down, a)
+        b = down_step(behind(k), 1, inner, down, b)
+    back = last_step(z.astype(jnp.int32), inner, down, onward(a), onward(b))
     return mix(hidden, plane_exchange(back), ids, gates)[None]
 
 

time: 222 us -> 246 us (1.11)
  starting transfers between devices: 96.3 us -> 133 us
  waiting for transfers between devices: 73.6 us -> 54.1 us
  blocking collectives: 21.3 us -> 27.3 us
    ppermute x14 -> x28, starting transfers between devices: 45.4 us -> 90 us  [per_device(): onward = lambda v: lax.ppermute(v, ('att', 'exp'), turn)]
    all_to_all x5 -> x3, waiting for transfers between devices: 56.8 us -> 44.5 us  [exchange(): return lax.all_to_all(v, axes, split_axis=0, concat_axis=0, tiled=True)]
    all_to_all x5 -> x3, starting transfers between devices: 50.9 us -> 42.8 us  [exchange(): return lax.all_to_all(v, axes, split_axis=0, concat_axis=0, tiled=True)]
    ppermute x14 -> x28, waiting for transfers between devices: 16.8 us -> 9.61 us  [per_device(): onward = lambda v: lax.ppermute(v, ('att', 'exp'), turn)]
    all_to_all x1, blocking collectives: 21.3 us -> 27.3 us  [exchange(): return lax.all_to_all(v, axes, split_axis=0, concat_axis=0, tiled=True)]
    pallas_call x4 -> x15, Pallas kernels: 5.27 us -> 6.05 us  [the longest x12 2.36 us: down_step(): ring_call(down_kernel, 'down', 25000000, HALF, [rows, columns(0), whole(1...]
    unnamed x60 -> x56, local copies, waits for them, and re-layouts: 14.4 us -> 15.1 us
  transfers between devices with their start and end apart: 19 -> 31, of which waited for: 5 -> 12; matrix products, arithmetic and copies ran while one was open for 0% -> 0% of each run, Pallas kernels for 1% -> 2%
where the time goes in v5:
time: 246 us; the launch traced here: 244 us
  starting transfers between devices  133 us (54%)
  waiting for transfers between devices  54.1 us (22%)
  blocking collectives  27.3 us (11%)
  local copies, waits for them, and re-layouts  17.6 us (7%)
  Pallas kernels  11.8 us (5%)
    ppermute x28, starting transfers between devices, per_device(): onward = lambda v: lax.ppermute(v, ('att', 'exp'), turn)  90 us
    all_to_all x3, waiting for transfers between devices, exchange(): return lax.all_to_all(v, axes, split_axis=0, concat_axis=0, tiled=True)  44.5 us
    all_to_all x3, starting transfers between devices, exchange(): return lax.all_to_all(v, axes, split_axis=0, concat_axis=0, tiled=True)  42.8 us
    all_to_all x1, blocking collectives, exchange(): return lax.all_to_all(v, axes, split_axis=0, concat_axis=0, tiled=True)  27.3 us
    unnamed x56, local copies, waits for them, and re-layouts  15.1 us
    ppermute x28, waiting for transfers between devices, per_device(): onward = lambda v: lax.ppermute(v, ('att', 'exp'), turn)  9.61 us
  transfers between devices with their start and end apart: 31, of which 12 were waited for; matrix products, arithmetic and copies ran while one was open for 0% of the time, Pallas kernels for 2%

profile of v5, /device:TPU:1, one launch (start us, length us, event | category | flops | bytes accessed | tf_op | source)
XLA Modules:
  0.0 244.3 jit_solution(3714286925092271677)
XLA Ops:
  2.0 13.7 %all-to-all-start = ((bf16[32,2,4096]{2,1,0:T(2,128)(2,1)}), bf16[32,2,4096]{2,1,0:T(2,128)(2,1)S(1)}, u32[]{:S(2)}, u32[]{:S(2)}) async-start(bf16[32,2,4096]{2,1,0:T(2,128)(2,1)} %broadcast_in_dim.11), calls=%async_computation | async-start | bytes 1048576 | tf_op jit(solution)/shard_map/all_to_all | solution.py:332
  16.4 13.6 %all-to-all-done = bf16[32,2,4096]{2,1,0:T(2,128)(2,1)S(1)} async-done(((bf16[32,2,4096]{2,1,0:T(2,128)(2,1)}), bf16[32,2,4096]{2,1,0:T(2,128)(2,1)S(1)}, u32[]{:S(2)}, u32[]{:S(2)}) %all-to-all-start) | async-done | bytes 524320 | tf_op jit(solution)/shard_map/all_to_all | solution.py:332
  30.3 3.8 %attention.1 = bf16[32,80,128]{2,1,0:T(8,128)(2,1)} custom-call(s32[2]{0:T(128)S(1)} %subtract_bitcast_fusion.limit_ref, bf16[64,4096]{1,0:T(8,128)(2,1)S(1)} %reshape.17.q_ref, bf16[2,512,256]{2,1,0:T(8,128)(2,1)S(1)} %bitcast.46, bf16[2,512,256]{2,1,0:T(8,128)(2,1)S(1)} %bitcast.47), custom_call_target="tpu_custom_call" | custom-call | flops 540000000 | bytes 2200000 | tf_op jit(solution)/shard_map/attention/pallas_call | solution.py:76
  34.1 7.6 %all-to-all-start.1 = ((bf16[32,80,128]{2,1,0:T(8,128)(2,1)}), bf16[32,80,128]{2,1,0:T(8,128)(2,1)S(1)}, u32[]{:S(2)}, u32[]{:S(2)}) async-start(bf16[32,80,128]{2,1,0:T(8,128)(2,1)} %attention.1), calls=%async_computation.1 | async-start | bytes 1310720 | tf_op jit(solution)/shard_map/all_to_all | solution.py:332
  41.8 16.3 %all-to-all-done.1.part_ref = bf16[32,80,128]{2,1,0:T(8,128)(2,1)S(1)} async-done(((bf16[32,80,128]{2,1,0:T(8,128)(2,1)}), bf16[32,80,128]{2,1,0:T(8,128)(2,1)S(1)}, u32[]{:S(2)}, u32[]{:S(2)}) %all-to-all-start.1) | async-done | bytes 655392 | tf_op jit(solution)/shard_map/all_to_all | solution.py:332
  58.9 27.3 %all_to_all.20 = bf16[64,24,128]{2,1,0:T(8,128)(2,1)S(1)} all-to-all(bf16[64,24,128]{2,1,0:T(8,128)(2,1)S(1)} %bitcast.48), channel_id=1, replica_groups=mesh['ctx'=4,'att'=16,'exp'=8] {'ctx','att'}, dimensions={0} | all-to-all | bytes 786432 | tf_op jit(solution)/shard_map/all_to_all | solution.py:332
  86.4 3.6 %collective-permute-start = (bf16[192,512]{1,0:T(8,128)(2,1)S(1)}, bf16[192,512]{1,0:T(8,128)(2,1)S(1)}, u32[]{:S(2)}, u32[]{:S(2)}) collective-permute-start(bf16[192,512]{1,0:T(8,128)(2,1)S(1)} %get-tuple-element.14.refs_0_), channel_id=1, source_target_pairs={{0,1},{1,2},{2,3},{3,4},{4,5},{5,6},{6,7},{7,0},{8,15},{9,8},{10,9... | collective-permute-start | bytes 589832 | tf_op jit(solution)/shard_map/ppermute | solution.py:376
  93.8 3.8 %collective-permute-start.2 = (bf16[192,512]{1,0:T(8,128)(2,1)S(1)}, bf16[192,512]{1,0:T(8,128)(2,1)S(1)}, u32[]{:S(2)}, u32[]{:S(2)}) collective-permute-start(bf16[192,512]{1,0:T(8,128)(2,1)S(1)} %collective-permute-done.refs_2_), channel_id=1, source_target_pairs={{0,1},{1,2},{2,3},{3,4},{4,5},{5,6},{6,7},{7,0},{8,15},{9,8},{10,9... | collective-permute-start | bytes 589832 | tf_op jit(solution)/shard_map/ppermute | solution.py:376
  100.8 4.5 %collective-permute-start.4 = (bf16[192,512]{1,0:T(8,128)(2,1)S(1)}, bf16[192,512]{1,0:T(8,128)(2,1)S(1)}, u32[]{:S(2)}, u32[]{:S(2)}) collective-permute-start(bf16[192,512]{1,0:T(8,128)(2,1)S(1)} %collective-permute-done.2.refs_4_), channel_id=1, source_target_pairs={{0,1},{1,2},{2,3},{3,4},{4,5},{5,6},{6,7},{7,0},{8,15},{9,8},{10,9... | collective-permute-start | bytes 589832 | tf_op jit(solution)/shard_map/ppermute | solution.py:376
  108.5 4.3 %collective-permute-start.6 = (bf16[192,512]{1,0:T(8,128)(2,1)S(1)}, bf16[192,512]{1,0:T(8,128)(2,1)S(1)}, u32[]{:S(2)}, u32[]{:S(2)}) collective-permute-start(bf16[192,512]{1,0:T(8,128)(2,1)S(1)} %collective-permute-done.4.refs_6_), channel_id=1, source_target_pairs={{0,1},{1,2},{2,3},{3,4},{4,5},{5,6},{6,7},{7,0},{8,15},{9,8},{10,9... | collective-permute-start | bytes 589832 | tf_op jit(solution)/shard_map/ppermute | solution.py:376
  116.2 4.3 %collective-permute-start.8 = (bf16[192,512]{1,0:T(8,128)(2,1)S(1)}, bf16[192,512]{1,0:T(8,128)(2,1)S(1)}, u32[]{:S(2)}, u32[]{:S(2)}) collective-permute-start(bf16[192,512]{1,0:T(8,128)(2,1)S(1)} %collective-permute-done.6.refs_8_), channel_id=1, source_target_pairs={{0,1},{1,2},{2,3},{3,4},{4,5},{5,6},{6,7},{7,0},{8,15},{9,8},{10,9... | collective-permute-start | bytes 589832 | tf_op jit(solution)/shard_map/ppermute | solution.py:376
  123.8 4.3 %collective-permute-start.10 = (bf16[192,512]{1,0:T(8,128)(2,1)S(1)}, bf16[192,512]{1,0:T(8,128)(2,1)S(1)}, u32[]{:S(2)}, u32[]{:S(2)}) collective-permute-start(bf16[192,512]{1,0:T(8,128)(2,1)S(1)} %collective-permute-done.8.refs_10_), channel_id=1, source_target_pairs={{0,1},{1,2},{2,3},{3,4},{4,5},{5,6},{6,7},{7,0},{8,15},{9,8},{10,9... | collective-permute-start | bytes 589832 | tf_op jit(solution)/shard_map/ppermute | solution.py:376
  131.4 4.3 %collective-permute-start.12 = (bf16[192,512]{1,0:T(8,128)(2,1)S(1)}, bf16[192,512]{1,0:T(8,128)(2,1)S(1)}, u32[]{:S(2)}, u32[]{:S(2)}) collective-permute-start(bf16[192,512]{1,0:T(8,128)(2,1)S(1)} %collective-permute-done.10.refs_0_), channel_id=1, source_target_pairs={{0,1},{1,2},{2,3},{3,4},{4,5},{5,6},{6,7},{7,0},{8,15},{9,8},{10,9... | collective-permute-start | bytes 589832 | tf_op jit(solution)/shard_map/ppermute | solution.py:376
  135.7 2.6 %collective-permute-start.13 = (bf16[192,512]{1,0:T(8,128)(2,1)S(1)}, bf16[192,512]{1,0:T(8,128)(2,1)S(1)}, u32[]{:S(2)}, u32[]{:S(2)}) collective-permute-start(bf16[192,512]{1,0:T(8,128)(2,1)S(1)} %collective-permute-done.11.refs_1_), channel_id=1, source_target_pairs={{0,1},{1,2},{2,3},{3,4},{4,5},{5,6},{6,7},{7,0},{8,15},{9,8},{10,9... | collective-permute-start | bytes 589832 | tf_op jit(solution)/shard_map/ppermute | solution.py:376
  149.5 2.9 %collective-permute-start.21 = (bf16[192,512]{1,0:T(8,128)(2,1)S(1)}, bf16[192,512]{1,0:T(8,128)(2,1)S(1)}, u32[]{:S(2)}, u32[]{:S(2)}) collective-permute-start(bf16[192,512]{1,0:T(8,128)(2,1)S(1)} %get-tuple-element.18), channel_id=1, source_target_pairs={{0,1},{1,2},{2,3},{3,4},{4,5},{5,6},{6,7},{7,0},{8,15},{9,8},{10,9... | collective-permute-start | bytes 589832 | tf_op jit(solution)/shard_map/ppermute | solution.py:376
  156.1 4.1 %collective-permute-start.22 = (bf16[192,512]{1,0:T(8,128)(2,1)S(1)}, bf16[192,512]{1,0:T(8,128)(2,1)S(1)}, u32[]{:S(2)}, u32[]{:S(2)}) collective-permute-start(bf16[192,512]{1,0:T(8,128)(2,1)S(1)} %down.18), channel_id=1, source_target_pairs={{0,1},{1,2},{2,3},{3,4},{4,5},{5,6},{6,7},{7,0},{8,15},{9,8},{10,9... | collective-permute-start | bytes 589832 | tf_op jit(solution)/shard_map/ppermute | solution.py:376
  163.1 5.0 %collective-permute-start.23 = (bf16[192,512]{1,0:T(8,128)(2,1)S(1)}, bf16[192,512]{1,0:T(8,128)(2,1)S(1)}, u32[]{:S(2)}, u32[]{:S(2)}) collective-permute-start(bf16[192,512]{1,0:T(8,128)(2,1)S(1)} %down.19), channel_id=1, source_target_pairs={{0,1},{1,2},{2,3},{3,4},{4,5},{5,6},{6,7},{7,0},{8,15},{9,8},{10,9... | collective-permute-start | bytes 589832 | tf_op jit(solution)/shard_map/ppermute | solution.py:376
  170.9 5.0 %collective-permute-start.24 = (bf16[192,512]{1,0:T(8,128)(2,1)S(1)}, bf16[192,512]{1,0:T(8,128)(2,1)S(1)}, u32[]{:S(2)}, u32[]{:S(2)}) collective-permute-start(bf16[192,512]{1,0:T(8,128)(2,1)S(1)} %down.20), channel_id=1, source_target_pairs={{0,1},{1,2},{2,3},{3,4},{4,5},{5,6},{6,7},{7,0},{8,15},{9,8},{10,9... | collective-permute-start | bytes 589832 | tf_op jit(solution)/shard_map/ppermute | solution.py:376
  178.7 5.0 %collective-permute-start.25 = (bf16[192,512]{1,0:T(8,128)(2,1)S(1)}, bf16[192,512]{1,0:T(8,128)(2,1)S(1)}, u32[]{:S(2)}, u32[]{:S(2)}) collective-permute-start(bf16[192,512]{1,0:T(8,128)(2,1)S(1)} %down.21), channel_id=1, source_target_pairs={{0,1},{1,2},{2,3},{3,4},{4,5},{5,6},{6,7},{7,0},{8,15},{9,8},{10,9... | collective-permute-start | bytes 589832 | tf_op jit(solution)/shard_map/ppermute | solution.py:376
  186.6 5.0 %collective-permute-start.26 = (bf16[192,512]{1,0:T(8,128)(2,1)S(1)}, bf16[192,512]{1,0:T(8,128)(2,1)S(1)}, u32[]{:S(2)}, u32[]{:S(2)}) collective-permute-start(bf16[192,512]{1,0:T(8,128)(2,1)S(1)} %down.22), channel_id=1, source_target_pairs={{0,1},{1,2},{2,3},{3,4},{4,5},{5,6},{6,7},{7,0},{8,15},{9,8},{10,9... | collective-permute-start | bytes 589832 | tf_op jit(solution)/shard_map/ppermute | solution.py:376
  194.4 5.0 %collective-permute-start.27 = (bf16[192,512]{1,0:T(8,128)(2,1)S(1)}, bf16[192,512]{1,0:T(8,128)(2,1)S(1)}, u32[]{:S(2)}, u32[]{:S(2)}) collective-permute-start(bf16[192,512]{1,0:T(8,128)(2,1)S(1)} %down.23), channel_id=1, source_target_pairs={{0,1},{1,2},{2,3},{3,4},{4,5},{5,6},{6,7},{7,0},{8,15},{9,8},{10,9... | collective-permute-start | bytes 589832 | tf_op jit(solution)/shard_map/ppermute | solution.py:376
  202.0 4.0 %collective-permute-done.20.a_ref = bf16[192,512]{1,0:T(8,128)(2,1)S(1)} collective-permute-done((bf16[192,512]{1,0:T(8,128)(2,1)S(1)}, bf16[192,512]{1,0:T(8,128)(2,1)S(1)}, u32[]{:S(2)}, u32[]{:S(2)}) %collective-permute-start.20) | collective-permute-done | bytes 196640 | tf_op jit(solution)/shard_map/ppermute | solution.py:376
  207.1 21.5 %all-to-all-start.3 = ((bf16[64,24,128]{2,1,0:T(8,128)(2,1)}), bf16[64,24,128]{2,1,0:T(8,128)(2,1)S(1)}, u32[]{:S(2)}, u32[]{:S(2)}) async-start(bf16[64,24,128]{2,1,0:T(8,128)(2,1)} %bitcast.21), calls=%async_computation.3 | async-start | bytes 786432 | tf_op jit(solution)/shard_map/all_to_all | solution.py:332
  228.7 14.5 %all-to-all-done.3 = bf16[64,24,128]{2,1,0:T(8,128)(2,1)S(1)} async-done(((bf16[64,24,128]{2,1,0:T(8,128)(2,1)}), bf16[64,24,128]{2,1,0:T(8,128)(2,1)S(1)}, u32[]{:S(2)}, u32[]{:S(2)}) %all-to-all-start.3) | async-done | bytes 393248 | tf_op jit(solution)/shard_map/all_to_all | solution.py:332
  (121 shorter events, 57.3 us)
Async XLA Ops:
  2.0 28.0 %all-to-all-start = ((bf16[32,2,4096]{2,1,0:T(2,128)(2,1)}), bf16[32,2,4096]{2,1,0:T(2,128)(2,1)S(1)}, u32[]{:S(2)}, u32[]{:S(2)}) async-start(bf16[32,2,4096]{2,1,0:T(2,128)(2,1)} %broadcast_in_dim.11), calls=%async_computation | async-start | bytes 1048576 | tf_op jit(solution)/shard_map/all_to_all | solution.py:332
  34.1 24.1 %all-to-all-start.1 = ((bf16[32,80,128]{2,1,0:T(8,128)(2,1)}), bf16[32,80,128]{2,1,0:T(8,128)(2,1)S(1)}, u32[]{:S(2)}, u32[]{:S(2)}) async-start(bf16[32,80,128]{2,1,0:T(8,128)(2,1)} %attention.1), calls=%async_computation.1 | async-start | bytes 1310720 | tf_op jit(solution)/shard_map/all_to_all | solution.py:332
  90.0 7.6 %collective-permute-start.1 = (bf16[192,512]{1,0:T(8,128)(2,1)S(1)}, bf16[192,512]{1,0:T(8,128)(2,1)S(1)}, u32[]{:S(2)}, u32[]{:S(2)}) collective-permute-start(bf16[192,512]{1,0:T(8,128)(2,1)S(1)} %get-tuple-element.15.refs_1_), channel_id=1, source_target_pairs={{0,1},{1,2},{2,3},{3,4},{4,5},{5,6},{6,7},{7,0},{8,15},{9,8},{10,9... | collective-permute-start | bytes 589832 | tf_op jit(solution)/shard_map/ppermute | solution.py:376
  97.6 8.3 %collective-permute-start.3 = (bf16[192,512]{1,0:T(8,128)(2,1)S(1)}, bf16[192,512]{1,0:T(8,128)(2,1)S(1)}, u32[]{:S(2)}, u32[]{:S(2)}) collective-permute-start(bf16[192,512]{1,0:T(8,128)(2,1)S(1)} %collective-permute-done.1.refs_3_), channel_id=1, source_target_pairs={{0,1},{1,2},{2,3},{3,4},{4,5},{5,6},{6,7},{7,0},{8,15},{9,8},{10,9... | collective-permute-start | bytes 589832 | tf_op jit(solution)/shard_map/ppermute | solution.py:376
  100.8 7.8 %collective-permute-start.4 = (bf16[192,512]{1,0:T(8,128)(2,1)S(1)}, bf16[192,512]{1,0:T(8,128)(2,1)S(1)}, u32[]{:S(2)}, u32[]{:S(2)}) collective-permute-start(bf16[192,512]{1,0:T(8,128)(2,1)S(1)} %collective-permute-done.2.refs_4_), channel_id=1, source_target_pairs={{0,1},{1,2},{2,3},{3,4},{4,5},{5,6},{6,7},{7,0},{8,15},{9,8},{10,9... | collective-permute-start | bytes 589832 | tf_op jit(solution)/shard_map/ppermute | solution.py:376
  105.9 7.6 %collective-permute-start.5 = (bf16[192,512]{1,0:T(8,128)(2,1)S(1)}, bf16[192,512]{1,0:T(8,128)(2,1)S(1)}, u32[]{:S(2)}, u32[]{:S(2)}) collective-permute-start(bf16[192,512]{1,0:T(8,128)(2,1)S(1)} %collective-permute-done.3.refs_5_), channel_id=1, source_target_pairs={{0,1},{1,2},{2,3},{3,4},{4,5},{5,6},{6,7},{7,0},{8,15},{9,8},{10,9... | collective-permute-start | bytes 589832 | tf_op jit(solution)/shard_map/ppermute | solution.py:376
  108.5 7.6 %collective-permute-start.6 = (bf16[192,512]{1,0:T(8,128)(2,1)S(1)}, bf16[192,512]{1,0:T(8,128)(2,1)S(1)}, u32[]{:S(2)}, u32[]{:S(2)}) collective-permute-start(bf16[192,512]{1,0:T(8,128)(2,1)S(1)} %collective-permute-done.4.refs_6_), channel_id=1, source_target_pairs={{0,1},{1,2},{2,3},{3,4},{4,5},{5,6},{6,7},{7,0},{8,15},{9,8},{10,9... | collective-permute-start | bytes 589832 | tf_op jit(solution)/shard_map/ppermute | solution.py:376
  113.5 7.6 %collective-permute-start.7 = (bf16[192,512]{1,0:T(8,128)(2,1)S(1)}, bf16[192,512]{1,0:T(8,128)(2,1)S(1)}, u32[]{:S(2)}, u32[]{:S(2)}) collective-permute-start(bf16[192,512]{1,0:T(8,128)(2,1)S(1)} %collective-permute-done.5.refs_7_), channel_id=1, source_target_pairs={{0,1},{1,2},{2,3},{3,4},{4,5},{5,6},{6,7},{7,0},{8,15},{9,8},{10,9... | collective-permute-start | bytes 589832 | tf_op jit(solution)/shard_map/ppermute | solution.py:376
  116.2 7.6 %collective-permute-start.8 = (bf16[192,512]{1,0:T(8,128)(2,1)S(1)}, bf16[192,512]{1,0:T(8,128)(2,1)S(1)}, u32[]{:S(2)}, u32[]{:S(2)}) collective-permute-start(bf16[192,512]{1,0:T(8,128)(2,1)S(1)} %collective-permute-done.6.refs_8_), channel_id=1, source_target_pairs={{0,1},{1,2},{2,3},{3,4},{4,5},{5,6},{6,7},{7,0},{8,15},{9,8},{10,9... | collective-permute-start | bytes 589832 | tf_op jit(solution)/shard_map/ppermute | solution.py:376
  123.8 7.6 %collective-permute-start.10 = (bf16[192,512]{1,0:T(8,128)(2,1)S(1)}, bf16[192,512]{1,0:T(8,128)(2,1)S(1)}, u32[]{:S(2)}, u32[]{:S(2)}) collective-permute-start(bf16[192,512]{1,0:T(8,128)(2,1)S(1)} %collective-permute-done.8.refs_10_), channel_id=1, source_target_pairs={{0,1},{1,2},{2,3},{3,4},{4,5},{5,6},{6,7},{7,0},{8,15},{9,8},{10,9... | collective-permute-start | bytes 589832 | tf_op jit(solution)/shard_map/ppermute | solution.py:376
  131.4 16.9 %collective-permute-start.12 = (bf16[192,512]{1,0:T(8,128)(2,1)S(1)}, bf16[192,512]{1,0:T(8,128)(2,1)S(1)}, u32[]{:S(2)}, u32[]{:S(2)}) collective-permute-start(bf16[192,512]{1,0:T(8,128)(2,1)S(1)} %collective-permute-done.10.refs_0_), channel_id=1, source_target_pairs={{0,1},{1,2},{2,3},{3,4},{4,5},{5,6},{6,7},{7,0},{8,15},{9,8},{10,9... | collective-permute-start | bytes 589832 | tf_op jit(solution)/shard_map/ppermute | solution.py:376
  135.7 12.6 %collective-permute-start.13 = (bf16[192,512]{1,0:T(8,128)(2,1)S(1)}, bf16[192,512]{1,0:T(8,128)(2,1)S(1)}, u32[]{:S(2)}, u32[]{:S(2)}) collective-permute-start(bf16[192,512]{1,0:T(8,128)(2,1)S(1)} %collective-permute-done.11.refs_1_), channel_id=1, source_target_pairs={{0,1},{1,2},{2,3},{3,4},{4,5},{5,6},{6,7},{7,0},{8,15},{9,8},{10,9... | collective-permute-start | bytes 589832 | tf_op jit(solution)/shard_map/ppermute | solution.py:376
  152.5 7.8 %collective-permute-start.14 = (bf16[192,512]{1,0:T(8,128)(2,1)S(1)}, bf16[192,512]{1,0:T(8,128)(2,1)S(1)}, u32[]{:S(2)}, u32[]{:S(2)}) collective-permute-start(bf16[192,512]{1,0:T(8,128)(2,1)S(1)} %get-tuple-element.17), channel_id=1, source_target_pairs={{0,1},{1,2},{2,3},{3,4},{4,5},{5,6},{6,7},{7,0},{8,15},{9,8},{10,9... | collective-permute-start | bytes 589832 | tf_op jit(solution)/shard_map/ppermute | solution.py:376
  160.5 7.6 %collective-permute-start.15 = (bf16[192,512]{1,0:T(8,128)(2,1)S(1)}, bf16[192,512]{1,0:T(8,128)(2,1)S(1)}, u32[]{:S(2)}, u32[]{:S(2)}) collective-permute-start(bf16[192,512]{1,0:T(8,128)(2,1)S(1)} %down.12), channel_id=1, source_target_pairs={{0,1},{1,2},{2,3},{3,4},{4,5},{5,6},{6,7},{7,0},{8,15},{9,8},{10,9... | collective-permute-start | bytes 589832 | tf_op jit(solution)/shard_map/ppermute | solution.py:376
  163.1 7.6 %collective-permute-start.23 = (bf16[192,512]{1,0:T(8,128)(2,1)S(1)}, bf16[192,512]{1,0:T(8,128)(2,1)S(1)}, u32[]{:S(2)}, u32[]{:S(2)}) collective-permute-start(bf16[192,512]{1,0:T(8,128)(2,1)S(1)} %down.19), channel_id=1, source_target_pairs={{0,1},{1,2},{2,3},{3,4},{4,5},{5,6},{6,7},{7,0},{8,15},{9,8},{10,9... | collective-permute-start | bytes 589832 | tf_op jit(solution)/shard_map/ppermute | solution.py:376
  168.3 7.6 %collective-permute-start.16 = (bf16[192,512]{1,0:T(8,128)(2,1)S(1)}, bf16[192,512]{1,0:T(8,128)(2,1)S(1)}, u32[]{:S(2)}, u32[]{:S(2)}) collective-permute-start(bf16[192,512]{1,0:T(8,128)(2,1)S(1)} %down.13), channel_id=1, source_target_pairs={{0,1},{1,2},{2,3},{3,4},{4,5},{5,6},{6,7},{7,0},{8,15},{9,8},{10,9... | collective-permute-start | bytes 589832 | tf_op jit(solution)/shard_map/ppermute | solution.py:376
  170.9 7.6 %collective-permute-start.24 = (bf16[192,512]{1,0:T(8,128)(2,1)S(1)}, bf16[192,512]{1,0:T(8,128)(2,1)S(1)}, u32[]{:S(2)}, u32[]{:S(2)}) collective-permute-start(bf16[192,512]{1,0:T(8,128)(2,1)S(1)} %down.20), channel_id=1, source_target_pairs={{0,1},{1,2},{2,3},{3,4},{4,5},{5,6},{6,7},{7,0},{8,15},{9,8},{10,9... | collective-permute-start | bytes 589832 | tf_op jit(solution)/shard_map/ppermute | solution.py:376
  176.2 7.6 %collective-permute-start.17 = (bf16[192,512]{1,0:T(8,128)(2,1)S(1)}, bf16[192,512]{1,0:T(8,128)(2,1)S(1)}, u32[]{:S(2)}, u32[]{:S(2)}) collective-permute-start(bf16[192,512]{1,0:T(8,128)(2,1)S(1)} %down.14), channel_id=1, source_target_pairs={{0,1},{1,2},{2,3},{3,4},{4,5},{5,6},{6,7},{7,0},{8,15},{9,8},{10,9... | collective-permute-start | bytes 589832 | tf_op jit(solution)/shard_map/ppermute | solution.py:376
  178.7 7.6 %collective-permute-start.25 = (bf16[192,512]{1,0:T(8,128)(2,1)S(1)}, bf16[192,512]{1,0:T(8,128)(2,1)S(1)}, u32[]{:S(2)}, u32[]{:S(2)}) collective-permute-start(bf16[192,512]{1,0:T(8,128)(2,1)S(1)} %down.21), channel_id=1, source_target_pairs={{0,1},{1,2},{2,3},{3,4},{4,5},{5,6},{6,7},{7,0},{8,15},{9,8},{10,9... | collective-permute-start | bytes 589832 | tf_op jit(solution)/shard_map/ppermute | solution.py:376
  184.0 7.6 %collective-permute-start.18 = (bf16[192,512]{1,0:T(8,128)(2,1)S(1)}, bf16[192,512]{1,0:T(8,128)(2,1)S(1)}, u32[]{:S(2)}, u32[]{:S(2)}) collective-permute-start(bf16[192,512]{1,0:T(8,128)(2,1)S(1)} %down.15), channel_id=1, source_target_pairs={{0,1},{1,2},{2,3},{3,4},{4,5},{5,6},{6,7},{7,0},{8,15},{9,8},{10,9... | collective-permute-start | bytes 589832 | tf_op jit(solution)/shard_map/ppermute | solution.py:376
  186.6 7.6 %collective-permute-start.26 = (bf16[192,512]{1,0:T(8,128)(2,1)S(1)}, bf16[192,512]{1,0:T(8,128)(2,1)S(1)}, u32[]{:S(2)}, u32[]{:S(2)}) collective-permute-start(bf16[192,512]{1,0:T(8,128)(2,1)S(1)} %down.22), channel_id=1, source_target_pairs={{0,1},{1,2},{2,3},{3,4},{4,5},{5,6},{6,7},{7,0},{8,15},{9,8},{10,9... | collective-permute-start | bytes 589832 | tf_op jit(solution)/shard_map/ppermute | solution.py:376
  191.8 7.6 %collective-permute-start.19 = (bf16[192,512]{1,0:T(8,128)(2,1)S(1)}, bf16[192,512]{1,0:T(8,128)(2,1)S(1)}, u32[]{:S(2)}, u32[]{:S(2)}) collective-permute-start(bf16[192,512]{1,0:T(8,128)(2,1)S(1)} %down.16), channel_id=1, source_target_pairs={{0,1},{1,2},{2,3},{3,4},{4,5},{5,6},{6,7},{7,0},{8,15},{9,8},{10,9... | collective-permute-start | bytes 589832 | tf_op jit(solution)/shard_map/ppermute | solution.py:376
  194.4 7.6 %collective-permute-start.27 = (bf16[192,512]{1,0:T(8,128)(2,1)S(1)}, bf16[192,512]{1,0:T(8,128)(2,1)S(1)}, u32[]{:S(2)}, u32[]{:S(2)}) collective-permute-start(bf16[192,512]{1,0:T(8,128)(2,1)S(1)} %down.23), channel_id=1, source_target_pairs={{0,1},{1,2},{2,3},{3,4},{4,5},{5,6},{6,7},{7,0},{8,15},{9,8},{10,9... | collective-permute-start | bytes 589832 | tf_op jit(solution)/shard_map/ppermute | solution.py:376
  207.1 36.1 %all-to-all-start.3 = ((bf16[64,24,128]{2,1,0:T(8,128)(2,1)}), bf16[64,24,128]{2,1,0:T(8,128)(2,1)S(1)}, u32[]{:S(2)}, u32[]{:S(2)}) async-start(bf16[64,24,128]{2,1,0:T(8,128)(2,1)} %bitcast.21), calls=%async_computation.3 | async-start | bytes 786432 | tf_op jit(solution)/shard_map/all_to_all | solution.py:332
  (35 other events, 363.7 us)

commit v6 on v4

--- a/solution.py
+++ b/solution.py
@@ -1,3 +1,5 @@
+import functools
+
 import jax
 import jax.numpy as jnp
 from jax import lax
@@ -187,16 +189,14 @@
     )(arrived)
 
 
-def chunk_sums(index_ref, halves, gate_ref, up_ref, gain_ref):
+def chunk_sums(chunks, refs):
     sums, squares = [None, None], [None, None]
-    for i in range(len(halves) // 2):
-        start = pl.multiple_of(index_ref[i] * 512, 512)
-        weight = jnp.concatenate(
-            [gate_ref[pl.ds(start, 512), :], up_ref[pl.ds(start, 512), :]], axis=1
-        )
-        inverse = 1.0 / gain_ref[:, pl.ds(start, 512)]
+    for i in range(chunks):
+        gate_ref, up_ref, gain_ref, *halves = refs[5 * i : 5 * i + 5]
+        weight = jnp.concatenate([gate_ref[...], up_ref[...]], axis=1)
+        inverse = 1.0 / gain_ref[...]
         for half in range(2):
-            x = halves[2 * i + half][...]
+            x = halves[half][...]
             dot = jnp.dot(x, weight, preferred_element_type=F32)
             plain = x.astype(F32) * inverse
             sq = plain * plain
@@ -206,28 +206,44 @@
     return sums, squares
 
 
-def early_kernel(index_ref, gate_ref, up_ref, gain_ref, *refs):
-    sums, squares = chunk_sums(index_ref, refs[:-1], gate_ref, up_ref, gain_ref)
+def whole(*shape):
+    return pl.BlockSpec(shape, lambda g, index: (0,) * len(shape))
+
+
+def chunk_call(kernel, name, out_shape, indices, gate, up, gain, halves, extra=()):
+    in_specs, operands = [whole(*v.shape) for v in extra], list(extra)
+    for i in range(len(indices)):
+        rows = pl.BlockSpec((512, 128), lambda g, index, i=i: (index[i], 0))
+        lanes = pl.BlockSpec((1, 512), lambda g, index, i=i: (0, index[i]))
+        in_specs += [rows, rows, lanes, whole(192, 512), whole(192, 512)]
+        operands += [gate, up, gain, halves[2 * i], halves[2 * i + 1]]
+    return pl.pallas_call(
+        functools.partial(kernel, len(indices)),
+        out_shape=out_shape,
+        grid_spec=pltpu.PrefetchScalarGridSpec(
+            num_scalar_prefetch=1, grid=(1,), in_specs=in_specs, out_specs=whole(*out_shape.shape)
+        ),
+        compiler_params=params(),
+        cost_estimate=cost(100_000_000 * len(indices), 4_000_000, 50_000),
+        name=name,
+    )(jnp.stack(indices), *operands)
+
+
+def early_kernel(chunks, index_ref, *refs):
+    sums, squares = chunk_sums(chunks, refs)
     for half in range(2):
         refs[-1][half * 192 : (half + 1) * 192, 0:256] = sums[half]
         refs[-1][half * 192 : (half + 1) * 192, 256:384] = squares[half]
 
 
 def early_sums(indices, gate, up, gain, halves):
-    return pl.pallas_call(
-        early_kernel,
-        out_shape=jax.ShapeDtypeStruct((384, 384), F32),
-        in_specs=[SMEM_SPEC] + [VMEM_SPEC] * (3 + len(halves)),
-        out_specs=VMEM_SPEC,
-        compiler_params=params(),
-        cost_estimate=cost(50_000_000 * len(halves), 4_000_000),
-        name="early_sums",
-    )(jnp.stack(indices), gate, up, gain, *halves)
-
-
-def gated_kernel(index_ref, early_ref, gate_ref, up_ref, gain_ref, *refs):
+    shape = jax.ShapeDtypeStruct((384, 384), F32)
+    return chunk_call(early_kernel, "early_sums", shape, indices, gate, up, gain, halves)
+
+
+def gated_kernel(chunks, index_ref, early_ref, *refs):
     out_ref = refs[-1]
-    sums, squares = chunk_sums(index_ref, refs[:-1], gate_ref, up_ref, gain_ref)
+    sums, squares = chunk_sums(chunks, refs)
     for half in range(2):
         rows = slice(half * 192, (half + 1) * 192)
         square = early_ref[rows, 256:384] + squares[half]
@@ -240,15 +256,8 @@
 
 
 def gated(indices, early, gate, up, gain, halves):
-    return pl.pallas_call(
-        gated_kernel,
-        out_shape=jax.ShapeDtypeStruct((8, 384, 128), BF16),
-        in_specs=[SMEM_SPEC] + [VMEM_SPEC] * (4 + len(halves)),
-        out_specs=VMEM_SPEC,
-        compiler_params=params(),
-        cost_estimate=cost(50_000_000 * len(halves), 4_000_000, 50_000),
-        name="gated",
-    )(jnp.stack(indices), early, gate, up, gain, *halves)
+    shape = jax.ShapeDtypeStruct((8, 384, 128), BF16)
+    return chunk_call(gated_kernel, "gated", shape, indices, gate, up, gain, halves, (early,))
 
 
 def down_kernel(inner_ref, weight_ref, out_ref, wide):

time: 222 us -> 223 us (level)
  no operation moved by 1% of the time
where the time goes in v6:
time: 223 us; the launch traced here: 222 us
  starting transfers between devices  96.3 us (43%)
  waiting for transfers between devices  73.6 us (33%)
  blocking collectives  21.3 us (10%)
  local copies, waits for them, and re-layouts  17.3 us (8%)
  Pallas kernels  12.9 us (6%)
    all_to_all x5, waiting for transfers between devices, exchange(): return lax.all_to_all(v, axes, split_axis=0, concat_axis=0, tiled=True)  56.8 us
    all_to_all x5, starting transfers between devices, exchange(): return lax.all_to_all(v, axes, split_axis=0, concat_axis=0, tiled=True)  50.9 us
    ppermute x7, starting transfers between devices, per_device(): left = lambda v: lax.ppermute(v, 'exp', to_left)  29.7 us
    all_to_all x1, blocking collectives, exchange(): return lax.all_to_all(v, axes, split_axis=0, concat_axis=0, tiled=True)  21.3 us
    ppermute x7, waiting for transfers between devices, per_device(): right = lambda v: lax.ppermute(v, 'exp', to_right)  16.8 us
    ppermute x7, starting transfers between devices, per_device(): right = lambda v: lax.ppermute(v, 'exp', to_right)  15.7 us
    unnamed x60, local copies, waits for them, and re-layouts  14.4 us
    pallas_call x2, Pallas kernels, chunk_call(): pl.pallas_call(functools.partial(kernel, len(indices)), out_shape=out_sha...  4.82 us
  transfers between devices with their start and end apart: 19, of which 5 were waited for; matrix products, arithmetic and copies ran while one was open for 0% of the time, Pallas kernels for 1%

profile of v6, /device:TPU:1, one launch (start us, length us, event | category | flops | bytes accessed | tf_op | source)
XLA Modules:
  0.0 221.8 jit_solution(6512654680276536562)
XLA Ops:
  0.0 2.0 broadcast_in_dim.11
  2.0 13.7 %all-to-all-start = ((bf16[32,2,4096]{2,1,0:T(2,128)(2,1)}), bf16[32,2,4096]{2,1,0:T(2,128)(2,1)S(1)}, u32[]{:S(2)}, u32[]{:S(2)}) async-start(bf16[32,2,4096]{2,1,0:T(2,128)(2,1)} %broadcast_in_dim.11), calls=%async_computation | async-start | bytes 1048576 | tf_op jit(solution)/shard_map/all_to_all | solution.py:317
  16.4 13.6 %all-to-all-done = bf16[32,2,4096]{2,1,0:T(2,128)(2,1)S(1)} async-done(((bf16[32,2,4096]{2,1,0:T(2,128)(2,1)}), bf16[32,2,4096]{2,1,0:T(2,128)(2,1)S(1)}, u32[]{:S(2)}, u32[]{:S(2)}) %all-to-all-start) | async-done | bytes 524320 | tf_op jit(solution)/shard_map/all_to_all | solution.py:317
  30.2 3.8 %attention.1 = bf16[32,80,128]{2,1,0:T(8,128)(2,1)} custom-call(s32[2]{0:T(128)S(1)} %subtract_bitcast_fusion.limit_ref, bf16[64,4096]{1,0:T(8,128)(2,1)S(1)} %reshape.24.q_ref, bf16[2,512,256]{2,1,0:T(8,128)(2,1)S(1)} %bitcast.54, bf16[2,512,256]{2,1,0:T(8,128)(2,1)S(1)} %bitcast.55), custom_call_target="tpu_custom_call" | custom-call | flops 540000000 | bytes 2200000 | tf_op jit(solution)/shard_map/attention/pallas_call | solution.py:78
  34.0 7.6 %all-to-all-start.1 = ((bf16[32,80,128]{2,1,0:T(8,128)(2,1)}), bf16[32,80,128]{2,1,0:T(8,128)(2,1)S(1)}, u32[]{:S(2)}, u32[]{:S(2)}) async-start(bf16[32,80,128]{2,1,0:T(8,128)(2,1)} %attention.1), calls=%async_computation.1 | async-start | bytes 1310720 | tf_op jit(solution)/shard_map/all_to_all | solution.py:317
  41.8 16.3 %all-to-all-done.1.part_ref = bf16[32,80,128]{2,1,0:T(8,128)(2,1)S(1)} async-done(((bf16[32,80,128]{2,1,0:T(8,128)(2,1)}), bf16[32,80,128]{2,1,0:T(8,128)(2,1)S(1)}, u32[]{:S(2)}, u32[]{:S(2)}) %all-to-all-start.1) | async-done | bytes 655392 | tf_op jit(solution)/shard_map/all_to_all | solution.py:317
  60.2 12.9 %all-to-all-start.2 = ((bf16[64,24,128]{2,1,0:T(8,128)(2,1)}), bf16[64,24,128]{2,1,0:T(8,128)(2,1)S(1)}, u32[]{:S(2)}, u32[]{:S(2)}) async-start(bf16[64,24,128]{2,1,0:T(8,128)(2,1)} %bitcast.18), calls=%async_computation.2 | async-start | bytes 786432 | tf_op jit(solution)/shard_map/all_to_all | solution.py:317
  75.5 12.3 %all-to-all-done.2 = bf16[64,24,128]{2,1,0:T(8,128)(2,1)S(1)} async-done(((bf16[64,24,128]{2,1,0:T(8,128)(2,1)}), bf16[64,24,128]{2,1,0:T(8,128)(2,1)S(1)}, u32[]{:S(2)}, u32[]{:S(2)}) %all-to-all-start.2) | async-done | bytes 393248 | tf_op jit(solution)/shard_map/all_to_all | solution.py:317
  88.0 4.0 %all-to-all-start.3 = ((bf16[8,128,512]{2,1,0:T(8,128)(2,1)}), bf16[8,128,512]{2,1,0:T(8,128)(2,1)S(1)}, u32[]{:S(2)}, u32[]{:S(2)}) async-start(bf16[8,128,512]{2,1,0:T(8,128)(2,1)} %copy-done.2), calls=%async_computation.3 | async-start | bytes 2097152 | tf_op jit(solution)/shard_map/all_to_all | solution.py:317
  92.0 3.7 %collective-permute-start = (bf16[192,512]{1,0:T(8,128)(2,1)S(1)}, bf16[192,512]{1,0:T(8,128)(2,1)S(1)}, u32[]{:S(2)}, u32[]{:S(2)}) collective-permute-start(bf16[192,512]{1,0:T(8,128)(2,1)S(1)} %get-tuple-element.19.refs_3_), channel_id=1, source_target_pairs={{0,1},{1,2},{2,3},{3,4},{4,5},{5,6},{6,7},{7,0},{8,9},{9,10},{10,1... | collective-permute-start | bytes 589832 | tf_op jit(solution)/shard_map/ppermute | solution.py:358
  95.7 2.8 %collective-permute-start.3 = (bf16[192,512]{1,0:T(8,128)(2,1)S(1)}, bf16[192,512]{1,0:T(8,128)(2,1)S(1)}, u32[]{:S(2)}, u32[]{:S(2)}) collective-permute-start(bf16[192,512]{1,0:T(8,128)(2,1)S(1)} %get-tuple-element.20.refs_4_), channel_id=1, source_target_pairs={{0,7},{1,0},{2,1},{3,2},{4,3},{5,4},{6,5},{7,6},{8,15},{9,8},{10,9... | collective-permute-start | bytes 589832 | tf_op jit(solution)/shard_map/ppermute | solution.py:359
  98.5 2.5 %collective-permute-start.1 = (bf16[192,512]{1,0:T(8,128)(2,1)S(1)}, bf16[192,512]{1,0:T(8,128)(2,1)S(1)}, u32[]{:S(2)}, u32[]{:S(2)}) collective-permute-start(bf16[192,512]{1,0:T(8,128)(2,1)S(1)} %get-tuple-element.20.refs_4_), channel_id=1, source_target_pairs={{0,1},{1,2},{2,3},{3,4},{4,5},{5,6},{6,7},{7,0},{8,9},{9,10},{10,1... | collective-permute-start | bytes 589832 | tf_op jit(solution)/shard_map/ppermute | solution.py:358
  101.0 4.0 %collective-permute-start.2 = (bf16[192,512]{1,0:T(8,128)(2,1)S(1)}, bf16[192,512]{1,0:T(8,128)(2,1)S(1)}, u32[]{:S(2)}, u32[]{:S(2)}) collective-permute-start(bf16[192,512]{1,0:T(8,128)(2,1)S(1)} %get-tuple-element.19.refs_3_), channel_id=1, source_target_pairs={{0,7},{1,0},{2,1},{3,2},{4,3},{5,4},{6,5},{7,6},{8,15},{9,8},{10,9... | collective-permute-start | bytes 589832 | tf_op jit(solution)/shard_map/ppermute | solution.py:359
  105.0 16.8 %collective-permute-done.refs_8_ = bf16[192,512]{1,0:T(8,128)(2,1)S(1)} collective-permute-done((bf16[192,512]{1,0:T(8,128)(2,1)S(1)}, bf16[192,512]{1,0:T(8,128)(2,1)S(1)}, u32[]{:S(2)}, u32[]{:S(2)}) %collective-permute-start) | collective-permute-done | bytes 196640 | tf_op jit(solution)/shard_map/ppermute | solution.py:358
  124.4 4.6 %collective-permute-start.7 = (bf16[192,512]{1,0:T(8,128)(2,1)S(1)}, bf16[192,512]{1,0:T(8,128)(2,1)S(1)}, u32[]{:S(2)}, u32[]{:S(2)}) collective-permute-start(bf16[192,512]{1,0:T(8,128)(2,1)S(1)} %collective-permute-done.3.refs_14_), channel_id=1, source_target_pairs={{0,7},{1,0},{2,1},{3,2},{4,3},{5,4},{6,5},{7,6},{8,15},{9,8},{10,9... | collective-permute-start | bytes 589832 | tf_op jit(solution)/shard_map/ppermute | solution.py:359
  132.3 4.6 %collective-permute-start.6 = (bf16[192,512]{1,0:T(8,128)(2,1)S(1)}, bf16[192,512]{1,0:T(8,128)(2,1)}, u32[]{:S(2)}, u32[]{:S(2)}) collective-permute-start(bf16[192,512]{1,0:T(8,128)(2,1)S(1)} %collective-permute-done.2.refs_13_), channel_id=1, source_target_pairs={{0,7},{1,0},{2,1},{3,2},{4,3},{5,4},{6,5},{7,6},{8,15},{9,8},{10,9... | collective-permute-start | bytes 589832 | tf_op jit(solution)/shard_map/ppermute | solution.py:359
  140.1 4.6 %collective-permute-start.11 = (bf16[192,512]{1,0:T(8,128)(2,1)S(1)}, bf16[192,512]{1,0:T(8,128)(2,1)}, u32[]{:S(2)}, u32[]{:S(2)}) collective-permute-start(bf16[192,512]{1,0:T(8,128)(2,1)S(1)} %collective-permute-done.7.refs_24_), channel_id=1, source_target_pairs={{0,7},{1,0},{2,1},{3,2},{4,3},{5,4},{6,5},{7,6},{8,15},{9,8},{10,9... | collective-permute-start | bytes 589832 | tf_op jit(solution)/shard_map/ppermute | solution.py:359
  147.3 4.6 %collective-permute-start.10 = (bf16[192,512]{1,0:T(8,128)(2,1)}, bf16[192,512]{1,0:T(8,128)(2,1)}, u32[]{:S(2)}, u32[]{:S(2)}) collective-permute-start(bf16[192,512]{1,0:T(8,128)(2,1)} %collective-permute-done.6.refs_23_), channel_id=1, source_target_pairs={{0,7},{1,0},{2,1},{3,2},{4,3},{5,4},{6,5},{7,6},{8,15},{9,8},{10,9... | collective-permute-start | bytes 589832 | tf_op jit(solution)/shard_map/ppermute | solution.py:359
  154.5 4.6 %collective-permute-start.13 = (bf16[192,512]{1,0:T(8,128)(2,1)}, bf16[192,512]{1,0:T(8,128)(2,1)}, u32[]{:S(2)}, u32[]{:S(2)}) collective-permute-start(bf16[192,512]{1,0:T(8,128)(2,1)} %collective-permute-done.11.refs_9_), channel_id=1, source_target_pairs={{0,7},{1,0},{2,1},{3,2},{4,3},{5,4},{6,5},{7,6},{8,15},{9,8},{10,9... | collective-permute-start | bytes 589832 | tf_op jit(solution)/shard_map/ppermute | solution.py:359
  165.9 2.3 %early_sums.1.early_ref = f32[384,384]{1,0:T(8,128)S(1)} custom-call(s32[5]{0:T(128)S(1)} %copy-done.26, bf16[4096,128]{1,0:T(8,128)(2,1)S(1)} %bitcast.26, bf16[4096,128]{1,0:T(8,128)(2,1)S(1)} %bitcast.34, f32[1,4096]{1,0:T(1,128)S(1)} %bitcast.45, bf16[192,512]{1,0:T(8,128)(2,1)S(1)} %get-tuple-element.19.refs_3_, ...), custom_call_target="tpu_custom_call" | custom-call | flops 500000000 | bytes 4000000 | tf_op jit(solution)/shard_map/early_sums/pallas_call | solution.py:220
  168.3 2.5 %gated.1 = bf16[8,384,128]{2,1,0:T(8,128)(2,1)S(1)} custom-call(s32[3]{0:T(128)S(1)} %pad_add_fusion.index_ref, f32[384,384]{1,0:T(8,128)S(1)} %early_sums.1.early_ref, bf16[4096,128]{1,0:T(8,128)(2,1)S(1)} %bitcast.31, bf16[4096,128]{1,0:T(8,128)(2,1)S(1)} %bitcast.39, f32[1,4096]{1,0:T(1,128)S(1)} %bitcast.50, bf16[192,512]{1,0:T(8,128)(2,1)S(1)} %copy-done.20, ...), custom_call_target="tpu_custom_call" | custom-call | flops 300000000 | bytes 4000000 | tf_op jit(solution)/shard_map/gated/pallas_call | solution.py:220
  170.8 21.3 %all_to_all.30.inner_ref = bf16[8,384,128]{2,1,0:T(8,128)(2,1)S(1)} all-to-all(bf16[8,384,128]{2,1,0:T(8,128)(2,1)S(1)} %gated.1), channel_id=1, replica_groups=mesh['ctx'=4,'att'=16,'exp'=8] {'exp'}, dimensions={0} | all-to-all | bytes 1572864 | tf_op jit(solution)/shard_map/all_to_all | solution.py:317
  193.5 12.6 %all-to-all-start.5 = ((bf16[64,24,128]{2,1,0:T(8,128)(2,1)}), bf16[64,24,128]{2,1,0:T(8,128)(2,1)S(1)}, u32[]{:S(2)}, u32[]{:S(2)}) async-start(bf16[64,24,128]{2,1,0:T(8,128)(2,1)} %bitcast.21), calls=%async_computation.5 | async-start | bytes 786432 | tf_op jit(solution)/shard_map/all_to_all | solution.py:317
  206.3 14.5 %all-to-all-done.5 = bf16[64,24,128]{2,1,0:T(8,128)(2,1)S(1)} async-done(((bf16[64,24,128]{2,1,0:T(8,128)(2,1)}), bf16[64,24,128]{2,1,0:T(8,128)(2,1)S(1)}, u32[]{:S(2)}, u32[]{:S(2)}) %all-to-all-start.5) | async-done | bytes 393248 | tf_op jit(solution)/shard_map/all_to_all | solution.py:317
  (90 shorter events, 29.2 us)
Async XLA Ops:
  2.0 28.0 %all-to-all-start = ((bf16[32,2,4096]{2,1,0:T(2,128)(2,1)}), bf16[32,2,4096]{2,1,0:T(2,128)(2,1)S(1)}, u32[]{:S(2)}, u32[]{:S(2)}) async-start(bf16[32,2,4096]{2,1,0:T(2,128)(2,1)} %broadcast_in_dim.11), calls=%async_computation | async-start | bytes 1048576 | tf_op jit(solution)/shard_map/all_to_all | solution.py:317
  34.0 24.1 %copy-start.21 = (bf16[1,16,4096]{2,1,0:T(8,128)(2,1)S(1)}, bf16[1,16,4096]{2,1,0:T(8,128)(2,1)}, u32[]{:S(2)}) copy-start(bf16[1,16,4096]{2,1,0:T(8,128)(2,1)} %param.15) | copy-start | bytes 393220
  34.0 24.1 %all-to-all-start.1 = ((bf16[32,80,128]{2,1,0:T(8,128)(2,1)}), bf16[32,80,128]{2,1,0:T(8,128)(2,1)S(1)}, u32[]{:S(2)}, u32[]{:S(2)}) async-start(bf16[32,80,128]{2,1,0:T(8,128)(2,1)} %attention.1), calls=%async_computation.1 | async-start | bytes 1310720 | tf_op jit(solution)/shard_map/all_to_all | solution.py:317
  41.8 17.9 %copy-start.22 = (s32[16,8]{1,0:T(8,128)}, s32[16,8]{1,0:T(8,128)S(1)}, u32[]{:S(2)}) copy-start(s32[16,8]{1,0:T(8,128)S(1)} %copy.12.ids_ref) | copy-start | bytes 1540
  60.2 27.5 %all-to-all-start.2 = ((bf16[64,24,128]{2,1,0:T(8,128)(2,1)}), bf16[64,24,128]{2,1,0:T(8,128)(2,1)S(1)}, u32[]{:S(2)}, u32[]{:S(2)}) async-start(bf16[64,24,128]{2,1,0:T(8,128)(2,1)} %bitcast.18), calls=%async_computation.2 | async-start | bytes 786432 | tf_op jit(solution)/shard_map/all_to_all | solution.py:317
  88.0 71.8 %copy-start = (bf16[1,4096,128]{2,1,0:T(8,128)(2,1)S(1)}, bf16[1,4096,128]{2,1,0:T(8,128)(2,1)}, u32[]{:S(2)}) copy-start(bf16[1,4096,128]{2,1,0:T(8,128)(2,1)} %param.19) | copy-start | bytes 3145732
  88.0 71.8 %copy-start.1 = (bf16[1,4096,128]{2,1,0:T(8,128)(2,1)S(1)}, bf16[1,4096,128]{2,1,0:T(8,128)(2,1)}, u32[]{:S(2)}) copy-start(bf16[1,4096,128]{2,1,0:T(8,128)(2,1)} %param.20) | copy-start | bytes 3145732
  88.0 64.6 %all-to-all-start.3 = ((bf16[8,128,512]{2,1,0:T(8,128)(2,1)}), bf16[8,128,512]{2,1,0:T(8,128)(2,1)S(1)}, u32[]{:S(2)}, u32[]{:S(2)}) async-start(bf16[8,128,512]{2,1,0:T(8,128)(2,1)} %copy-done.2), calls=%async_computation.3 | async-start | bytes 2097152 | tf_op jit(solution)/shard_map/all_to_all | solution.py:317
  92.0 29.8 %collective-permute-start = (bf16[192,512]{1,0:T(8,128)(2,1)S(1)}, bf16[192,512]{1,0:T(8,128)(2,1)S(1)}, u32[]{:S(2)}, u32[]{:S(2)}) collective-permute-start(bf16[192,512]{1,0:T(8,128)(2,1)S(1)} %get-tuple-element.19.refs_3_), channel_id=1, source_target_pairs={{0,1},{1,2},{2,3},{3,4},{4,5},{5,6},{6,7},{7,0},{8,9},{9,10},{10,1... | collective-permute-start | bytes 589832 | tf_op jit(solution)/shard_map/ppermute | solution.py:358
  95.7 28.7 %collective-permute-start.3 = (bf16[192,512]{1,0:T(8,128)(2,1)S(1)}, bf16[192,512]{1,0:T(8,128)(2,1)S(1)}, u32[]{:S(2)}, u32[]{:S(2)}) collective-permute-start(bf16[192,512]{1,0:T(8,128)(2,1)S(1)} %get-tuple-element.20.refs_4_), channel_id=1, source_target_pairs={{0,7},{1,0},{2,1},{3,2},{4,3},{5,4},{6,5},{7,6},{8,15},{9,8},{10,9... | collective-permute-start | bytes 589832 | tf_op jit(solution)/shard_map/ppermute | solution.py:359
  98.5 31.2 %collective-permute-start.1 = (bf16[192,512]{1,0:T(8,128)(2,1)S(1)}, bf16[192,512]{1,0:T(8,128)(2,1)S(1)}, u32[]{:S(2)}, u32[]{:S(2)}) collective-permute-start(bf16[192,512]{1,0:T(8,128)(2,1)S(1)} %get-tuple-element.20.refs_4_), channel_id=1, source_target_pairs={{0,1},{1,2},{2,3},{3,4},{4,5},{5,6},{6,7},{7,0},{8,9},{9,10},{10,1... | collective-permute-start | bytes 589832 | tf_op jit(solution)/shard_map/ppermute | solution.py:358
  101.0 31.3 %collective-permute-start.2 = (bf16[192,512]{1,0:T(8,128)(2,1)S(1)}, bf16[192,512]{1,0:T(8,128)(2,1)S(1)}, u32[]{:S(2)}, u32[]{:S(2)}) collective-permute-start(bf16[192,512]{1,0:T(8,128)(2,1)S(1)} %get-tuple-element.19.refs_3_), channel_id=1, source_target_pairs={{0,7},{1,0},{2,1},{3,2},{4,3},{5,4},{6,5},{7,6},{8,15},{9,8},{10,9... | collective-permute-start | bytes 589832 | tf_op jit(solution)/shard_map/ppermute | solution.py:359
  121.8 15.7 %collective-permute-start.4 = (bf16[192,512]{1,0:T(8,128)(2,1)S(1)}, bf16[192,512]{1,0:T(8,128)(2,1)S(1)}, u32[]{:S(2)}, u32[]{:S(2)}) collective-permute-start(bf16[192,512]{1,0:T(8,128)(2,1)S(1)} %collective-permute-done.refs_8_), channel_id=1, source_target_pairs={{0,1},{1,2},{2,3},{3,4},{4,5},{5,6},{6,7},{7,0},{8,9},{9,10},{10,1... | collective-permute-start | bytes 589832 | tf_op jit(solution)/shard_map/ppermute | solution.py:358
  124.4 15.7 %collective-permute-start.7 = (bf16[192,512]{1,0:T(8,128)(2,1)S(1)}, bf16[192,512]{1,0:T(8,128)(2,1)S(1)}, u32[]{:S(2)}, u32[]{:S(2)}) collective-permute-start(bf16[192,512]{1,0:T(8,128)(2,1)S(1)} %collective-permute-done.3.refs_14_), channel_id=1, source_target_pairs={{0,7},{1,0},{2,1},{3,2},{4,3},{5,4},{6,5},{7,6},{8,15},{9,8},{10,9... | collective-permute-start | bytes 589832 | tf_op jit(solution)/shard_map/ppermute | solution.py:359
  129.7 15.7 %collective-permute-start.5 = (bf16[192,512]{1,0:T(8,128)(2,1)S(1)}, bf16[192,512]{1,0:T(8,128)(2,1)}, u32[]{:S(2)}, u32[]{:S(2)}) collective-permute-start(bf16[192,512]{1,0:T(8,128)(2,1)S(1)} %collective-permute-done.1.refs_9_), channel_id=1, source_target_pairs={{0,1},{1,2},{2,3},{3,4},{4,5},{5,6},{6,7},{7,0},{8,9},{9,10},{10,1... | collective-permute-start | bytes 589832 | tf_op jit(solution)/shard_map/ppermute | solution.py:358
  132.3 15.0 %collective-permute-start.6 = (bf16[192,512]{1,0:T(8,128)(2,1)S(1)}, bf16[192,512]{1,0:T(8,128)(2,1)}, u32[]{:S(2)}, u32[]{:S(2)}) collective-permute-start(bf16[192,512]{1,0:T(8,128)(2,1)S(1)} %collective-permute-done.2.refs_13_), channel_id=1, source_target_pairs={{0,7},{1,0},{2,1},{3,2},{4,3},{5,4},{6,5},{7,6},{8,15},{9,8},{10,9... | collective-permute-start | bytes 589832 | tf_op jit(solution)/shard_map/ppermute | solution.py:359
  137.5 14.4 %collective-permute-start.8 = (bf16[192,512]{1,0:T(8,128)(2,1)S(1)}, bf16[192,512]{1,0:T(8,128)(2,1)S(1)}, u32[]{:S(2)}, u32[]{:S(2)}) collective-permute-start(bf16[192,512]{1,0:T(8,128)(2,1)S(1)} %collective-permute-done.4.refs_18_), channel_id=1, source_target_pairs={{0,1},{1,2},{2,3},{3,4},{4,5},{5,6},{6,7},{7,0},{8,9},{9,10},{10,1... | collective-permute-start | bytes 589832 | tf_op jit(solution)/shard_map/ppermute | solution.py:358
  140.1 12.4 %collective-permute-start.11 = (bf16[192,512]{1,0:T(8,128)(2,1)S(1)}, bf16[192,512]{1,0:T(8,128)(2,1)}, u32[]{:S(2)}, u32[]{:S(2)}) collective-permute-start(bf16[192,512]{1,0:T(8,128)(2,1)S(1)} %collective-permute-done.7.refs_24_), channel_id=1, source_target_pairs={{0,7},{1,0},{2,1},{3,2},{4,3},{5,4},{6,5},{7,6},{8,15},{9,8},{10,9... | collective-permute-start | bytes 589832 | tf_op jit(solution)/shard_map/ppermute | solution.py:359
  145.4 22.9 %collective-permute-start.9 = (bf16[192,512]{1,0:T(8,128)(2,1)}, bf16[192,512]{1,0:T(8,128)(2,1)}, u32[]{:S(2)}, u32[]{:S(2)}) collective-permute-start(bf16[192,512]{1,0:T(8,128)(2,1)} %collective-permute-done.5.refs_19_), channel_id=1, source_target_pairs={{0,1},{1,2},{2,3},{3,4},{4,5},{5,6},{6,7},{7,0},{8,9},{9,10},{10,1... | collective-permute-start | bytes 589832 | tf_op jit(solution)/shard_map/ppermute | solution.py:358
  147.3 20.9 %collective-permute-start.10 = (bf16[192,512]{1,0:T(8,128)(2,1)}, bf16[192,512]{1,0:T(8,128)(2,1)}, u32[]{:S(2)}, u32[]{:S(2)}) collective-permute-start(bf16[192,512]{1,0:T(8,128)(2,1)} %collective-permute-done.6.refs_23_), channel_id=1, source_target_pairs={{0,7},{1,0},{2,1},{3,2},{4,3},{5,4},{6,5},{7,6},{8,15},{9,8},{10,9... | collective-permute-start | bytes 589832 | tf_op jit(solution)/shard_map/ppermute | solution.py:359
  152.6 15.7 %collective-permute-start.12 = (bf16[192,512]{1,0:T(8,128)(2,1)}, bf16[192,512]{1,0:T(8,128)(2,1)}, u32[]{:S(2)}, u32[]{:S(2)}) collective-permute-start(bf16[192,512]{1,0:T(8,128)(2,1)} %copy-done.19), channel_id=1, source_target_pairs={{0,1},{1,2},{2,3},{3,4},{4,5},{5,6},{6,7},{7,0},{8,9},{9,10},{10,1... | collective-permute-start | bytes 589832 | tf_op jit(solution)/shard_map/ppermute | solution.py:358
  154.5 13.8 %collective-permute-start.13 = (bf16[192,512]{1,0:T(8,128)(2,1)}, bf16[192,512]{1,0:T(8,128)(2,1)}, u32[]{:S(2)}, u32[]{:S(2)}) collective-permute-start(bf16[192,512]{1,0:T(8,128)(2,1)} %collective-permute-done.11.refs_9_), channel_id=1, source_target_pairs={{0,7},{1,0},{2,1},{3,2},{4,3},{5,4},{6,5},{7,6},{8,15},{9,8},{10,9... | collective-permute-start | bytes 589832 | tf_op jit(solution)/shard_map/ppermute | solution.py:359
  193.5 27.2 %copy-start.25 = (f32[16,512]{1,0:T(8,128)S(1)}, f32[16,512]{1,0:T(8,128)}, u32[]{:S(2)}) copy-start(f32[16,512]{1,0:T(8,128)} %copy-done.24) | copy-start | bytes 98308
  193.5 27.2 %all-to-all-start.5 = ((bf16[64,24,128]{2,1,0:T(8,128)(2,1)}), bf16[64,24,128]{2,1,0:T(8,128)(2,1)S(1)}, u32[]{:S(2)}, u32[]{:S(2)}) async-start(bf16[64,24,128]{2,1,0:T(8,128)(2,1)} %bitcast.21), calls=%async_computation.5 | async-start | bytes 786432 | tf_op jit(solution)/shard_map/all_to_all | solution.py:317
  (25 other events, 95.8 us)

commit v7 on v6

--- a/solution.py
+++ b/solution.py
@@ -229,16 +229,22 @@
     )(jnp.stack(indices), *operands)
 
 
-def early_kernel(chunks, index_ref, *refs):
-    sums, squares = chunk_sums(chunks, refs)
+def step_kernel(chunks, index_ref, *refs):
+    sums, squares = chunk_sums(chunks, refs[-1 - 5 * chunks :])
     for half in range(2):
-        refs[-1][half * 192 : (half + 1) * 192, 0:256] = sums[half]
-        refs[-1][half * 192 : (half + 1) * 192, 256:384] = squares[half]
-
-
-def early_sums(indices, gate, up, gain, halves):
+        rows = slice(half * 192, (half + 1) * 192)
+        if len(refs) > 1 + 5 * chunks:
+            refs[-1][rows, 0:256] = refs[0][rows, 0:256] + sums[half]
+            refs[-1][rows, 256:384] = refs[0][rows, 256:384] + squares[half]
+        else:
+            refs[-1][rows, 0:256] = sums[half]
+            refs[-1][rows, 256:384] = squares[half]
+
+
+def gate_step(total, indices, gate, up, gain, halves):
     shape = jax.ShapeDtypeStruct((384, 384), F32)
-    return chunk_call(early_kernel, "early_sums", shape, indices, gate, up, gain, halves)
+    extra = () if total is None else (total,)
+    return chunk_call(step_kernel, "gate_up", shape, indices, gate, up, gain, halves, extra)
 
 
 def gated_kernel(chunks, index_ref, early_ref, *refs):
@@ -358,19 +364,17 @@
     right = lambda v: lax.ppermute(v, "exp", to_right)
     left = lambda v: lax.ppermute(v, "exp", to_left)
     at = lambda k: lax.rem(z + (k + ring), ring).astype(jnp.int32)
-    halves, indices = [own_a, own_b], [at(0)]
     ra, rb, la, lb = own_a, own_b, own_a, own_b
+    total = gate_step(None, [at(0)], gate, up, gain, [own_a, own_b])
     for k in range(1, 4):
         ra, lb = right(ra), left(lb)
         rb, la = right(rb), left(la)
-        halves += [ra, rb, la, lb]
-        indices += [at(-k), at(k)]
-    ra, lb, by_column = lax.optimization_barrier((ra, lb, by_column))
-    halves += [right(ra), left(lb)]
-    indices.append(at(4))
-
-    early = early_sums(indices[:5], gate, up, gain, halves[:10])
-    units = exchange(gated(indices[5:], early, gate, up, gain, halves[10:]), "exp")
+        ra, lb, total = lax.optimization_barrier((ra, lb, total))
+        if k == 3:
+            ra, lb, by_column = lax.optimization_barrier((ra, lb, by_column))
+            far_a, far_b = right(ra), left(lb)
+        total = gate_step(total, [at(-k), at(k)], gate, up, gain, [ra, rb, la, lb])
+    units = exchange(gated([at(4)], total, gate, up, gain, [far_a, far_b]), "exp")
     back = down_columns(units, by_column)
     return mix(hidden, plane_exchange(back), ids, gates)[None]
 

time: 223 us -> 220 us (0.987)
  local copies, waits for them, and re-layouts: 17.3 us -> 11.5 us
  Pallas kernels: 12.9 us -> 15.9 us
    unnamed x60 -> x42, local copies, waits for them, and re-layouts: 14.4 us -> 9.2 us
    pallas_call x2 -> x5, Pallas kernels: 4.82 us -> 7.93 us  [chunk_call(): pl.pallas_call(functools.partial(kernel, len(indices)), out_shape=out_sha...]
  transfers between devices with their start and end apart: 19 -> 19, of which waited for: 5 -> 5; matrix products, arithmetic and copies ran while one was open for 0% -> 0% of each run, Pallas kernels for 1% -> 3%
where the time goes in v7:
time: 220 us; the launch traced here: 219 us
  starting transfers between devices  97.6 us (44%)
  waiting for transfers between devices  72.6 us (33%)
  blocking collectives  20.2 us (9%)
  Pallas kernels  15.9 us (7%)
  local copies, waits for them, and re-layouts  11.5 us (5%)
    all_to_all x5, waiting for transfers between devices, exchange(): return lax.all_to_all(v, axes, split_axis=0, concat_axis=0, tiled=True)  56.8 us
    all_to_all x5, starting transfers between devices, exchange(): return lax.all_to_all(v, axes, split_axis=0, concat_axis=0, tiled=True)  52.2 us
    ppermute x7, starting transfers between devices, per_device(): left = lambda v: lax.ppermute(v, 'exp', to_left)  29.7 us
    all_to_all x1, blocking collectives, exchange(): return lax.all_to_all(v, axes, split_axis=0, concat_axis=0, tiled=True)  20.2 us
    ppermute x7, waiting for transfers between devices, per_device(): right = lambda v: lax.ppermute(v, 'exp', to_right)  15.8 us
    ppermute x7, starting transfers between devices, per_device(): right = lambda v: lax.ppermute(v, 'exp', to_right)  15.7 us
    unnamed x42, local copies, waits for them, and re-layouts  9.2 us
    pallas_call x5, Pallas kernels, chunk_call(): pl.pallas_call(functools.partial(kernel, len(indices)), out_shape=out_sha...  7.93 us
  transfers between devices with their start and end apart: 19, of which 5 were waited for; matrix products, arithmetic and copies ran while one was open for 0% of the time, Pallas kernels for 3%

profile of v7, /device:TPU:1, one launch (start us, length us, event | category | flops | bytes accessed | tf_op | source)
XLA Modules:
  0.0 218.6 jit_solution(6989262475729155720)
XLA Ops:
  0.0 2.0 broadcast_in_dim.11
  2.0 13.7 %all-to-all-start = ((bf16[32,2,4096]{2,1,0:T(2,128)(2,1)}), bf16[32,2,4096]{2,1,0:T(2,128)(2,1)S(1)}, u32[]{:S(2)}, u32[]{:S(2)}) async-start(bf16[32,2,4096]{2,1,0:T(2,128)(2,1)} %broadcast_in_dim.11), calls=%async_computation | async-start | bytes 1048576 | tf_op jit(solution)/shard_map/all_to_all | solution.py:323
  16.4 13.6 %all-to-all-done = bf16[32,2,4096]{2,1,0:T(2,128)(2,1)S(1)} async-done(((bf16[32,2,4096]{2,1,0:T(2,128)(2,1)}), bf16[32,2,4096]{2,1,0:T(2,128)(2,1)S(1)}, u32[]{:S(2)}, u32[]{:S(2)}) %all-to-all-start) | async-done | bytes 524320 | tf_op jit(solution)/shard_map/all_to_all | solution.py:323
  30.3 3.8 %attention.1 = bf16[32,80,128]{2,1,0:T(8,128)(2,1)} custom-call(s32[2]{0:T(128)S(1)} %subtract_bitcast_fusion.limit_ref, bf16[64,4096]{1,0:T(8,128)(2,1)S(1)} %reshape.24.q_ref, bf16[2,512,256]{2,1,0:T(8,128)(2,1)S(1)} %bitcast.54, bf16[2,512,256]{2,1,0:T(8,128)(2,1)S(1)} %bitcast.55), custom_call_target="tpu_custom_call" | custom-call | flops 540000000 | bytes 2200000 | tf_op jit(solution)/shard_map/attention/pallas_call | solution.py:78
  34.0 7.6 %all-to-all-start.1 = ((bf16[32,80,128]{2,1,0:T(8,128)(2,1)}), bf16[32,80,128]{2,1,0:T(8,128)(2,1)S(1)}, u32[]{:S(2)}, u32[]{:S(2)}) async-start(bf16[32,80,128]{2,1,0:T(8,128)(2,1)} %attention.1), calls=%async_computation.1 | async-start | bytes 1310720 | tf_op jit(solution)/shard_map/all_to_all | solution.py:323
  41.8 16.3 %all-to-all-done.1.part_ref = bf16[32,80,128]{2,1,0:T(8,128)(2,1)S(1)} async-done(((bf16[32,80,128]{2,1,0:T(8,128)(2,1)}), bf16[32,80,128]{2,1,0:T(8,128)(2,1)S(1)}, u32[]{:S(2)}, u32[]{:S(2)}) %all-to-all-start.1) | async-done | bytes 655392 | tf_op jit(solution)/shard_map/all_to_all | solution.py:323
  60.2 12.9 %all-to-all-start.2 = ((bf16[64,24,128]{2,1,0:T(8,128)(2,1)}), bf16[64,24,128]{2,1,0:T(8,128)(2,1)S(1)}, u32[]{:S(2)}, u32[]{:S(2)}) async-start(bf16[64,24,128]{2,1,0:T(8,128)(2,1)} %bitcast.11), calls=%async_computation.2 | async-start | bytes 786432 | tf_op jit(solution)/shard_map/all_to_all | solution.py:323
  75.4 12.3 %all-to-all-done.2 = bf16[64,24,128]{2,1,0:T(8,128)(2,1)S(1)} async-done(((bf16[64,24,128]{2,1,0:T(8,128)(2,1)}), bf16[64,24,128]{2,1,0:T(8,128)(2,1)S(1)}, u32[]{:S(2)}, u32[]{:S(2)}) %all-to-all-start.2) | async-done | bytes 393248 | tf_op jit(solution)/shard_map/all_to_all | solution.py:323
  88.0 4.0 %all-to-all-start.3 = ((bf16[8,128,512]{2,1,0:T(8,128)(2,1)}), bf16[8,128,512]{2,1,0:T(8,128)(2,1)S(1)}, u32[]{:S(2)}, u32[]{:S(2)}) async-start(bf16[8,128,512]{2,1,0:T(8,128)(2,1)} %copy-done.2), calls=%async_computation.3 | async-start | bytes 2097152 | tf_op jit(solution)/shard_map/all_to_all | solution.py:323
  92.0 3.7 %collective-permute-start = (bf16[192,512]{1,0:T(8,128)(2,1)S(1)}, bf16[192,512]{1,0:T(8,128)(2,1)}, u32[]{:S(2)}, u32[]{:S(2)}) collective-permute-start(bf16[192,512]{1,0:T(8,128)(2,1)S(1)} %get-tuple-element.28.refs_3_), channel_id=1, source_target_pairs={{0,1},{1,2},{2,3},{3,4},{4,5},{5,6},{6,7},{7,0},{8,9},{9,10},{10,1... | collective-permute-start | bytes 589832 | tf_op jit(solution)/shard_map/ppermute | solution.py:364
  95.7 2.8 %collective-permute-start.1 = (bf16[192,512]{1,0:T(8,128)(2,1)S(1)}, bf16[192,512]{1,0:T(8,128)(2,1)}, u32[]{:S(2)}, u32[]{:S(2)}) collective-permute-start(bf16[192,512]{1,0:T(8,128)(2,1)S(1)} %get-tuple-element.29.refs_4_), channel_id=1, source_target_pairs={{0,7},{1,0},{2,1},{3,2},{4,3},{5,4},{6,5},{7,6},{8,15},{9,8},{10,9... | collective-permute-start | bytes 589832 | tf_op jit(solution)/shard_map/ppermute | solution.py:365
  98.5 2.5 %collective-permute-start.4 = (bf16[192,512]{1,0:T(8,128)(2,1)S(1)}, bf16[192,512]{1,0:T(8,128)(2,1)}, u32[]{:S(2)}, u32[]{:S(2)}) collective-permute-start(bf16[192,512]{1,0:T(8,128)(2,1)S(1)} %get-tuple-element.29.refs_4_), channel_id=1, source_target_pairs={{0,1},{1,2},{2,3},{3,4},{4,5},{5,6},{6,7},{7,0},{8,9},{9,10},{10,1... | collective-permute-start | bytes 589832 | tf_op jit(solution)/shard_map/ppermute | solution.py:364
  101.0 4.0 %collective-permute-start.5 = (bf16[192,512]{1,0:T(8,128)(2,1)S(1)}, bf16[192,512]{1,0:T(8,128)(2,1)}, u32[]{:S(2)}, u32[]{:S(2)}) collective-permute-start(bf16[192,512]{1,0:T(8,128)(2,1)S(1)} %get-tuple-element.28.refs_3_), channel_id=1, source_target_pairs={{0,7},{1,0},{2,1},{3,2},{4,3},{5,4},{6,5},{7,6},{8,15},{9,8},{10,9... | collective-permute-start | bytes 589832 | tf_op jit(solution)/shard_map/ppermute | solution.py:365
  106.2 15.7 %collective-permute-done.refs_4_ = bf16[192,512]{1,0:T(8,128)(2,1)} collective-permute-done((bf16[192,512]{1,0:T(8,128)(2,1)S(1)}, bf16[192,512]{1,0:T(8,128)(2,1)}, u32[]{:S(2)}, u32[]{:S(2)}) %collective-permute-start) | collective-permute-done | bytes 196640 | tf_op jit(solution)/shard_map/ppermute | solution.py:364
  123.8 4.6 %collective-permute-start.3 = (bf16[192,512]{1,0:T(8,128)(2,1)}, bf16[192,512]{1,0:T(8,128)(2,1)}, u32[]{:S(2)}, u32[]{:S(2)}) collective-permute-start(bf16[192,512]{1,0:T(8,128)(2,1)} %collective-permute-done.1.refs_10_), channel_id=1, source_target_pairs={{0,7},{1,0},{2,1},{3,2},{4,3},{5,4},{6,5},{7,6},{8,15},{9,8},{10,9... | collective-permute-start | bytes 589832 | tf_op jit(solution)/shard_map/ppermute | solution.py:365
  130.4 4.6 %collective-permute-start.9 = (bf16[192,512]{1,0:T(8,128)(2,1)}, bf16[192,512]{1,0:T(8,128)(2,1)S(1)}, u32[]{:S(2)}, u32[]{:S(2)}) collective-permute-start(bf16[192,512]{1,0:T(8,128)(2,1)} %collective-permute-done.5.refs_9_), channel_id=1, source_target_pairs={{0,7},{1,0},{2,1},{3,2},{4,3},{5,4},{6,5},{7,6},{8,15},{9,8},{10,9... | collective-permute-start | bytes 589832 | tf_op jit(solution)/shard_map/ppermute | solution.py:365
  136.1 2.2 gate_up.5.refs_0_
  141.0 4.6 %collective-permute-start.7 = (bf16[192,512]{1,0:T(8,128)(2,1)}, bf16[192,512]{1,0:T(8,128)(2,1)}, u32[]{:S(2)}, u32[]{:S(2)}) collective-permute-start(bf16[192,512]{1,0:T(8,128)(2,1)} %collective-permute-done.3.refs_10_), channel_id=1, source_target_pairs={{0,7},{1,0},{2,1},{3,2},{4,3},{5,4},{6,5},{7,6},{8,15},{9,8},{10,9... | collective-permute-start | bytes 589832 | tf_op jit(solution)/shard_map/ppermute | solution.py:365
  147.6 4.6 %collective-permute-start.11 = (bf16[192,512]{1,0:T(8,128)(2,1)S(1)}, bf16[192,512]{1,0:T(8,128)(2,1)}, u32[]{:S(2)}, u32[]{:S(2)}) collective-permute-start(bf16[192,512]{1,0:T(8,128)(2,1)S(1)} %collective-permute-done.9.refs_9_), channel_id=1, source_target_pairs={{0,7},{1,0},{2,1},{3,2},{4,3},{5,4},{6,5},{7,6},{8,15},{9,8},{10,9... | collective-permute-start | bytes 589832 | tf_op jit(solution)/shard_map/ppermute | solution.py:365
  158.0 4.6 %collective-permute-start.13 = (bf16[192,512]{1,0:T(8,128)(2,1)}, bf16[192,512]{1,0:T(8,128)(2,1)}, u32[]{:S(2)}, u32[]{:S(2)}) collective-permute-start(bf16[192,512]{1,0:T(8,128)(2,1)} %collective-permute-done.7.refs_10_), channel_id=1, source_target_pairs={{0,7},{1,0},{2,1},{3,2},{4,3},{5,4},{6,5},{7,6},{8,15},{9,8},{10,9... | collective-permute-start | bytes 589832 | tf_op jit(solution)/shard_map/ppermute | solution.py:365
  163.7 2.2 gate_up.7.early_ref
  167.3 20.2 %all_to_all.30.inner_ref = bf16[8,384,128]{2,1,0:T(8,128)(2,1)S(1)} all-to-all(bf16[8,384,128]{2,1,0:T(8,128)(2,1)S(1)} %gated.1), channel_id=1, replica_groups=mesh['ctx'=4,'att'=16,'exp'=8] {'exp'}, dimensions={0} | all-to-all | bytes 1572864 | tf_op jit(solution)/shard_map/all_to_all | solution.py:323
  188.9 13.9 %all-to-all-start.5 = ((bf16[64,24,128]{2,1,0:T(8,128)(2,1)}), bf16[64,24,128]{2,1,0:T(8,128)(2,1)S(1)}, u32[]{:S(2)}, u32[]{:S(2)}) async-start(bf16[64,24,128]{2,1,0:T(8,128)(2,1)} %bitcast.21), calls=%async_computation.5 | async-start | bytes 786432 | tf_op jit(solution)/shard_map/all_to_all | solution.py:323
  203.0 14.5 %all-to-all-done.5 = bf16[64,24,128]{2,1,0:T(8,128)(2,1)S(1)} async-done(((bf16[64,24,128]{2,1,0:T(8,128)(2,1)}), bf16[64,24,128]{2,1,0:T(8,128)(2,1)S(1)}, u32[]{:S(2)}, u32[]{:S(2)}) %all-to-all-start.5) | async-done | bytes 393248 | tf_op jit(solution)/shard_map/all_to_all | solution.py:323
  (76 shorter events, 27.2 us)
Async XLA Ops:
  2.0 28.0 %all-to-all-start = ((bf16[32,2,4096]{2,1,0:T(2,128)(2,1)}), bf16[32,2,4096]{2,1,0:T(2,128)(2,1)S(1)}, u32[]{:S(2)}, u32[]{:S(2)}) async-start(bf16[32,2,4096]{2,1,0:T(2,128)(2,1)} %broadcast_in_dim.11), calls=%async_computation | async-start | bytes 1048576 | tf_op jit(solution)/shard_map/all_to_all | solution.py:323
  34.0 24.1 %copy-start.13 = (bf16[1,16,4096]{2,1,0:T(8,128)(2,1)S(1)}, bf16[1,16,4096]{2,1,0:T(8,128)(2,1)}, u32[]{:S(2)}) copy-start(bf16[1,16,4096]{2,1,0:T(8,128)(2,1)} %param.15) | copy-start | bytes 393220
  34.0 24.1 %all-to-all-start.1 = ((bf16[32,80,128]{2,1,0:T(8,128)(2,1)}), bf16[32,80,128]{2,1,0:T(8,128)(2,1)S(1)}, u32[]{:S(2)}, u32[]{:S(2)}) async-start(bf16[32,80,128]{2,1,0:T(8,128)(2,1)} %attention.1), calls=%async_computation.1 | async-start | bytes 1310720 | tf_op jit(solution)/shard_map/all_to_all | solution.py:323
  41.8 17.9 %copy-start.14 = (s32[16,8]{1,0:T(8,128)}, s32[16,8]{1,0:T(8,128)S(1)}, u32[]{:S(2)}) copy-start(s32[16,8]{1,0:T(8,128)S(1)} %copy.12.ids_ref) | copy-start | bytes 1540
  60.2 27.5 %all-to-all-start.2 = ((bf16[64,24,128]{2,1,0:T(8,128)(2,1)}), bf16[64,24,128]{2,1,0:T(8,128)(2,1)S(1)}, u32[]{:S(2)}, u32[]{:S(2)}) async-start(bf16[64,24,128]{2,1,0:T(8,128)(2,1)} %bitcast.11), calls=%async_computation.2 | async-start | bytes 786432 | tf_op jit(solution)/shard_map/all_to_all | solution.py:323
  87.9 17.1 %copy-start = (bf16[1,4096,128]{2,1,0:T(8,128)(2,1)S(1)}, bf16[1,4096,128]{2,1,0:T(8,128)(2,1)}, u32[]{:S(2)}) copy-start(bf16[1,4096,128]{2,1,0:T(8,128)(2,1)} %param.19) | copy-start | bytes 3145732
  88.0 17.1 %copy-start.1 = (bf16[1,4096,128]{2,1,0:T(8,128)(2,1)S(1)}, bf16[1,4096,128]{2,1,0:T(8,128)(2,1)}, u32[]{:S(2)}) copy-start(bf16[1,4096,128]{2,1,0:T(8,128)(2,1)} %param.20) | copy-start | bytes 3145732
  88.0 68.1 %all-to-all-start.3 = ((bf16[8,128,512]{2,1,0:T(8,128)(2,1)}), bf16[8,128,512]{2,1,0:T(8,128)(2,1)S(1)}, u32[]{:S(2)}, u32[]{:S(2)}) async-start(bf16[8,128,512]{2,1,0:T(8,128)(2,1)} %copy-done.2), calls=%async_computation.3 | async-start | bytes 2097152 | tf_op jit(solution)/shard_map/all_to_all | solution.py:323
  92.0 29.9 %collective-permute-start = (bf16[192,512]{1,0:T(8,128)(2,1)S(1)}, bf16[192,512]{1,0:T(8,128)(2,1)}, u32[]{:S(2)}, u32[]{:S(2)}) collective-permute-start(bf16[192,512]{1,0:T(8,128)(2,1)S(1)} %get-tuple-element.28.refs_3_), channel_id=1, source_target_pairs={{0,1},{1,2},{2,3},{3,4},{4,5},{5,6},{6,7},{7,0},{8,9},{9,10},{10,1... | collective-permute-start | bytes 589832 | tf_op jit(solution)/shard_map/ppermute | solution.py:364
  95.7 26.2 %collective-permute-start.1 = (bf16[192,512]{1,0:T(8,128)(2,1)S(1)}, bf16[192,512]{1,0:T(8,128)(2,1)}, u32[]{:S(2)}, u32[]{:S(2)}) collective-permute-start(bf16[192,512]{1,0:T(8,128)(2,1)S(1)} %get-tuple-element.29.refs_4_), channel_id=1, source_target_pairs={{0,7},{1,0},{2,1},{3,2},{4,3},{5,4},{6,5},{7,6},{8,15},{9,8},{10,9... | collective-permute-start | bytes 589832 | tf_op jit(solution)/shard_map/ppermute | solution.py:365
  98.5 30.0 %collective-permute-start.4 = (bf16[192,512]{1,0:T(8,128)(2,1)S(1)}, bf16[192,512]{1,0:T(8,128)(2,1)}, u32[]{:S(2)}, u32[]{:S(2)}) collective-permute-start(bf16[192,512]{1,0:T(8,128)(2,1)S(1)} %get-tuple-element.29.refs_4_), channel_id=1, source_target_pairs={{0,1},{1,2},{2,3},{3,4},{4,5},{5,6},{6,7},{7,0},{8,9},{9,10},{10,1... | collective-permute-start | bytes 589832 | tf_op jit(solution)/shard_map/ppermute | solution.py:364
  101.0 29.4 %collective-permute-start.5 = (bf16[192,512]{1,0:T(8,128)(2,1)S(1)}, bf16[192,512]{1,0:T(8,128)(2,1)}, u32[]{:S(2)}, u32[]{:S(2)}) collective-permute-start(bf16[192,512]{1,0:T(8,128)(2,1)S(1)} %get-tuple-element.28.refs_3_), channel_id=1, source_target_pairs={{0,7},{1,0},{2,1},{3,2},{4,3},{5,4},{6,5},{7,6},{8,15},{9,8},{10,9... | collective-permute-start | bytes 589832 | tf_op jit(solution)/shard_map/ppermute | solution.py:365
  121.9 17.2 %collective-permute-start.2 = (bf16[192,512]{1,0:T(8,128)(2,1)}, bf16[192,512]{1,0:T(8,128)(2,1)}, u32[]{:S(2)}, u32[]{:S(2)}) collective-permute-start(bf16[192,512]{1,0:T(8,128)(2,1)} %collective-permute-done.refs_4_), channel_id=1, source_target_pairs={{0,1},{1,2},{2,3},{3,4},{4,5},{5,6},{6,7},{7,0},{8,9},{9,10},{10,1... | collective-permute-start | bytes 589832 | tf_op jit(solution)/shard_map/ppermute | solution.py:364
  123.8 15.2 %collective-permute-start.3 = (bf16[192,512]{1,0:T(8,128)(2,1)}, bf16[192,512]{1,0:T(8,128)(2,1)}, u32[]{:S(2)}, u32[]{:S(2)}) collective-permute-start(bf16[192,512]{1,0:T(8,128)(2,1)} %collective-permute-done.1.refs_10_), channel_id=1, source_target_pairs={{0,7},{1,0},{2,1},{3,2},{4,3},{5,4},{6,5},{7,6},{8,15},{9,8},{10,9... | collective-permute-start | bytes 589832 | tf_op jit(solution)/shard_map/ppermute | solution.py:365
  128.5 17.2 %collective-permute-start.8 = (bf16[192,512]{1,0:T(8,128)(2,1)}, bf16[192,512]{1,0:T(8,128)(2,1)S(1)}, u32[]{:S(2)}, u32[]{:S(2)}) collective-permute-start(bf16[192,512]{1,0:T(8,128)(2,1)} %collective-permute-done.4.refs_5_), channel_id=1, source_target_pairs={{0,1},{1,2},{2,3},{3,4},{4,5},{5,6},{6,7},{7,0},{8,9},{9,10},{10,1... | collective-permute-start | bytes 589832 | tf_op jit(solution)/shard_map/ppermute | solution.py:364
  130.4 17.2 %collective-permute-start.9 = (bf16[192,512]{1,0:T(8,128)(2,1)}, bf16[192,512]{1,0:T(8,128)(2,1)S(1)}, u32[]{:S(2)}, u32[]{:S(2)}) collective-permute-start(bf16[192,512]{1,0:T(8,128)(2,1)} %collective-permute-done.5.refs_9_), channel_id=1, source_target_pairs={{0,7},{1,0},{2,1},{3,2},{4,3},{5,4},{6,5},{7,6},{8,15},{9,8},{10,9... | collective-permute-start | bytes 589832 | tf_op jit(solution)/shard_map/ppermute | solution.py:365
  139.1 17.0 %collective-permute-start.6 = (bf16[192,512]{1,0:T(8,128)(2,1)}, bf16[192,512]{1,0:T(8,128)(2,1)}, u32[]{:S(2)}, u32[]{:S(2)}) collective-permute-start(bf16[192,512]{1,0:T(8,128)(2,1)} %collective-permute-done.2.refs_4_), channel_id=1, source_target_pairs={{0,1},{1,2},{2,3},{3,4},{4,5},{5,6},{6,7},{7,0},{8,9},{9,10},{10,1... | collective-permute-start | bytes 589832 | tf_op jit(solution)/shard_map/ppermute | solution.py:364
  141.0 15.0 %collective-permute-start.7 = (bf16[192,512]{1,0:T(8,128)(2,1)}, bf16[192,512]{1,0:T(8,128)(2,1)}, u32[]{:S(2)}, u32[]{:S(2)}) collective-permute-start(bf16[192,512]{1,0:T(8,128)(2,1)} %collective-permute-done.3.refs_10_), channel_id=1, source_target_pairs={{0,7},{1,0},{2,1},{3,2},{4,3},{5,4},{6,5},{7,6},{8,15},{9,8},{10,9... | collective-permute-start | bytes 589832 | tf_op jit(solution)/shard_map/ppermute | solution.py:365
  145.7 17.0 %collective-permute-start.10 = (bf16[192,512]{1,0:T(8,128)(2,1)S(1)}, bf16[192,512]{1,0:T(8,128)(2,1)}, u32[]{:S(2)}, u32[]{:S(2)}) collective-permute-start(bf16[192,512]{1,0:T(8,128)(2,1)S(1)} %collective-permute-done.8.refs_5_), channel_id=1, source_target_pairs={{0,1},{1,2},{2,3},{3,4},{4,5},{5,6},{6,7},{7,0},{8,9},{9,10},{10,1... | collective-permute-start | bytes 589832 | tf_op jit(solution)/shard_map/ppermute | solution.py:364
  147.6 15.1 %collective-permute-start.11 = (bf16[192,512]{1,0:T(8,128)(2,1)S(1)}, bf16[192,512]{1,0:T(8,128)(2,1)}, u32[]{:S(2)}, u32[]{:S(2)}) collective-permute-start(bf16[192,512]{1,0:T(8,128)(2,1)S(1)} %collective-permute-done.9.refs_9_), channel_id=1, source_target_pairs={{0,7},{1,0},{2,1},{3,2},{4,3},{5,4},{6,5},{7,6},{8,15},{9,8},{10,9... | collective-permute-start | bytes 589832 | tf_op jit(solution)/shard_map/ppermute | solution.py:365
  156.0 9.8 %collective-permute-start.12 = (bf16[192,512]{1,0:T(8,128)(2,1)}, bf16[192,512]{1,0:T(8,128)(2,1)}, u32[]{:S(2)}, u32[]{:S(2)}) collective-permute-start(bf16[192,512]{1,0:T(8,128)(2,1)} %collective-permute-done.6.refs_4_), channel_id=1, source_target_pairs={{0,1},{1,2},{2,3},{3,4},{4,5},{5,6},{6,7},{7,0},{8,9},{9,10},{10,1... | collective-permute-start | bytes 589832 | tf_op jit(solution)/shard_map/ppermute | solution.py:364
  158.0 7.9 %collective-permute-start.13 = (bf16[192,512]{1,0:T(8,128)(2,1)}, bf16[192,512]{1,0:T(8,128)(2,1)}, u32[]{:S(2)}, u32[]{:S(2)}) collective-permute-start(bf16[192,512]{1,0:T(8,128)(2,1)} %collective-permute-done.7.refs_10_), channel_id=1, source_target_pairs={{0,7},{1,0},{2,1},{3,2},{4,3},{5,4},{6,5},{7,6},{8,15},{9,8},{10,9... | collective-permute-start | bytes 589832 | tf_op jit(solution)/shard_map/ppermute | solution.py:365
  188.9 28.6 %copy-start.17 = (f32[16,512]{1,0:T(8,128)S(1)}, f32[16,512]{1,0:T(8,128)}, u32[]{:S(2)}) copy-start(f32[16,512]{1,0:T(8,128)} %copy-done.16) | copy-start | bytes 98308
  188.9 28.6 %all-to-all-start.5 = ((bf16[64,24,128]{2,1,0:T(8,128)(2,1)}), bf16[64,24,128]{2,1,0:T(8,128)(2,1)S(1)}, u32[]{:S(2)}, u32[]{:S(2)}) async-start(bf16[64,24,128]{2,1,0:T(8,128)(2,1)} %bitcast.21), calls=%async_computation.5 | async-start | bytes 786432 | tf_op jit(solution)/shard_map/all_to_all | solution.py:323
  (16 other events, 89.6 us)

commit v8 on v2

--- a/solution.py
+++ b/solution.py
@@ -14,13 +14,15 @@
 F32 = jnp.float32
 BF16 = jnp.bfloat16
 VMEM_LIMIT = 48 * 1024 * 1024
+WHOLE_VMEM = 60 * 1024 * 1024
 
 VMEM_SPEC = pl.BlockSpec(memory_space=pltpu.VMEM)
+HBM_SPEC = pl.BlockSpec(memory_space=pltpu.HBM)
 SMEM_SPEC = pl.BlockSpec(memory_space=pltpu.SMEM)
 
 
-def params():
-    return pltpu.CompilerParams(vmem_limit_bytes=VMEM_LIMIT)
+def params(limit=VMEM_LIMIT):
+    return pltpu.CompilerParams(vmem_limit_bytes=limit)
 
 
 def cost(flops, bytes_accessed, transcendentals=0):
@@ -186,20 +188,29 @@
     )(arrived)
 
 
-def gated_kernel(rows_ref, gate_ref, up_ref, gain_ref, out_ref, chunks, arrivals):
-    copies = [
-        pltpu.make_async_copy(rows_ref.at[d], chunks.at[d], arrivals.at[d]) for d in range(8)
-    ]
-    for copy in copies:
-        copy.start()
+def gated_kernel(
+    rows_ref, gate_ref, up_ref, gain_ref, out_ref, chunks, gate_chunks, up_chunks, arrivals
+):
+    copies = []
+    for d in range(8):
+        cols = pl.ds(d * 512, 512)
+        copies.append(
+            (
+                pltpu.make_async_copy(gate_ref.at[cols], gate_chunks.at[d], arrivals.at[0, d]),
+                pltpu.make_async_copy(up_ref.at[cols], up_chunks.at[d], arrivals.at[1, d]),
+                pltpu.make_async_copy(rows_ref.at[d], chunks.at[d], arrivals.at[2, d]),
+            )
+        )
+        for copy in copies[d]:
+            copy.start()
     acc, square = None, None
     for d in range(8):
-        copies[d].wait()
+        for copy in copies[d]:
+            copy.wait()
         x = chunks[d]
-        cols = slice(d * 512, (d + 1) * 512)
-        weight = jnp.concatenate([gate_ref[cols, :], up_ref[cols, :]], axis=1)
+        weight = jnp.concatenate([gate_chunks[d], up_chunks[d]], axis=1)
         dot = jnp.dot(x, weight, preferred_element_type=F32)
-        plain = x.astype(F32) * (1.0 / gain_ref[:, cols])
+        plain = x.astype(F32) * (1.0 / gain_ref[:, d * 512 : (d + 1) * 512])
         sq = plain * plain
         sq = sq[:, 0:128] + sq[:, 128:256] + sq[:, 256:384] + sq[:, 384:512]
         acc = dot if acc is None else acc + dot
@@ -217,10 +228,15 @@
     return pl.pallas_call(
         gated_kernel,
         out_shape=jax.ShapeDtypeStruct((8, 384, 128), BF16),
-        in_specs=[pl.BlockSpec(memory_space=pl.ANY)] + [VMEM_SPEC] * 3,
-        out_specs=VMEM_SPEC,
-        scratch_shapes=[pltpu.VMEM((8, 384, 512), BF16), pltpu.SemaphoreType.DMA((8,))],
-        compiler_params=params(),
+        in_specs=[HBM_SPEC] * 3 + [VMEM_SPEC],
+        out_specs=VMEM_SPEC,
+        scratch_shapes=[
+            pltpu.VMEM((8, 384, 512), BF16),
+            pltpu.VMEM((8, 512, 128), BF16),
+            pltpu.VMEM((8, 512, 128), BF16),
+            pltpu.SemaphoreType.DMA((3, 8)),
+        ],
+        compiler_params=params(WHOLE_VMEM),
         cost_estimate=cost(810_000_000, 6_000_000, 50_000),
         name="gated",
     )(rows, gate, up, gain)
@@ -303,19 +319,14 @@
 ):
     z = lax.axis_index("exp")
     devices = lax.axis_size(("ctx", "exp"))
-    ring = lax.axis_size("exp")
     context = keys.shape[2]
     start = lax.axis_index(("ctx", "exp")) * context
     gain = norm_gain.reshape(1, D)
     ids, gates = expert_ids[0], gate_values[0]
     gate, up, down = gate_weight[0], up_weight[0], down_weight[0]
 
-    def gathered(v, axis):
-        v = jnp.broadcast_to(v[None], (lax.axis_size(axis),) + v.shape)
-        return exchange(v, axis)
-
-    q = gathered(queries[0], "exp").reshape(ring * queries.shape[1], D)
-    q = gathered(q, "ctx").reshape(devices * queries.shape[1], D)
+    spread = jnp.broadcast_to(queries, (devices,) + queries.shape[1:])
+    q = exchange(spread, ("ctx", "exp")).reshape(devices * queries.shape[1], D)
     part = attention(lengths[0] - start, q, keys[0], values[0])
     part = exchange(part, ("ctx", "exp"))
     hidden, outbound = combine(z.reshape(1), part, residual[0], gain, ids)

time: 220 us -> 221 us (level)
  blocking collectives: 74.7 us -> 54.1 us
  starting transfers between devices: 20 us -> 32.8 us
  waiting for transfers between devices: 90.6 us -> 101 us
  local copies, waits for them, and re-layouts: 7.09 us -> 4.49 us
    all_to_all x3 -> x2, blocking collectives: 74.7 us -> 54.1 us  [exchange(): return lax.all_to_all(v, axes, split_axis=0, concat_axis=0, tiled=True)]
    all_to_all x4, starting transfers between devices: 20 us -> 32.8 us  [exchange(): return lax.all_to_all(v, axes, split_axis=0, concat_axis=0, tiled=True)]
    all_to_all x4, waiting for transfers between devices: 34.4 us -> 44.5 us  [exchange(): return lax.all_to_all(v, axes, split_axis=0, concat_axis=0, tiled=True)]
    unnamed x20 -> x14, local copies, waits for them, and re-layouts: 5.22 us -> 2.1 us
  transfers between devices with their start and end apart: 5 -> 5, of which waited for: 4 -> 4; matrix products, arithmetic and copies ran while one was open for 0% -> 0% of each run, Pallas kernels for 2% -> 3%
where the time goes in v8:
time: 221 us
  waiting for transfers between devices  101 us (46%)
  blocking collectives  54.1 us (24%)
  starting transfers between devices  32.8 us (15%)
  Pallas kernels  14.3 us (6%)
  between operations  13.5 us (6%)
  local copies, waits for them, and re-layouts  4.49 us (2%)
    all_gather x1, waiting for transfers between devices, per_device(): rows = lax.all_gather(own, 'exp', axis=0)  56.1 us
    all_to_all x2, blocking collectives, exchange(): return lax.all_to_all(v, axes, split_axis=0, concat_axis=0, tiled=True)  54.1 us
    all_to_all x4, waiting for transfers between devices, exchange(): return lax.all_to_all(v, axes, split_axis=0, concat_axis=0, tiled=True)  44.5 us
    all_to_all x4, starting transfers between devices, exchange(): return lax.all_to_all(v, axes, split_axis=0, concat_axis=0, tiled=True)  32.8 us
    pallas_call x1, Pallas kernels, gated(): pl.pallas_call(gated_kernel, out_shape=jax.ShapeDtypeStruct((8, 384, 128)...  5.29 us
  transfers between devices with their start and end apart: 5, of which 4 were waited for; matrix products, arithmetic and copies ran while one was open for 0% of the time, Pallas kernels for 3%

profile of v8, /device:TPU:1, one launch (start us, length us, event | category | flops | bytes accessed | tf_op | source)
XLA Modules:
  0.0 220.5 jit_solution(9558875035707980182)
XLA Ops:
  6.5 2.0 broadcast_in_dim.11
  8.6 13.7 %all-to-all-start = ((bf16[32,2,4096]{2,1,0:T(2,128)(2,1)}), bf16[32,2,4096]{2,1,0:T(2,128)(2,1)S(1)}, u32[]{:S(2)}, u32[]{:S(2)}) async-start(bf16[32,2,4096]{2,1,0:T(2,128)(2,1)} %broadcast_in_dim.11), calls=%async_computation | async-start | bytes 1048576 | tf_op jit(solution)/shard_map/all_to_all | solution.py:299
  22.3 0.7 subtract_bitcast_fusion.limit_ref
  23.0 13.6 %all-to-all-done = bf16[32,2,4096]{2,1,0:T(2,128)(2,1)S(1)} async-done(((bf16[32,2,4096]{2,1,0:T(2,128)(2,1)}), bf16[32,2,4096]{2,1,0:T(2,128)(2,1)S(1)}, u32[]{:S(2)}, u32[]{:S(2)}) %all-to-all-start) | async-done | bytes 524320 | tf_op jit(solution)/shard_map/all_to_all | solution.py:299
  36.6 0.2 reshape.24.q_ref
  36.8 1.0 copy-done.1
  37.9 1.0 copy-done.2
  38.9 3.8 %attention.1 = bf16[32,80,128]{2,1,0:T(8,128)(2,1)} custom-call(s32[2]{0:T(128)S(1)} %subtract_bitcast_fusion.limit_ref, bf16[64,4096]{1,0:T(8,128)(2,1)S(1)} %reshape.24.q_ref, bf16[2,512,256]{2,1,0:T(8,128)(2,1)S(1)} %bitcast.22, bf16[2,512,256]{2,1,0:T(8,128)(2,1)S(1)} %bitcast.23), custom_call_target="tpu_custom_call" | custom-call | flops 540000000 | bytes 2200000 | tf_op jit(solution)/shard_map/attention/pallas_call | solution.py:78
  42.7 7.5 %all-to-all-start.1 = ((bf16[32,80,128]{2,1,0:T(8,128)(2,1)}), bf16[32,80,128]{2,1,0:T(8,128)(2,1)S(1)}, u32[]{:S(2)}, u32[]{:S(2)}) async-start(bf16[32,80,128]{2,1,0:T(8,128)(2,1)} %attention.1), calls=%async_computation.1 | async-start | bytes 1310720 | tf_op jit(solution)/shard_map/all_to_all | solution.py:299
  50.3 0.1 copy.12.ids_ref
  50.3 16.3 %all-to-all-done.1.part_ref = bf16[32,80,128]{2,1,0:T(8,128)(2,1)S(1)} async-done(((bf16[32,80,128]{2,1,0:T(8,128)(2,1)}), bf16[32,80,128]{2,1,0:T(8,128)(2,1)S(1)}, u32[]{:S(2)}, u32[]{:S(2)}) %all-to-all-start.1) | async-done | bytes 655392 | tf_op jit(solution)/shard_map/all_to_all | solution.py:299
  66.7 0.7 combine.1
  67.4 27.3 %all_to_all.30 = bf16[64,24,128]{2,1,0:T(8,128)(2,1)S(1)} all-to-all(bf16[64,24,128]{2,1,0:T(8,128)(2,1)S(1)} %bitcast.24), channel_id=1, replica_groups=mesh['ctx'=4,'att'=16,'exp'=8] {'ctx','att'}, dimensions={0} | all-to-all | bytes 786432 | tf_op jit(solution)/shard_map/all_to_all | solution.py:299
  94.7 1.0 compact.1
  95.7 1.1 pack.1
  96.8 3.9 %all-to-all-start.4 = ((bf16[8,128,512]{2,1,0:T(8,128)(2,1)}), bf16[8,128,512]{2,1,0:T(8,128)(2,1)S(1)}, u32[]{:S(2)}, u32[]{:S(2)}) async-start(bf16[8,128,512]{2,1,0:T(8,128)(2,1)} %pack.1), calls=%async_computation.4 | async-start | bytes 2097152 | tf_op jit(solution)/shard_map/all_to_all | solution.py:299
  100.7 56.1 %all-gather.3.cloned.1.call-done = bf16[3072,512]{1,0:T(8,128)(2,1)} async-done(((bf16[384,512]{1,0:T(8,128)(2,1)}), bf16[3072,512]{1,0:T(8,128)(2,1)}) %all-gather.3.cloned.1.call-update) | async-done | bytes 3145744 | tf_op jit(solution)/shard_map/all_gather | solution.py:336
  156.8 5.3 %gated.1 = bf16[8,384,128]{2,1,0:T(8,128)(2,1)} custom-call(bf16[8,384,512]{2,1,0:T(8,128)(2,1)} %bitcast.28, bf16[4096,128]{1,0:T(8,128)(2,1)} %bitcast.29, bf16[4096,128]{1,0:T(8,128)(2,1)} %bitcast.30, f32[1,4096]{1,0:T(1,128)} %bitcast.26), custom_call_target="tpu_custom_call" | custom-call | flops 810000000 | bytes 6000000 | tf_op jit(solution)/shard_map/gated/pallas_call | solution.py:228
  162.1 26.8 %all_to_all.31.inner_ref = bf16[8,384,128]{2,1,0:T(8,128)(2,1)S(1)} all-to-all(bf16[8,384,128]{2,1,0:T(8,128)(2,1)} %gated.1), channel_id=1, replica_groups=mesh['ctx'=4,'att'=16,'exp'=8] {'exp'}, dimensions={0} | all-to-all | bytes 1572864 | tf_op jit(solution)/shard_map/all_to_all | solution.py:299
  188.9 1.4 down.1
  190.3 7.7 %all-to-all-start.5 = ((bf16[64,24,128]{2,1,0:T(8,128)(2,1)}), bf16[64,24,128]{2,1,0:T(8,128)(2,1)S(1)}, u32[]{:S(2)}, u32[]{:S(2)}) async-start(bf16[64,24,128]{2,1,0:T(8,128)(2,1)} %bitcast.14), calls=%async_computation.5 | async-start | bytes 786432 | tf_op jit(solution)/shard_map/all_to_all | solution.py:299
  198.0 0.1 copy.14.gates_ref
  198.1 14.5 %all-to-all-done.5 = bf16[64,24,128]{2,1,0:T(8,128)(2,1)S(1)} async-done(((bf16[64,24,128]{2,1,0:T(8,128)(2,1)}), bf16[64,24,128]{2,1,0:T(8,128)(2,1)S(1)}, u32[]{:S(2)}, u32[]{:S(2)}) %all-to-all-start.5) | async-done | bytes 393248 | tf_op jit(solution)/shard_map/all_to_all | solution.py:299
  212.6 1.1 mix.1
  (15 shorter events, 0.1 us)
Async XLA Ops:
  6.5 43.7 %copy-start.5 = (s32[1,16,8]{1,2,0:T(8,128)S(1)}, s32[1,16,8]{1,2,0:T(8,128)}, u32[]{:S(2)}) copy-start(s32[1,16,8]{1,2,0:T(8,128)} %param.17) | copy-start | bytes 1540
  6.5 60.1 %copy-start.3 = (bf16[1,16,4096]{2,1,0:T(8,128)(2,1)S(1)}, bf16[1,16,4096]{2,1,0:T(8,128)(2,1)}, u32[]{:S(2)}) copy-start(bf16[1,16,4096]{2,1,0:T(8,128)(2,1)} %param.15) | copy-start | bytes 393220
  6.5 60.1 %copy-start.4 = (f32[4096]{0:T(1024)S(1)}, f32[4096]{0:T(1024)}, u32[]{:S(2)}) copy-start(f32[4096]{0:T(1024)} %param.16) | copy-start | bytes 49156
  8.6 28.0 %all-to-all-start = ((bf16[32,2,4096]{2,1,0:T(2,128)(2,1)}), bf16[32,2,4096]{2,1,0:T(2,128)(2,1)S(1)}, u32[]{:S(2)}, u32[]{:S(2)}) async-start(bf16[32,2,4096]{2,1,0:T(2,128)(2,1)} %broadcast_in_dim.11), calls=%async_computation | async-start | bytes 1048576 | tf_op jit(solution)/shard_map/all_to_all | solution.py:299
  36.8 1.0 copy-start.1
  37.9 1.0 copy-start.2
  38.9 56.8 %copy-start = (bf16[1,128,4096]{2,1,0:T(8,128)(2,1)S(1)}, bf16[1,128,4096]{2,1,0:T(8,128)(2,1)}, u32[]{:S(2)}) copy-start(bf16[1,128,4096]{2,1,0:T(8,128)(2,1)} %param.21) | copy-start | bytes 3145732
  42.7 23.9 %all-to-all-start.1 = ((bf16[32,80,128]{2,1,0:T(8,128)(2,1)}), bf16[32,80,128]{2,1,0:T(8,128)(2,1)S(1)}, u32[]{:S(2)}, u32[]{:S(2)}) async-start(bf16[32,80,128]{2,1,0:T(8,128)(2,1)} %attention.1), calls=%async_computation.1 | async-start | bytes 1310720 | tf_op jit(solution)/shard_map/all_to_all | solution.py:299
  50.2 106.6 %all-gather.3.cloned.1.call-start = ((), (), s32[]{:S(2)}) async-start(), calls=%async_computation.6 | async-start | bytes 3538944 | tf_op jit(solution)/shard_map/all_gather | solution.py:336
  96.8 65.3 %all-to-all-start.4 = ((bf16[8,128,512]{2,1,0:T(8,128)(2,1)}), bf16[8,128,512]{2,1,0:T(8,128)(2,1)S(1)}, u32[]{:S(2)}, u32[]{:S(2)}) async-start(bf16[8,128,512]{2,1,0:T(8,128)(2,1)} %pack.1), calls=%async_computation.4 | async-start | bytes 2097152 | tf_op jit(solution)/shard_map/all_to_all | solution.py:299
  162.1 35.9 %copy-start.6 = (bf16[1,16,8]{1,2,0:T(8,128)(2,1)S(1)}, bf16[1,16,8]{1,2,0:T(8,128)(2,1)}, u32[]{:S(2)}) copy-start(bf16[1,16,8]{1,2,0:T(8,128)(2,1)} %param.18) | copy-start | bytes 772
  190.3 22.3 %all-to-all-start.5 = ((bf16[64,24,128]{2,1,0:T(8,128)(2,1)}), bf16[64,24,128]{2,1,0:T(8,128)(2,1)S(1)}, u32[]{:S(2)}, u32[]{:S(2)}) async-start(bf16[64,24,128]{2,1,0:T(8,128)(2,1)} %bitcast.14), calls=%async_computation.5 | async-start | bytes 786432 | tf_op jit(solution)/shard_map/all_to_all | solution.py:299
Sparse Core Ops, SparseCore 0:
  95.8 60.9 all-gather.2
